TPU v7x, 128 devices: a whole 4x4x4 slice. The times are simulated.
128 devices in a mesh: row: 8 (over x, core), mat: 16 (over z, y).
Axes of the slice: x: 4, y: 4, z: 4, core: 2. Of those that a mesh axis runs over, the one named last changes fastest.
Arguments:
- gradients: bfloat16 [4, 28672, 8192], P(None, 'row', 'mat'), may hold values from -140 to 140
- sketch: bfloat16 [8192, 256], P('mat'), may hold values from -0.0625 to 0.0625
Outputs:
- basis: bfloat16 [4, 28672, 256], P(None, ('row', 'mat'))
- projected: float32 [4, 256, 8192], P(None, 'row', 'mat')
All inputs are finite; a program needn't handle non-finite values.
Results may differ from a plain program's by a relative error of at most 0.015.
Values may be sent and summed in bfloat16 or wider, within the bound.
No kernel may reach another device: no remote copies, remote signals or barrier semaphores. Data moves between devices by JAX's collectives and lax.ppermute only.
A program may use at most 128 MiB of HBM per device.

v0:
```python
import jax
import jax.numpy as jnp
from jax import lax
from jax.sharding import PartitionSpec as P


def factor(sketched_rows, gram):
    lower = jnp.linalg.cholesky(gram)
    qmat_t = lax.linalg.triangular_solve(
        lower, jnp.swapaxes(sketched_rows, 1, 2), left_side=True, lower=True
    )
    return jnp.swapaxes(qmat_t, 1, 2)


def local(gradients, sketch):
    mats, rows_local, cols_local = gradients.shape
    root = float(rows_local * lax.axis_size("row")) ** 0.5
    share = rows_local // lax.axis_size("mat")
    term = jnp.einsum("mrc,ck->mrk", gradients, sketch, preferred_element_type=jnp.float32)
    sketched = lax.psum(term, "mat")
    gram_part = jnp.einsum(
        "mrk,mrl->mkl",
        sketched,
        sketched,
        precision=lax.Precision.HIGHEST,
        preferred_element_type=jnp.float32,
    )
    gram = lax.psum(gram_part, "row")
    full_basis = (factor(sketched, gram) * root).astype(jnp.bfloat16)
    partial_proj = jnp.einsum(
        "mrk,mrc->mkc", full_basis, gradients, preferred_element_type=jnp.float32
    )
    basis = lax.dynamic_slice_in_dim(full_basis, lax.axis_index("mat") * share, share, 1)
    projected = (
        lax.psum_scatter(
            partial_proj.astype(jnp.bfloat16), "row", scatter_dimension=1, tiled=True
        ).astype(jnp.float32)
        / root
    )
    return (basis, projected)


def solution(mesh):
    placed = (P(None, "row", "mat"), P("mat", None))
    return jax.shard_map(
        local,
        mesh=mesh,
        in_specs=placed,
        out_specs=(P(None, ("row", "mat"), None), P(None, "row", "mat")),
        check_vma=False,
    )
```

profile of v0, /device:TPU:0, one launch (start us, length us, event | category | flops | bytes accessed | tf_op | source)
XLA Modules:
  0.0 629.9 jit_solution(10462972371644993253)
XLA Ops:
  7.2 0.9 copy-done
  8.1 14.3 %fusion.10 = f32[4,3584,256]{2,1,0:T(8,128)} fusion(bf16[4,3584,512]{2,1,0:T(8,128)(2,1)} %param.2, bf16[512,256]{1,0:T(8,128)(2,1)S(1)} %copy-done), kind=kOutput, calls=%fused_computation.21 | convolution fusion | flops 3758096384 | bytes 29622272 | tf_op jit(solution)/shard_map/mrc,ck->mrk/dot_general | solution.py:19
  22.5 0.6 all-reduce.6.cloned.1.call-start
  23.0 201.3 %all-reduce.4.cloned.1.call-done = f32[4,3584,256]{2,1,0:T(8,128)} async-done(((f32[4,3584,256]{2,1,0:T(8,128)}), f32[4,3584,256]{2,1,0:T(8,128)}) %all-reduce.4.cloned.1.call-update) | async-done | bytes 14680080 | tf_op jit(solution)/shard_map/psum | solution.py:20
  224.3 29.5 %fusion.13 = f32[4,256,256]{1,2,0:T(8,128)} fusion(f32[4,3584,256]{2,1,0:T(8,128)} %all-reduce.4.cloned.1.call-done), kind=kOutput, calls=%fused_computation.36 | convolution fusion | flops 11274289152 | bytes 15728640 | tf_op jit(solution)/shard_map/mrk,mrl->mkl/dot_general | solution.py:21
  253.8 0.2 reduce-scatter.2.cloned.1.call-start
  254.2 61.9 %all-reduce.6.cloned.1.call-done = f32[4,256,256]{1,2,0:T(8,128)} async-done(((f32[4,256,256]{1,2,0:T(8,128)}), f32[4,256,256]{1,2,0:T(8,128)}) %all-reduce.6.cloned.1.call-update) | async-done | bytes 1048592 | tf_op jit(solution)/shard_map/psum | solution.py:28
  316.1 1.6 copy.17
  317.6 1.4 fusion.4
  319.0 46.9 %custom-call.16 = f32[4,128,128]{2,1,0:T(8,128)S(1)} custom-call(f32[4,128,128]{2,1,0:T(8,128)S(1)} %cholesky.122), custom_call_target="Cholesky" | custom-call | tf_op jit(solution)/shard_map/jit(cholesky)/cholesky | solution.py:8
  366.0 39.3 %custom-call.17 = f32[4,1,128,128]{2,3,1,0:T(8,128)S(1)} custom-call(f32[4,1,128,128]{3,2,1,0:T(8,128)S(1)} %select_bitcast_fusion), custom_call_target="InvertDiagBlocksLowerTriangular" | custom-call | tf_op jit(solution)/shard_map/jit(cholesky)/cholesky | solution.py:8
  405.4 0.4 constant_dynamic-update-slice_fusion.1
  405.8 0.7 convolution_subtract_fusion
  406.4 46.9 %custom-call.18 = f32[4,128,128]{2,1,0:T(8,128)S(1)} custom-call(f32[4,128,128]{2,1,0:T(8,128)S(1)} %convolution_subtract_fusion), custom_call_target="Cholesky" | custom-call | tf_op jit(solution)/shard_map/jit(cholesky)/cholesky | solution.py:8
  453.4 0.1 compare_reduce_fusion
  453.5 0.2 select_select_fusion
  453.8 5.6 while.1
  453.8 0.6 fusion.23
  454.4 2.2 bitcast_dynamic-update-slice_fusion.2
  456.6 0.6 fusion.23
  457.2 2.2 bitcast_dynamic-update-slice_fusion.2
  459.4 80.2 %custom-call.19 = f32[4,2,128,128]{2,3,1,0:T(8,128)} custom-call(f32[4,2,128,128]{3,2,1,0:T(8,128)} %bitcast.50), custom_call_target="InvertDiagBlocksLowerTriangular" | custom-call | tf_op jit(solution)/shard_map/triangular_solve | solution.py:9
  539.6 9.5 %fusion.2 = f32[4,128,3584]{2,1,0:T(8,128)S(1)} fusion(f32[4,256,3584]{1,2,0:T(8,128)} %bitcast.46, f32[4,2,128,128]{2,3,1,0:T(8,128)} %custom-call.19), kind=kOutput, calls=%fused_computation.6 | convolution fusion | flops 2818572288 | bytes 14942208 | tf_op jit(solution)/shard_map/triangular_solve | solution.py:9
  549.1 13.9 %fusion.5 = f32[4,128,3584]{1,2,0:T(8,128)} fusion(f32[4,128,3584]{2,1,0:T(8,128)S(1)} %fusion.2, f32[4,256,256]{2,1,0:T(8,128)S(1)} %get-tuple-element.83), kind=kOutput, calls=%fused_computation.14 | convolution fusion | flops 2818572288 | bytes 14942208 | tf_op jit(solution)/shard_map/triangular_solve | solution.py:9
  563.1 11.4 %fusion.1 = f32[4,128,3584]{2,1,0:T(8,128)} fusion(f32[4,128,3584]{1,2,0:T(8,128)} %fusion.5, f32[4,256,3584]{1,2,0:T(8,128)S(1)} %bitcast.49, f32[4,2,128,128]{2,3,1,0:T(8,128)S(1)} %copy-done.3), kind=kOutput, calls=%fused_computation.5 | convolution fusion | flops 2820407296 | bytes 22282240 | tf_op jit(solution)/shard_map/triangular_solve | solution.py:9
  574.5 4.3 fusion
  578.8 2.9 copy-done.2
  581.7 8.4 %convolution_convert_fusion = bf16[4,256,512]{2,1,0:T(8,128)(2,1)} fusion(bf16[4,256,3584]{2,1,0:T(8,128)(2,1)S(1)} %fusion, bf16[4,3584,512]{2,1,0:T(8,128)(2,1)} %param.2), kind=kOutput, calls=%fused_computation.8 | convolution fusion | flops 3758620672 | bytes 23068672 | tf_op jit(solution)/shard_map/mrk,mrc->mkc/dot_general | solution.py:30
  590.1 1.4 dynamic-slice_bitcast_fusion
  591.5 1.0 copy.25
  592.5 29.0 %reduce-scatter.2.cloned.1.call-done = bf16[4,32,512]{2,1,0:T(8,128)(2,1)} async-done(((bf16[4,256,512]{2,1,0:T(8,128)(2,1)}), bf16[4,32,512]{2,1,0:T(8,128)(2,1)}) %reduce-scatter.2.cloned.1.call-update) | async-done | bytes 131088 | tf_op jit(solution)/shard_map/reduce_scatter | solution.py:35
  621.5 1.6 convert_multiply_fusion
  (32 shorter events, 0.5 us)
Async XLA Ops:
  7.2 1.0 copy-start
  7.2 217.2 %all-reduce.4.cloned.1.call-start = ((), (), s32[]{:S(2)}) async-start(), calls=%async_computation.1 | async-start | bytes 29360128 | tf_op jit(solution)/shard_map/psum | solution.py:20
  22.5 293.6 %all-reduce.6.cloned.1.call-start = ((), (), s32[]{:S(2)}) async-start(), calls=%async_computation.2 | async-start | bytes 2097152 | tf_op jit(solution)/shard_map/psum | solution.py:28
  253.8 367.6 %reduce-scatter.2.cloned.1.call-start = ((), (), s32[]{:S(2)}) async-start(), calls=%async_computation.3 | async-start | bytes 1179648 | tf_op jit(solution)/shard_map/reduce_scatter | solution.py:35
  453.8 109.2 %slice-start = ((s8[14680064]{0:T(1024)(128)(4,1)}), s8[2097152]{0:T(1024)(128)(4,1)S(1)}, s32[]{:S(2)}) async-start(s8[14680064]{0:T(1024)(128)(4,1)} %bitcast.47), calls=%async_computation.4 | async-start | bytes 4194304
  539.6 23.4 %slice-start.1 = ((s8[14680064]{0:T(1024)(128)(4,1)}), s8[4194304]{0:T(1024)(128)(4,1)S(1)}, s32[]{:S(2)}) async-start(s8[14680064]{0:T(1024)(128)(4,1)} %bitcast.47), calls=%async_computation.5 | async-start | bytes 8388608
  539.6 23.4 %slice-start.2 = ((s8[14680064]{0:T(1024)(128)(4,1)}), s8[4194304]{0:T(1024)(128)(4,1)S(1)}, s32[]{:S(2)}) async-start(s8[14680064]{0:T(1024)(128)(4,1)} %bitcast.47), calls=%async_computation.6 | async-start | bytes 8388608
  549.1 13.9 %slice-start.3 = ((s8[14680064]{0:T(1024)(128)(4,1)}), s8[4194304]{0:T(1024)(128)(4,1)S(1)}, s32[]{:S(2)}) async-start(s8[14680064]{0:T(1024)(128)(4,1)} %bitcast.47), calls=%async_computation.7 | async-start | bytes 8388608
  549.1 13.9 %copy-start.3 = (f32[4,2,128,128]{2,3,1,0:T(8,128)S(1)}, f32[4,2,128,128]{2,3,1,0:T(8,128)}, u32[]{:S(2)}) copy-start(f32[4,2,128,128]{2,3,1,0:T(8,128)} %custom-call.19) | copy-start | bytes 1572868
  578.8 2.9 copy-start.2
  581.7 41.4 %copy-start.1 = (bf16[512,256]{1,0:T(8,128)(2,1)S(1)}, bf16[512,256]{1,0:T(8,128)(2,1)}, u32[]{:S(2)}) copy-start(bf16[512,256]{1,0:T(8,128)(2,1)} %param.3) | copy-start | bytes 786436
Sparse Core Ops, SparseCore 0:
  22.6 201.7 all-reduce.3
  254.0 62.0 all-reduce.5
  590.3 31.1 reduce-scatter.1
where the time goes:
time: 634 us; the launch traced here: 630 us
  waiting for transfers between devices  292 us (46%)
  other arithmetic  221 us (35%)
  matrix products  88 us (14%)
  between operations  14.2 us (2%)
  local copies, waits for them, and re-layouts  13.5 us (2%)
    psum x1, waiting for transfers between devices, local(): sketched = lax.psum(term, 'mat')  201 us
    another operation x9, other arithmetic, factor(): lower = jnp.linalg.cholesky(gram)  133 us
    another operation x4, other arithmetic, factor(): lax.linalg.triangular_solve(lower, jnp.swapaxes(sketched_rows, 1, 2), lef...  80.5 us
    psum x1, waiting for transfers between devices, local(): gram = lax.psum(gram_part, 'row')  61.9 us
    another operation x3, matrix products, factor(): lax.linalg.triangular_solve(lower, jnp.swapaxes(sketched_rows, 1, 2), lef...  34.8 us
    dot_general x1, matrix products, local(): jnp.einsum('mrk,mrl->mkl', sketched, sketched, precision=lax.Precision.HI...  29.5 us
    reduce_scatter x1, waiting for transfers between devices, local(): lax.psum_scatter(partial_proj.astype(jnp.bfloat16), 'row', scatter_dimens...  29 us
    dot_general x1, matrix products, local(): jnp.einsum('mrc,ck->mrk', gradients, sketch, preferred_element_type=jnp.f...  14.3 us
  transfers between devices with their start and end apart: 3, of which 3 were waited for; matrix products, arithmetic and copies ran while one was open for 0% of the time, Pallas kernels for 0%

commit v1 on v0

v1 whole, which is shorter than its diff:
```python
import functools

import jax
import jax.numpy as jnp
from jax import lax
from jax.experimental import pallas as pl
from jax.experimental.pallas import tpu as pltpu
from jax.sharding import PartitionSpec as P

MATS, RANK, SHARE, WIDTH, SHARES, RING = 4, 256, 224, 512, 16, 4
HALF = RANK // 2
BLOCK = RANK // 8
OFFS = (0, 1, 3, 2)
F32, BF16 = jnp.float32, jnp.bfloat16
EXACT = lax.Precision.HIGHEST
NEWTON_TOL = 1e-4
NEWTON_MAX = 10


def params():
    return pltpu.CompilerParams(vmem_limit_bytes=52 * 1024 * 1024)


def shift(value, axis, step):
    pairs = []
    if axis in ("y", "z"):
        for z in range(RING):
            for y in range(RING):
                to = z * RING + (y + step) % RING if axis == "y" else (z + step) % RING * RING + y
                pairs.append((z * RING + y, to))
        return lax.ppermute(value, "mat", pairs)
    for x in range(RING):
        for core in range(2):
            to = (x + step) % RING * 2 + core if axis == "x" else x * 2 + (core + step) % 2
            pairs.append((x * 2 + core, to))
    return lax.ppermute(value, "row", pairs)


def place():
    row, mat = lax.axis_index("row"), lax.axis_index("mat")
    return row // 2, row % 2, mat % RING, mat // RING


def chunk_row(index, along, dest):
    _, _, y, z = place()
    if along == "y":
        shares = [(z + off) % RING * RING + dest % RING for off in OFFS]
    else:
        shares = [dest % RING * RING + (y + off) % RING for off in OFFS]
    return jnp.stack([jnp.asarray(v, jnp.int32) for v in [index] + shares])


def gradient_specs(step=lambda *ids: ids[0]):
    return [
        pl.BlockSpec(
            (1, 1, SHARE, WIDTH),
            lambda *a, j=j: (a[-1][step(*a[:-1]), 0], a[-1][step(*a[:-1]), 1 + j], 0, 0),
        )
        for j in range(RING)
    ]


def sketch_kernel(tab, g0, g1, g2, g3, sk, *rest):
    out = rest[-1]
    for j, g in enumerate((g0, g1, g2, g3)):
        term = jnp.dot(g[0, 0], sk[...], preferred_element_type=F32)
        for other in rest[:-1]:
            term = term + other[0, j].astype(F32)
        out[0, j] = term.astype(out.dtype)


def sketch_chunks(grads, sketch, rows, recv=None):
    count = len(rows)
    block = (1, RING, SHARE, RANK)
    extra = [] if recv is None else [recv]
    return pl.pallas_call(
        sketch_kernel,
        grid_spec=pltpu.PrefetchScalarGridSpec(
            num_scalar_prefetch=1,
            grid=(count,),
            in_specs=gradient_specs()
            + [pl.BlockSpec((WIDTH, RANK), lambda n, t: (0, 0))]
            + [pl.BlockSpec(block, lambda n, t: (0, 0, 0, 0)) for _ in extra],
            out_specs=pl.BlockSpec(block, lambda n, t: (n, 0, 0, 0)),
        ),
        out_shape=jax.ShapeDtypeStruct((count,) + block[1:], BF16),
        compiler_params=params(),
    )(jnp.stack(rows), grads, grads, grads, grads, sketch, *extra)


def own_kernel(tab, g0, g1, g2, g3, sk, comb0, comb1, near0, near1, own, ahead, behind, across):
    first = pl.program_id(0) == 0

    def run(comb, near):
        for j, (g, out) in enumerate(zip((g0, g1, g2, g3), (own, ahead, behind, across))):
            term = jnp.dot(g[0, 0], sk[...], preferred_element_type=F32)
            term = term + comb[0, j].astype(F32) + near[0, j].astype(F32)
            out[0] = term.astype(out.dtype)

    pl.when(first)(lambda: run(comb0, near0))
    pl.when(jnp.logical_not(first))(lambda: run(comb1, near1))


def own_chunks(grads, sketch, rows, combs, nears):
    block = (1, RING, SHARE, RANK)
    share = pl.BlockSpec((1, SHARE, RANK), lambda n, t: (n, 0, 0))
    return pl.pallas_call(
        own_kernel,
        grid_spec=pltpu.PrefetchScalarGridSpec(
            num_scalar_prefetch=1,
            grid=(2,),
            in_specs=gradient_specs()
            + [pl.BlockSpec((WIDTH, RANK), lambda n, t: (0, 0))]
            + [pl.BlockSpec(block, lambda n, t: (0, 0, 0, 0))] * 2
            + [pl.BlockSpec(block, lambda n, t: (1, 0, 0, 0))] * 2,
            out_specs=[share] * 4,
        ),
        out_shape=[jax.ShapeDtypeStruct((2, SHARE, RANK), F32)]
        + [jax.ShapeDtypeStruct((2, SHARE, RANK), BF16)] * 3,
        compiler_params=params(),
    )(jnp.stack(rows), grads, grads, grads, grads, sketch, *combs, *nears)


def total_kernel(own, a, b, c, total, rounded, gram):
    value = own[0] + a[0].astype(F32) + b[0].astype(F32) + c[0].astype(F32)
    total[0] = value
    rounded[0] = value.astype(BF16)
    gram[0] = lax.dot_general(
        value, value, (((0,), (0,)), ((), ())), precision=EXACT, preferred_element_type=F32
    )


def totals(own, parts):
    share = pl.BlockSpec((1, SHARE, RANK), lambda n: (n, 0, 0))
    return pl.pallas_call(
        total_kernel,
        grid=(2,),
        in_specs=[share] * 4,
        out_specs=[share, share, pl.BlockSpec((1, RANK, RANK), lambda n: (n, 0, 0))],
        out_shape=[
            jax.ShapeDtypeStruct((2, SHARE, RANK), F32),
            jax.ShapeDtypeStruct((2, SHARE, RANK), BF16),
            jax.ShapeDtypeStruct((2, RANK, RANK), F32),
        ],
        compiler_params=params(),
    )(own, *parts)


def accumulate(chunk, grads):
    total = None
    for j, g in enumerate(grads):
        term = lax.dot_general(
            chunk[0, j], g[0, 0], (((0,), (0,)), ((), ())), preferred_element_type=F32
        )
        total = term if total is None else total + term
    return total


def gather_kernel(tab, g0, g1, g2, g3, c0, c1, c2, out):
    step = pl.program_id(1)
    grads = (g0, g1, g2, g3)

    @pl.when(step == 0)
    def _():
        out[0] = accumulate(c0, grads)

    @pl.when(step == 1)
    def _():
        out[0] += accumulate(c1, grads)

    @pl.when(step == 2)
    def _():
        out[0] += accumulate(c2, grads)


def project_three(grads, rows, chunks):
    block = (1, RING, SHARE, RANK)
    return pl.pallas_call(
        gather_kernel,
        grid_spec=pltpu.PrefetchScalarGridSpec(
            num_scalar_prefetch=1,
            grid=(2, 3),
            in_specs=gradient_specs(lambda m, k: m * 3 + k)
            + [pl.BlockSpec(block, lambda m, k, t: (m, 0, 0, 0))] * 3,
            out_specs=pl.BlockSpec((1, RANK, WIDTH), lambda m, k, t: (m, 0, 0)),
        ),
        out_shape=jax.ShapeDtypeStruct((2, RANK, WIDTH), F32),
        compiler_params=params(),
    )(jnp.stack(rows), grads, grads, grads, grads, *chunks)


def last_kernel(ranks, tab, g0, g1, g2, g3, c0, c1, part, inv, mine, theirs, rows, whole):
    first = pl.program_id(0) == 0
    grads = (g0, g1, g2, g3)

    @pl.when(first)
    def _():
        whole[...] = part[0] + accumulate(c0, grads)

    @pl.when(jnp.logical_not(first))
    def _():
        whole[...] = part[0] + accumulate(c1, grads)

    for b in range(8):
        start = pl.multiple_of(ranks[b] * BLOCK, BLOCK)
        rows[b * BLOCK : (b + 1) * BLOCK] = inv[0, pl.ds(start, BLOCK), :]
    out = jnp.dot(rows[...], whole[...], precision=EXACT, preferred_element_type=F32)
    mine[0] = out[:HALF]
    theirs[0] = out[HALF:].astype(BF16)


def project_last(grads, rows, chunks, part, inverse, pair, ranks):
    block = (1, RING, SHARE, RANK)
    return pl.pallas_call(
        last_kernel,
        grid_spec=pltpu.PrefetchScalarGridSpec(
            num_scalar_prefetch=2,
            grid=(2,),
            in_specs=gradient_specs(lambda n, r: n)
            + [pl.BlockSpec(block, lambda n, r, t: (0, 0, 0, 0))] * 2
            + [pl.BlockSpec((1, RANK, WIDTH), lambda n, r, t: (n, 0, 0))]
            + [pl.BlockSpec((1, RANK, RANK), lambda n, r, t: (pair * 2 + n, 0, 0))],
            out_specs=[pl.BlockSpec((1, HALF, WIDTH), lambda n, r, t: (n, 0, 0))] * 2,
            scratch_shapes=[pltpu.VMEM((RANK, RANK), F32), pltpu.VMEM((RANK, WIDTH), F32)],
        ),
        out_shape=[
            jax.ShapeDtypeStruct((2, HALF, WIDTH), F32),
            jax.ShapeDtypeStruct((2, HALF, WIDTH), BF16),
        ],
        compiler_params=params(),
    )(ranks, jnp.stack(rows), grads, grads, grads, grads, *chunks, part, inverse)


def basis_kernel(root, s, inv, out):
    value = lax.dot_general(
        s[0], inv[0], (((1,), (1,)), ((), ())), precision=EXACT, preferred_element_type=F32
    )
    out[0] = (value * root).astype(BF16)


def make_basis(total, inverse, pair, root):
    share = pl.BlockSpec((1, SHARE, RANK), lambda n: (n, 0, 0))
    return pl.pallas_call(
        functools.partial(basis_kernel, root),
        grid=(2,),
        in_specs=[share, pl.BlockSpec((1, RANK, RANK), lambda n: (pair * 2 + n, 0, 0))],
        out_specs=share,
        out_shape=jax.ShapeDtypeStruct((2, SHARE, RANK), BF16),
        compiler_params=params(),
    )(total, inverse)


def inverse_kernel(where, own, other, out, gram, scaled):
    x, core = where[0], where[1]
    for j, off in enumerate(OFFS):
        q = lax.rem(x + off, RING)
        half = pl.multiple_of(lax.rem(q, 2) * HALF, HALF)
        gram[core * 2 + q // 2, pl.ds(half, HALF), :] = own[j]
        gram[(1 - core) * 2 + q // 2, pl.ds(half, HALF), :] = other[j]
    rows = lax.broadcasted_iota(jnp.int32, (RANK, RANK), 0)
    cols = lax.broadcasted_iota(jnp.int32, (RANK, RANK), 1)
    eye = (rows == cols).astype(F32)
    weight = jnp.where(rows > cols, 1.0, 0.5 * eye)

    def diagonal(a, axis):
        return jnp.sum(jnp.where(rows == cols, a, 0.0), axis=axis, keepdims=True)

    def residual(value, a, precision):
        if precision is None:
            value = value.astype(BF16)
            a = a.astype(BF16)
        half = jnp.dot(value, a, precision=precision, preferred_element_type=F32)
        if precision is None:
            half = half.astype(BF16)
        return (
            lax.dot_general(
                half, value, (((1,), (1,)), ((), ())), precision=precision, preferred_element_type=F32
            )
            - eye
        )

    for m in range(MATS):
        a = gram[m]
        scaled[m] = a * lax.rsqrt(diagonal(a, 1)) * lax.rsqrt(diagonal(a, 0))
    for m in range(MATS):
        out[m] = eye - weight * (scaled[m] - eye)
    for _ in range(2):
        for m in range(MATS):
            value = out[m]
            error = (weight * residual(value, scaled[m], None)).astype(BF16)
            out[m] = value - jnp.dot(error, value.astype(BF16), preferred_element_type=F32)

    def exact_step(carry):
        count, _ = carry
        large = jnp.zeros((RANK, RANK), F32)
        for m in range(MATS):
            value = out[m]
            error = residual(value, scaled[m], EXACT)
            large = jnp.maximum(large, jnp.where(error == error, jnp.abs(error), 1e9))
            large = jnp.maximum(large, jnp.where((rows == cols) & (value <= 0.0), 1e9, 0.0))
            out[m] = value - jnp.dot(weight * error, value, precision=EXACT, preferred_element_type=F32)
        return count + 1, jnp.max(large)

    _, left = lax.while_loop(
        lambda c: (c[0] < NEWTON_MAX) & (c[1] > NEWTON_TOL) & (c[1] < 1e8),
        exact_step,
        (jnp.int32(0), jnp.float32(1.0)),
    )
    done = left <= NEWTON_TOL

    @pl.when(done)
    def _():
        for m in range(MATS):
            out[m] = out[m] * lax.rsqrt(diagonal(gram[m], 0))

    @pl.when(jnp.logical_not(done))
    def _():
        row_ids = lax.broadcasted_iota(jnp.int32, (RANK, 1), 0)
        col_ids = lax.broadcasted_iota(jnp.int32, (1, RANK), 1)

        def matrix(m, _):
            out[m] = eye

            def column(j, _):
                pivot_row = gram[m, pl.ds(j, 1), :]
                pivot = jnp.sum(jnp.where(col_ids == j, pivot_row, 0.0), axis=1, keepdims=True)
                values = jnp.sum(jnp.where(cols == j, gram[m], 0.0), axis=1, keepdims=True)
                factor = jnp.where(row_ids > j, values / pivot, 0.0)
                known = out[m, pl.ds(j, 1), :]
                gram[m] = gram[m] - factor * pivot_row
                out[m] = out[m] - factor * known
                out[m, pl.ds(j, 1), :] = known / jnp.sqrt(pivot)
                return 0

            return lax.fori_loop(0, RANK, column, 0)

        lax.fori_loop(0, MATS, matrix, 0)


def inverse_factors(where, own, other):
    return pl.pallas_call(
        inverse_kernel,
        grid_spec=pltpu.PrefetchScalarGridSpec(
            num_scalar_prefetch=1,
            grid=(1,),
            in_specs=[pl.BlockSpec((RING, HALF, RANK), lambda n, w: (0, 0, 0))] * 2,
            out_specs=pl.BlockSpec((MATS, RANK, RANK), lambda n, w: (0, 0, 0)),
            scratch_shapes=[
                pltpu.VMEM((MATS, RANK, RANK), F32),
                pltpu.VMEM((MATS, RANK, RANK), F32),
            ],
        ),
        out_shape=jax.ShapeDtypeStruct((MATS, RANK, RANK), F32),
        compiler_params=params(),
    )(where, own, other)


def from_others(value, axis):
    return [shift(value, axis, -1), shift(value, axis, 1), shift(value, axis, 2)]


def sum_and_factor(gram01, gram23):
    x, core, _, _ = place()
    first = core == 0
    keep = jnp.where(first, gram01, gram23)
    send = jnp.where(first, gram23, gram01)
    pair = (keep + shift(send, "core", 1)).reshape(RING, HALF, RANK)

    def piece(off):
        return lax.dynamic_index_in_dim(pair, (x + off) % RING, 0, keepdims=False)

    arrived = [shift(piece(1), "x", 1), shift(piece(3), "x", -1), shift(piece(2), "x", 2)]
    part = piece(0) + arrived[0] + arrived[1] + arrived[2]
    for axis in ("y", "z"):
        a, b, c = from_others(part, axis)
        part = part + a + b + c
    own = jnp.stack([part] + from_others(part, "x"))
    other = shift(own, "core", 1)
    return inverse_factors(jnp.stack([x, core]).astype(jnp.int32), own, other)


def local(gradients, sketch):
    root = float(gradients.shape[1] * lax.axis_size("row")) ** 0.5
    grads = gradients.reshape(MATS, SHARES, SHARE, WIDTH)
    x, core, y, z = place()
    here = {"y": y, "z": z}
    pairs = (("y", "z"), ("z", "y"))

    hop1 = {}
    for sign in (1, -1):
        for p, (ring, _) in enumerate(pairs):
            far, near = (2 * p, 2 * p + 1) if sign == 1 else (2 * p + 1, 2 * p)
            rows = [
                chunk_row(far, ring, here[ring] + 2),
                chunk_row(near, ring, here[ring] + (sign % RING)),
            ]
            hop1[p, sign] = shift(sketch_chunks(grads, sketch, rows), ring, sign)
    hop2 = {}
    for sign in (1, -1):
        for p, (ring, _) in enumerate(pairs):
            far = 2 * p if sign == 1 else 2 * p + 1
            rows = [chunk_row(far, ring, here[ring] + (sign % RING))]
            hop2[p, sign] = shift(sketch_chunks(grads, sketch, rows, hop1[p, sign]), ring, sign)
    total, rounded, gram = [], [], []
    for p, (ring, cross) in enumerate(pairs):
        rows = [chunk_row(2 * p + i, ring, here[ring]) for i in range(2)]
        own, ahead, behind, across = own_chunks(
            grads, sketch, rows, (hop2[p, 1], hop2[p, -1]), (hop1[p, -1], hop1[p, 1])
        )
        parts = [shift(ahead, cross, 1), shift(behind, cross, -1), shift(across, cross, 2)]
        outs = totals(own, parts)
        for store, value in zip((total, rounded, gram), outs):
            store.append(value)

    inverse = sum_and_factor(*gram)

    ranks = [(x + off) % RING * 2 + core for off in OFFS]
    ranks += [(x + off) % RING * 2 + 1 - core for off in OFFS]
    ranks = jnp.stack(ranks).astype(jnp.int32)
    chunks, nexts, backs, befores, afters = [], [], [], [], []
    for p, (ring, cross) in enumerate(pairs):
        chunks.append(jnp.stack([rounded[p]] + from_others(rounded[p], cross), axis=1))
    for p, (ring, _) in enumerate(pairs):
        befores.append(shift(chunks[p], ring, 1))
        afters.append(shift(chunks[p], ring, -1))
    for p, (ring, _) in enumerate(pairs):
        nexts.append(shift(befores[p][0:1], ring, 1))
        backs.append(shift(afters[p][1:2], ring, -1))
    mine, theirs, basis = [], [], []
    for p, (ring, _) in enumerate(pairs):
        rows = [chunk_row(2 * p + i, ring, here[ring] + off) for i in range(2) for off in (0, 3, 1)]
        part = project_three(grads, rows, (chunks[p], befores[p], afters[p]))
        rows = [chunk_row(2 * p + i, ring, here[ring] + 2) for i in range(2)]
        a, b = project_last(grads, rows, (nexts[p], backs[p]), part, inverse, p, ranks)
        mine.append(a.reshape(2, RING, BLOCK, WIDTH))
        theirs.append(shift(b, "core", 1).reshape(2, RING, BLOCK, WIDTH))
        basis.append(make_basis(total[p], inverse, p, root))
    both = jnp.concatenate(
        [m + t.astype(F32) for m, t in zip(mine, theirs)], axis=0
    )
    out = both[:, 0]
    for j, step in ((1, 1), (2, -1), (3, 2)):
        out = out + shift(both[:, j].astype(BF16), "x", step).astype(F32)
    return jnp.concatenate(basis, axis=0), out


def solution(mesh):
    placed = (P(None, "row", "mat"), P("mat", None))
    return jax.shard_map(
        local,
        mesh=mesh,
        in_specs=placed,
        out_specs=(P(None, ("row", "mat"), None), P(None, "row", "mat")),
        check_vma=False,
    )
```

time: 634 us -> 220 us (0.35)
  waiting for transfers between devices: 292 us -> 60.2 us
  other arithmetic: 221 us -> 4.52 us
  matrix products: 88 us -> 0 us
  Pallas kernels: 0 us -> 74.5 us
  starting transfers between devices: 0.82 us -> 68.7 us
  between operations: 14.2 us -> 1.25 us
    psum x2 -> x0, waiting for transfers between devices: 263 us -> none  [the longest x1 201 us: local(): sketched = lax.psum(term, 'mat')]
    another operation x13 -> x8, other arithmetic: 214 us -> 0.38 us  [the longest x2 0.23 us: local(): jnp.stack([rounded[p]] + from_others(rounded[p], cross), axis=1)]
    pallas_call x0 -> x19, Pallas kernels: none -> 74.5 us  [the longest x8 24 us: sketch_chunks(): pl.pallas_call(sketch_kernel, grid_spec=pltpu.PrefetchScalarGridSpec(num_...]
    ppermute x0 -> x47, starting transfers between devices: none -> 68.7 us  [the longest x34 57.9 us: shift(): return lax.ppermute(value, 'mat', pairs)]
    ppermute x0 -> x47, waiting for transfers between devices: none -> 60.2 us  [the longest x34 36.9 us: shift(): return lax.ppermute(value, 'mat', pairs)]
    dot_general x3 -> x0, matrix products: 52.2 us -> none  [the longest x1 29.5 us: local(): jnp.einsum('mrk,mrl->mkl', sketched, sketched, precision=lax.Precision.HI...]
    another operation x5 -> x0, matrix products: 35.8 us -> none  [the longest x3 34.8 us: factor(): lax.linalg.triangular_solve(lower, jnp.swapaxes(sketched_rows, 1, 2), lef...]
    reduce_scatter x1 -> x0, waiting for transfers between devices: 29 us -> none  [local(): lax.psum_scatter(partial_proj.astype(jnp.bfloat16), 'row', scatter_dimens...]
  transfers between devices with their start and end apart: 3 -> 47, of which waited for: 3 -> 22; matrix products, arithmetic and copies ran while one was open for 0% -> 3% of each run, Pallas kernels for 0% -> 32%
where the time goes in v1:
time: 220 us; the launch traced here: 218 us
  Pallas kernels  74.5 us (34%)
  starting transfers between devices  68.7 us (31%)
  waiting for transfers between devices  60.2 us (27%)
  local copies, waits for them, and re-layouts  8.99 us (4%)
  other arithmetic  4.52 us (2%)
    ppermute x34, starting transfers between devices, shift(): return lax.ppermute(value, 'mat', pairs)  57.9 us
    ppermute x34, waiting for transfers between devices, shift(): return lax.ppermute(value, 'mat', pairs)  36.9 us
    pallas_call x8, Pallas kernels, sketch_chunks(): pl.pallas_call(sketch_kernel, grid_spec=pltpu.PrefetchScalarGridSpec(num_...  24 us
    ppermute x13, waiting for transfers between devices, shift(): return lax.ppermute(value, 'row', pairs)  23.4 us
    pallas_call x2, Pallas kernels, project_three(): pl.pallas_call(gather_kernel, grid_spec=pltpu.PrefetchScalarGridSpec(num_...  15.3 us
    pallas_call x1, Pallas kernels, inverse_factors(): pl.pallas_call(inverse_kernel, grid_spec=pltpu.PrefetchScalarGridSpec(num...  13.1 us
    ppermute x13, starting transfers between devices, shift(): return lax.ppermute(value, 'row', pairs)  10.8 us
    pallas_call x2, Pallas kernels, project_last(): pl.pallas_call(last_kernel, grid_spec=pltpu.PrefetchScalarGridSpec(num_sc...  9.86 us
  transfers between devices with their start and end apart: 47, of which 22 were waited for; matrix products, arithmetic and copies ran while one was open for 3% of the time, Pallas kernels for 32%

profile of v1, /device:TPU:0, one launch (start us, length us, event | category | flops | bytes accessed | tf_op | source)
XLA Modules:
  0.0 218.2 jit_solution(5285890566375430659)
XLA Ops:
  2.6 3.5 %shard_map.47 = bf16[2,4,224,256]{3,2,1,0:T(8,128)(2,1)} custom-call(s32[2,5]{1,0:T(2,128)S(1)} %get-tuple-element.49.tab, bf16[4,16,224,512]{3,2,1,0:T(8,128)(2,1)} %bitcast.94, bf16[4,16,224,512]{3,2,1,0:T(8,128)(2,1)} %bitcast.95, bf16[4,16,224,512]{3,2,1,0:T(8,128)(2,1)} %bitcast.96, bf16[4,16,224,512]{3,2,1,0:T(8,128)(2,1)} %bitcast.97, ...), custom_call_target="tpu_custom_call" | custom-call | tf_op jit(solution)/shard_map/pallas_call | solution.py:76
  8.2 3.5 %shard_map.49 = bf16[2,4,224,256]{3,2,1,0:T(8,128)(2,1)} custom-call(s32[2,5]{1,0:T(2,128)S(1)} %get-tuple-element.48.tab, bf16[4,16,224,512]{3,2,1,0:T(8,128)(2,1)} %bitcast.98, bf16[4,16,224,512]{3,2,1,0:T(8,128)(2,1)} %bitcast.99, bf16[4,16,224,512]{3,2,1,0:T(8,128)(2,1)} %bitcast.100, bf16[4,16,224,512]{3,2,1,0:T(8,128)(2,1)} %bitcast.101, ...), custom_call_target="tpu_custom_call" | custom-call | tf_op jit(solution)/shard_map/pallas_call | solution.py:76
  14.8 3.6 %shard_map.41 = bf16[2,4,224,256]{3,2,1,0:T(8,128)(2,1)} custom-call(s32[2,5]{1,0:T(2,128)S(1)} %get-tuple-element.46.tab, bf16[4,16,224,512]{3,2,1,0:T(8,128)(2,1)} %bitcast.105, bf16[4,16,224,512]{3,2,1,0:T(8,128)(2,1)} %bitcast.103, bf16[4,16,224,512]{3,2,1,0:T(8,128)(2,1)} %bitcast.104, bf16[4,16,224,512]{3,2,1,0:T(8,128)(2,1)} %bitcast.102, ...), custom_call_target="tpu_custom_call" | custom-call | tf_op jit(solution)/shard_map/pallas_call | solution.py:76
  19.9 3.5 %shard_map.43 = bf16[2,4,224,256]{3,2,1,0:T(8,128)(2,1)} custom-call(s32[2,5]{1,0:T(2,128)S(1)} %get-tuple-element.45.tab, bf16[4,16,224,512]{3,2,1,0:T(8,128)(2,1)} %bitcast.106, bf16[4,16,224,512]{3,2,1,0:T(8,128)(2,1)} %bitcast.107, bf16[4,16,224,512]{3,2,1,0:T(8,128)(2,1)} %bitcast.108, bf16[4,16,224,512]{3,2,1,0:T(8,128)(2,1)} %bitcast.109, ...), custom_call_target="tpu_custom_call" | custom-call | tf_op jit(solution)/shard_map/pallas_call | solution.py:76
  25.3 5.6 %collective-permute-done.7.rest_0_.near1 = bf16[2,4,224,256]{3,2,1,0:T(8,128)(2,1)S(1)} collective-permute-done((bf16[2,4,224,256]{3,2,1,0:T(8,128)(2,1)}, bf16[2,4,224,256]{3,2,1,0:T(8,128)(2,1)S(1)}, u32[]{:S(2)}, u32[]{:S(2)}) %collective-permute-start.7) | collective-permute-done | bytes 917536 | tf_op jit(solution)/shard_map/ppermute | solution.py:31
  30.8 3.0 %shard_map.48 = bf16[1,4,224,256]{3,2,1,0:T(8,128)(2,1)} custom-call(s32[1,5]{1,0:T(1,128)S(1)} %bitcast.90, bf16[4,16,224,512]{3,2,1,0:T(8,128)(2,1)} %bitcast.110, bf16[4,16,224,512]{3,2,1,0:T(8,128)(2,1)} %bitcast.111, bf16[4,16,224,512]{3,2,1,0:T(8,128)(2,1)} %bitcast.112, bf16[4,16,224,512]{3,2,1,0:T(8,128)(2,1)} %bitcast.113, ...), custom_call_target="tpu_custom_call" | custom-call | tf_op jit(solution)/shard_map/pallas_call | solution.py:76
  36.1 3.5 %collective-permute-start.10 = (bf16[1,4,224,256]{3,2,1,0:T(8,128)(2,1)S(1)}, bf16[1,4,224,256]{3,2,1,0:T(8,128)(2,1)}, u32[]{:S(2)}, u32[]{:S(2)}) collective-permute-start(bf16[1,4,224,256]{3,2,1,0:T(8,128)(2,1)S(1)} %shard_map.50), channel_id=1, source_target_pairs={{0,12},{1,13},{2,14},{3,15},{4,0},{5,1},{6,2},{7,3},{8,4},{9,5},{1... | collective-permute-start | bytes 1376264 | tf_op jit(solution)/shard_map/ppermute | solution.py:31
  45.3 2.4 %shard_map.44 = bf16[1,4,224,256]{3,2,1,0:T(8,128)(2,1)S(1)} custom-call(s32[1,5]{1,0:T(1,128)S(1)} %bitcast.88, bf16[4,16,224,512]{3,2,1,0:T(8,128)(2,1)} %bitcast.122, bf16[4,16,224,512]{3,2,1,0:T(8,128)(2,1)} %bitcast.123, bf16[4,16,224,512]{3,2,1,0:T(8,128)(2,1)} %bitcast.124, bf16[4,16,224,512]{3,2,1,0:T(8,128)(2,1)} %bitcast.125, ...), custom_call_target="tpu_custom_call" | custom-call | tf_op jit(solution)/shard_map/pallas_call | solution.py:76
  47.7 3.0 %collective-permute-start.3 = (bf16[1,4,224,256]{3,2,1,0:T(8,128)(2,1)S(1)}, bf16[1,4,224,256]{3,2,1,0:T(8,128)(2,1)}, u32[]{:S(2)}, u32[]{:S(2)}) collective-permute-start(bf16[1,4,224,256]{3,2,1,0:T(8,128)(2,1)S(1)} %shard_map.44), channel_id=1, source_target_pairs={{0,3},{1,0},{2,1},{3,2},{4,7},{5,4},{6,5},{7,6},{8,11},{9,8},{10,9... | collective-permute-start | bytes 1376264 | tf_op jit(solution)/shard_map/ppermute | solution.py:31
  50.9 4.0 %shard_map.51 = (f32[2,224,256]{2,1,0:T(8,128)S(1)}, bf16[2,224,256]{2,1,0:T(8,128)(2,1)}, bf16[2,224,256]{2,1,0:T(8,128)(2,1)}, bf16[2,224,256]{2,1,0:T(8,128)(2,1)S(1)}) custom-call(s32[2,5]{1,0:T(2,128)S(1)} %pad_add_fusion.6.tab, bf16[4,16,224,512]{3,2,1,0:T(8,128)(2,1)} %bitcast.126, bf16[4,16,224,512]{3,2,1,0:T(8,128)(2,1)} %bitcast.127, ...), custom_call_target="tpu_custom_call" | custom-call | tf_op jit(solution)/shard_map/pallas_call | solution.py:107
  55.7 3.3 %collective-permute-start.12 = (bf16[2,224,256]{2,1,0:T(8,128)(2,1)}, bf16[2,224,256]{2,1,0:T(8,128)(2,1)S(1)}, u32[]{:S(2)}, u32[]{:S(2)}) collective-permute-start(bf16[2,224,256]{2,1,0:T(8,128)(2,1)} %get-tuple-element.28), channel_id=1, source_target_pairs={{0,3},{1,0},{2,1},{3,2},{4,7},{5,4},{6,5},{7,6},{8,11},{9,8},{10,9... | collective-permute-start | bytes 688136 | tf_op jit(solution)/shard_map/ppermute | solution.py:31
  60.9 3.3 %shard_map.45 = (f32[2,224,256]{2,1,0:T(8,128)S(1)}, bf16[2,224,256]{2,1,0:T(8,128)(2,1)S(1)}, bf16[2,224,256]{2,1,0:T(8,128)(2,1)S(1)}, bf16[2,224,256]{2,1,0:T(8,128)(2,1)S(1)}) custom-call(s32[2,5]{1,0:T(2,128)S(1)} %pad_add_fusion.4.tab, bf16[4,16,224,512]{3,2,1,0:T(8,128)(2,1)} %bitcast.130, bf16[4,16,224,512]{3,2,1,0:T(8,128)(2,1)} %bitcast.131, ...), custom_call_target="tpu_custom_call" | custom-call | tf_op jit(solution)/shard_map/pallas_call | solution.py:107
  64.3 3.2 %collective-permute-start.5 = (bf16[2,224,256]{2,1,0:T(8,128)(2,1)S(1)}, bf16[2,224,256]{2,1,0:T(8,128)(2,1)S(1)}, u32[]{:S(2)}, u32[]{:S(2)}) collective-permute-start(bf16[2,224,256]{2,1,0:T(8,128)(2,1)S(1)} %get-tuple-element.22), channel_id=1, source_target_pairs={{0,12},{1,13},{2,14},{3,15},{4,0},{5,1},{6,2},{7,3},{8,4},{9,5},{1... | collective-permute-start | bytes 688136 | tf_op jit(solution)/shard_map/ppermute | solution.py:31
  82.1 3.1 %collective-permute-start.17 = (f32[128,256]{1,0:T(8,128)S(1)}, f32[128,256]{1,0:T(8,128)S(1)}, u32[]{:S(2)}, u32[]{:S(2)}) collective-permute-start(f32[128,256]{1,0:T(8,128)S(1)} %get-tuple-element.42), channel_id=1, source_target_pairs={{0,64},{16,80},{32,96},{48,112},{64,0},{80,16},{96,32},{112,48},{1... | collective-permute-start | bytes 393224 | tf_op jit(solution)/shard_map/ppermute | solution.py:36
  87.2 2.5 %collective-permute-start.38 = (bf16[2,224,256]{2,1,0:T(8,128)(2,1)S(1)}, bf16[2,224,256]{2,1,0:T(8,128)(2,1)S(1)}, u32[]{:S(2)}, u32[]{:S(2)}) collective-permute-start(bf16[2,224,256]{2,1,0:T(8,128)(2,1)S(1)} %get-tuple-element.35), channel_id=1, source_target_pairs={{0,2},{1,3},{2,0},{3,1},{4,6},{5,7},{6,4},{7,5},{8,10},{9,11},{10,... | collective-permute-start | bytes 688136 | tf_op jit(solution)/shard_map/ppermute | solution.py:31
  93.8 2.8 %collective-permute-start.29 = (bf16[2,224,256]{2,1,0:T(8,128)(2,1)S(1)}, bf16[2,224,256]{2,1,0:T(8,128)(2,1)S(1)}, u32[]{:S(2)}, u32[]{:S(2)}) collective-permute-start(bf16[2,224,256]{2,1,0:T(8,128)(2,1)S(1)} %get-tuple-element.32), channel_id=1, source_target_pairs={{0,4},{1,5},{2,6},{3,7},{4,8},{5,9},{6,10},{7,11},{8,12},{9,13},{1... | collective-permute-start | bytes 688136 | tf_op jit(solution)/shard_map/ppermute | solution.py:31
  97.3 2.6 %collective-permute-start.20 = (f32[128,256]{1,0:T(8,128)S(1)}, f32[128,256]{1,0:T(8,128)S(1)}, u32[]{:S(2)}, u32[]{:S(2)}) collective-permute-start(f32[128,256]{1,0:T(8,128)S(1)} %fusion.4), channel_id=1, source_target_pairs={{0,2},{1,3},{2,0},{3,1},{4,6},{5,7},{6,4},{7,5},{8,10},{9,11},{10,... | collective-permute-start | bytes 393224 | tf_op jit(solution)/shard_map/ppermute | solution.py:31
  102.9 2.4 %collective-permute-start.18 = (f32[128,256]{1,0:T(8,128)S(1)}, f32[128,256]{1,0:T(8,128)S(1)}, u32[]{:S(2)}, u32[]{:S(2)}) collective-permute-start(f32[128,256]{1,0:T(8,128)S(1)} %fusion.4), channel_id=1, source_target_pairs={{0,3},{1,0},{2,1},{3,2},{4,7},{5,4},{6,5},{7,6},{8,11},{9,8},{10,9... | collective-permute-start | bytes 393224 | tf_op jit(solution)/shard_map/ppermute | solution.py:31
  113.8 3.7 %collective-permute-start.21 = (f32[128,256]{1,0:T(8,128)S(1)}, f32[128,256]{1,0:T(8,128)S(1)}, u32[]{:S(2)}, u32[]{:S(2)}) collective-permute-start(f32[128,256]{1,0:T(8,128)S(1)} %add_add_fusion.1), channel_id=1, source_target_pairs={{0,12},{1,13},{2,14},{3,15},{4,0},{5,1},{6,2},{7,3},{8,4},{9,5},{1... | collective-permute-start | bytes 393224 | tf_op jit(solution)/shard_map/ppermute | solution.py:31
  117.6 16.6 %collective-permute-done.23 = f32[128,256]{1,0:T(8,128)S(1)} collective-permute-done((f32[128,256]{1,0:T(8,128)S(1)}, f32[128,256]{1,0:T(8,128)S(1)}, u32[]{:S(2)}, u32[]{:S(2)}) %collective-permute-start.23) | collective-permute-done | bytes 131104 | tf_op jit(solution)/shard_map/ppermute | solution.py:31
  138.9 5.1 %collective-permute-done.26 = f32[128,256]{1,0:T(8,128)S(1)} collective-permute-done((f32[128,256]{1,0:T(8,128)S(1)}, f32[128,256]{1,0:T(8,128)S(1)}, u32[]{:S(2)}, u32[]{:S(2)}) %collective-permute-start.26) | collective-permute-done | bytes 131104 | tf_op jit(solution)/shard_map/ppermute | solution.py:36
  144.0 6.2 %collective-permute-done.25 = f32[128,256]{1,0:T(8,128)S(1)} collective-permute-done((f32[128,256]{1,0:T(8,128)S(1)}, f32[128,256]{1,0:T(8,128)S(1)}, u32[]{:S(2)}, u32[]{:S(2)}) %collective-permute-start.25) | collective-permute-done | bytes 131104 | tf_op jit(solution)/shard_map/ppermute | solution.py:36
  151.1 4.1 %collective-permute-done.24 = f32[128,256]{1,0:T(8,128)S(1)} collective-permute-done((f32[128,256]{1,0:T(8,128)S(1)}, f32[128,256]{1,0:T(8,128)S(1)}, u32[]{:S(2)}, u32[]{:S(2)}) %collective-permute-start.24) | collective-permute-done | bytes 131104 | tf_op jit(solution)/shard_map/ppermute | solution.py:36
  156.2 4.4 %collective-permute-start.40 = (bf16[1,4,224,256]{3,2,1,0:T(8,128)(2,1)}, bf16[1,4,224,256]{3,2,1,0:T(8,128)(2,1)}, u32[]{:S(2)}, u32[]{:S(2)}) collective-permute-start(bf16[1,4,224,256]{3,2,1,0:T(8,128)(2,1)} %slice.37), channel_id=1, source_target_pairs={{0,4},{1,5},{2,6},{3,7},{4,8},{5,9},{6,10},{7,11},{8,12},{9,13},{1... | collective-permute-start | bytes 1376264 | tf_op jit(solution)/shard_map/ppermute | solution.py:31
  163.7 3.0 %collective-permute-start.34 = (bf16[1,4,224,256]{3,2,1,0:T(8,128)(2,1)}, bf16[1,4,224,256]{3,2,1,0:T(8,128)(2,1)}, u32[]{:S(2)}, u32[]{:S(2)}) collective-permute-start(bf16[1,4,224,256]{3,2,1,0:T(8,128)(2,1)} %slice.36), channel_id=1, source_target_pairs={{0,3},{1,0},{2,1},{3,2},{4,7},{5,4},{6,5},{7,6},{8,11},{9,8},{10,9... | collective-permute-start | bytes 1376264 | tf_op jit(solution)/shard_map/ppermute | solution.py:31
  166.8 7.7 %shard_map.58.part = f32[2,256,512]{2,1,0:T(8,128)} custom-call(s32[6,5]{1,0:T(8,128)S(1)} %stack.483.tab, bf16[4,16,224,512]{3,2,1,0:T(8,128)(2,1)} %bitcast.134, bf16[4,16,224,512]{3,2,1,0:T(8,128)(2,1)} %bitcast.135, bf16[4,16,224,512]{3,2,1,0:T(8,128)(2,1)} %bitcast.136, bf16[4,16,224,512]{3,2,1,0:T(8,128)(2,1)} %bitcast.137, ...), custom_call_target="tpu_custom_call" | custom-call | tf_op jit(solution)/shard_map/pallas_call | solution.py:178
  174.5 13.1 %shard_map.53.inv = f32[4,256,256]{2,1,0:T(8,128)} custom-call(s32[2]{0:T(128)S(1)} %pad_add_fusion.8.where, f32[4,128,256]{2,1,0:T(8,128)S(1)} %pad_maximum_fusion.3.own, f32[4,128,256]{2,1,0:T(8,128)} %collective-permute-done.27.other), custom_call_target="tpu_custom_call" | custom-call | tf_op jit(solution)/shard_map/pallas_call | solution.py:341
  187.7 4.9 %shard_map.59 = (f32[2,128,512]{2,1,0:T(8,128)S(1)}, bf16[2,128,512]{2,1,0:T(8,128)(2,1)S(1)}) custom-call(s32[8]{0:T(128)S(1)} %stack.469.ranks, s32[2,5]{1,0:T(2,128)S(1)} %get-tuple-element.47.tab, bf16[4,16,224,512]{3,2,1,0:T(8,128)(2,1)} %bitcast.138, bf16[4,16,224,512]{3,2,1,0:T(8,128)(2,1)} %bitcast.139, bf16[4,16,224,512]{3,2,1,0:T(8,128)(2,1)} %bitcast.140, ...), custom_call_target="tpu_custom_call" | custom-call | tf_op jit(solution)/shard_map/pallas_call | solution.py:214
  192.8 7.7 %shard_map.56.part = f32[2,256,512]{2,1,0:T(8,128)} custom-call(s32[6,5]{1,0:T(8,128)S(1)} %stack.476.tab, bf16[4,16,224,512]{3,2,1,0:T(8,128)(2,1)} %bitcast.142, bf16[4,16,224,512]{3,2,1,0:T(8,128)(2,1)} %bitcast.143, bf16[4,16,224,512]{3,2,1,0:T(8,128)(2,1)} %bitcast.144, bf16[4,16,224,512]{3,2,1,0:T(8,128)(2,1)} %bitcast.145, ...), custom_call_target="tpu_custom_call" | custom-call | tf_op jit(solution)/shard_map/pallas_call | solution.py:178
  200.5 4.9 %shard_map.57 = (f32[2,128,512]{2,1,0:T(8,128)S(1)}, bf16[2,128,512]{2,1,0:T(8,128)(2,1)S(1)}) custom-call(s32[8]{0:T(128)S(1)} %stack.469.ranks, s32[2,5]{1,0:T(2,128)S(1)} %get-tuple-element.44.tab, bf16[4,16,224,512]{3,2,1,0:T(8,128)(2,1)} %bitcast.146, bf16[4,16,224,512]{3,2,1,0:T(8,128)(2,1)} %bitcast.147, bf16[4,16,224,512]{3,2,1,0:T(8,128)(2,1)} %bitcast.148, ...), custom_call_target="tpu_custom_call" | custom-call | tf_op jit(solution)/shard_map/pallas_call | solution.py:214
  207.4 2.3 %collective-permute-start.45 = (bf16[4,32,512]{2,1,0:T(8,128)(2,1)S(1)}, bf16[4,32,512]{2,1,0:T(8,128)(2,1)S(1)}, u32[]{:S(2)}, u32[]{:S(2)}) collective-permute-start(bf16[4,32,512]{2,1,0:T(8,128)(2,1)S(1)} %get-tuple-element.40), channel_id=1, source_target_pairs={{0,96},{16,112},{32,0},{48,16},{64,32},{80,48},{96,64},{112,80},{1... | collective-permute-start | bytes 393224 | tf_op jit(solution)/shard_map/ppermute | solution.py:36
  212.4 2.8 %collective-permute-done.46 = bf16[4,32,512]{2,1,0:T(8,128)(2,1)S(1)} collective-permute-done((bf16[4,32,512]{2,1,0:T(8,128)(2,1)S(1)}, bf16[4,32,512]{2,1,0:T(8,128)(2,1)S(1)}, u32[]{:S(2)}, u32[]{:S(2)}) %collective-permute-start.46) | collective-permute-done | bytes 131104 | tf_op jit(solution)/shard_map/ppermute | solution.py:36
  (169 shorter events, 71.7 us)
Async XLA Ops:
  6.2 24.7 %collective-permute-start.7 = (bf16[2,4,224,256]{3,2,1,0:T(8,128)(2,1)}, bf16[2,4,224,256]{3,2,1,0:T(8,128)(2,1)S(1)}, u32[]{:S(2)}, u32[]{:S(2)}) collective-permute-start(bf16[2,4,224,256]{3,2,1,0:T(8,128)(2,1)} %shard_map.47), channel_id=1, source_target_pairs={{0,4},{1,5},{2,6},{3,7},{4,8},{5,9},{6,10},{7,11},{8,12},{9,13},{1... | collective-permute-start | bytes 2752520 | tf_op jit(solution)/shard_map/ppermute | solution.py:31
  11.7 22.2 %collective-permute-start.9 = (bf16[2,4,224,256]{3,2,1,0:T(8,128)(2,1)}, bf16[2,4,224,256]{3,2,1,0:T(8,128)(2,1)S(1)}, u32[]{:S(2)}, u32[]{:S(2)}) collective-permute-start(bf16[2,4,224,256]{3,2,1,0:T(8,128)(2,1)} %shard_map.49), channel_id=1, source_target_pairs={{0,12},{1,13},{2,14},{3,15},{4,0},{5,1},{6,2},{7,3},{8,4},{9,5},{1... | collective-permute-start | bytes 2752520 | tf_op jit(solution)/shard_map/ppermute | solution.py:31
  18.3 23.3 %collective-permute-start = (bf16[2,4,224,256]{3,2,1,0:T(8,128)(2,1)}, bf16[2,4,224,256]{3,2,1,0:T(8,128)(2,1)S(1)}, u32[]{:S(2)}, u32[]{:S(2)}) collective-permute-start(bf16[2,4,224,256]{3,2,1,0:T(8,128)(2,1)} %shard_map.41), channel_id=1, source_target_pairs={{0,1},{1,2},{2,3},{3,0},{4,5},{5,6},{6,7},{7,4},{8,9},{9,10},{10,1... | collective-permute-start | bytes 2752520 | tf_op jit(solution)/shard_map/ppermute | solution.py:31
  23.4 21.8 %collective-permute-start.2 = (bf16[2,4,224,256]{3,2,1,0:T(8,128)(2,1)}, bf16[2,4,224,256]{3,2,1,0:T(8,128)(2,1)}, u32[]{:S(2)}, u32[]{:S(2)}) collective-permute-start(bf16[2,4,224,256]{3,2,1,0:T(8,128)(2,1)} %shard_map.43), channel_id=1, source_target_pairs={{0,3},{1,0},{2,1},{3,2},{4,7},{5,4},{6,5},{7,6},{8,11},{9,8},{10,9... | collective-permute-start | bytes 2752520 | tf_op jit(solution)/shard_map/ppermute | solution.py:31
  33.8 17.0 %collective-permute-start.8 = (bf16[1,4,224,256]{3,2,1,0:T(8,128)(2,1)}, bf16[1,4,224,256]{3,2,1,0:T(8,128)(2,1)S(1)}, u32[]{:S(2)}, u32[]{:S(2)}) collective-permute-start(bf16[1,4,224,256]{3,2,1,0:T(8,128)(2,1)} %shard_map.48), channel_id=1, source_target_pairs={{0,4},{1,5},{2,6},{3,7},{4,8},{5,9},{6,10},{7,11},{8,12},{9,13},{1... | collective-permute-start | bytes 1376264 | tf_op jit(solution)/shard_map/ppermute | solution.py:31
  36.1 14.7 %collective-permute-start.10 = (bf16[1,4,224,256]{3,2,1,0:T(8,128)(2,1)S(1)}, bf16[1,4,224,256]{3,2,1,0:T(8,128)(2,1)}, u32[]{:S(2)}, u32[]{:S(2)}) collective-permute-start(bf16[1,4,224,256]{3,2,1,0:T(8,128)(2,1)S(1)} %shard_map.50), channel_id=1, source_target_pairs={{0,12},{1,13},{2,14},{3,15},{4,0},{5,1},{6,2},{7,3},{8,4},{9,5},{1... | collective-permute-start | bytes 1376264 | tf_op jit(solution)/shard_map/ppermute | solution.py:31
  43.9 15.2 %collective-permute-start.1 = (bf16[1,4,224,256]{3,2,1,0:T(8,128)(2,1)S(1)}, bf16[1,4,224,256]{3,2,1,0:T(8,128)(2,1)S(1)}, u32[]{:S(2)}, u32[]{:S(2)}) collective-permute-start(bf16[1,4,224,256]{3,2,1,0:T(8,128)(2,1)S(1)} %shard_map.42), channel_id=1, source_target_pairs={{0,1},{1,2},{2,3},{3,0},{4,5},{5,6},{6,7},{7,4},{8,9},{9,10},{10,1... | collective-permute-start | bytes 1376264 | tf_op jit(solution)/shard_map/ppermute | solution.py:31
  47.7 13.2 %collective-permute-start.3 = (bf16[1,4,224,256]{3,2,1,0:T(8,128)(2,1)S(1)}, bf16[1,4,224,256]{3,2,1,0:T(8,128)(2,1)}, u32[]{:S(2)}, u32[]{:S(2)}) collective-permute-start(bf16[1,4,224,256]{3,2,1,0:T(8,128)(2,1)S(1)} %shard_map.44), channel_id=1, source_target_pairs={{0,3},{1,0},{2,1},{3,2},{4,7},{5,4},{6,5},{7,6},{8,11},{9,8},{10,9... | collective-permute-start | bytes 1376264 | tf_op jit(solution)/shard_map/ppermute | solution.py:31
  55.5 12.4 %collective-permute-start.11 = (bf16[2,224,256]{2,1,0:T(8,128)(2,1)}, bf16[2,224,256]{2,1,0:T(8,128)(2,1)S(1)}, u32[]{:S(2)}, u32[]{:S(2)}) collective-permute-start(bf16[2,224,256]{2,1,0:T(8,128)(2,1)} %get-tuple-element.27), channel_id=1, source_target_pairs={{0,1},{1,2},{2,3},{3,0},{4,5},{5,6},{6,7},{7,4},{8,9},{9,10},{10,1... | collective-permute-start | bytes 688136 | tf_op jit(solution)/shard_map/ppermute | solution.py:31
  55.7 13.7 %collective-permute-start.12 = (bf16[2,224,256]{2,1,0:T(8,128)(2,1)}, bf16[2,224,256]{2,1,0:T(8,128)(2,1)S(1)}, u32[]{:S(2)}, u32[]{:S(2)}) collective-permute-start(bf16[2,224,256]{2,1,0:T(8,128)(2,1)} %get-tuple-element.28), channel_id=1, source_target_pairs={{0,3},{1,0},{2,1},{3,2},{4,7},{5,4},{6,5},{7,6},{8,11},{9,8},{10,9... | collective-permute-start | bytes 688136 | tf_op jit(solution)/shard_map/ppermute | solution.py:31
  59.0 10.5 %collective-permute-start.13 = (bf16[2,224,256]{2,1,0:T(8,128)(2,1)}, bf16[2,224,256]{2,1,0:T(8,128)(2,1)S(1)}, u32[]{:S(2)}, u32[]{:S(2)}) collective-permute-start(bf16[2,224,256]{2,1,0:T(8,128)(2,1)} %copy-done.12), channel_id=1, source_target_pairs={{0,2},{1,3},{2,0},{3,1},{4,6},{5,7},{6,4},{7,5},{8,10},{9,11},{10,... | collective-permute-start | bytes 688136 | tf_op jit(solution)/shard_map/ppermute | solution.py:31
  64.3 9.3 %collective-permute-start.5 = (bf16[2,224,256]{2,1,0:T(8,128)(2,1)S(1)}, bf16[2,224,256]{2,1,0:T(8,128)(2,1)S(1)}, u32[]{:S(2)}, u32[]{:S(2)}) collective-permute-start(bf16[2,224,256]{2,1,0:T(8,128)(2,1)S(1)} %get-tuple-element.22), channel_id=1, source_target_pairs={{0,12},{1,13},{2,14},{3,15},{4,0},{5,1},{6,2},{7,3},{8,4},{9,5},{1... | collective-permute-start | bytes 688136 | tf_op jit(solution)/shard_map/ppermute | solution.py:31
  82.1 9.5 %collective-permute-start.17 = (f32[128,256]{1,0:T(8,128)S(1)}, f32[128,256]{1,0:T(8,128)S(1)}, u32[]{:S(2)}, u32[]{:S(2)}) collective-permute-start(f32[128,256]{1,0:T(8,128)S(1)} %get-tuple-element.42), channel_id=1, source_target_pairs={{0,64},{16,80},{32,96},{48,112},{64,0},{80,16},{96,32},{112,48},{1... | collective-permute-start | bytes 393224 | tf_op jit(solution)/shard_map/ppermute | solution.py:36
  87.2 10.0 %collective-permute-start.38 = (bf16[2,224,256]{2,1,0:T(8,128)(2,1)S(1)}, bf16[2,224,256]{2,1,0:T(8,128)(2,1)S(1)}, u32[]{:S(2)}, u32[]{:S(2)}) collective-permute-start(bf16[2,224,256]{2,1,0:T(8,128)(2,1)S(1)} %get-tuple-element.35), channel_id=1, source_target_pairs={{0,2},{1,3},{2,0},{3,1},{4,6},{5,7},{6,4},{7,5},{8,10},{9,11},{10,... | collective-permute-start | bytes 688136 | tf_op jit(solution)/shard_map/ppermute | solution.py:31
  89.7 12.1 %collective-permute-start.37 = (bf16[2,224,256]{2,1,0:T(8,128)(2,1)S(1)}, bf16[2,224,256]{2,1,0:T(8,128)(2,1)S(1)}, u32[]{:S(2)}, u32[]{:S(2)}) collective-permute-start(bf16[2,224,256]{2,1,0:T(8,128)(2,1)S(1)} %get-tuple-element.35), channel_id=1, source_target_pairs={{0,1},{1,2},{2,3},{3,0},{4,5},{5,6},{6,7},{7,4},{8,9},{9,10},{10,1... | collective-permute-start | bytes 688136 | tf_op jit(solution)/shard_map/ppermute | solution.py:31
  91.6 11.3 %collective-permute-start.36 = (bf16[2,224,256]{2,1,0:T(8,128)(2,1)S(1)}, bf16[2,224,256]{2,1,0:T(8,128)(2,1)S(1)}, u32[]{:S(2)}, u32[]{:S(2)}) collective-permute-start(bf16[2,224,256]{2,1,0:T(8,128)(2,1)S(1)} %get-tuple-element.35), channel_id=1, source_target_pairs={{0,3},{1,0},{2,1},{3,2},{4,7},{5,4},{6,5},{7,6},{8,11},{9,8},{10,9... | collective-permute-start | bytes 688136 | tf_op jit(solution)/shard_map/ppermute | solution.py:31
  93.5 17.8 %collective-permute-start.30 = (bf16[2,224,256]{2,1,0:T(8,128)(2,1)S(1)}, bf16[2,224,256]{2,1,0:T(8,128)(2,1)S(1)}, u32[]{:S(2)}, u32[]{:S(2)}) collective-permute-start(bf16[2,224,256]{2,1,0:T(8,128)(2,1)S(1)} %get-tuple-element.32), channel_id=1, source_target_pairs={{0,8},{1,9},{2,10},{3,11},{4,12},{5,13},{6,14},{7,15},{8,0},{9,1},... | collective-permute-start | bytes 688136 | tf_op jit(solution)/shard_map/ppermute | solution.py:31
  93.8 18.4 %collective-permute-start.29 = (bf16[2,224,256]{2,1,0:T(8,128)(2,1)S(1)}, bf16[2,224,256]{2,1,0:T(8,128)(2,1)S(1)}, u32[]{:S(2)}, u32[]{:S(2)}) collective-permute-start(bf16[2,224,256]{2,1,0:T(8,128)(2,1)S(1)} %get-tuple-element.32), channel_id=1, source_target_pairs={{0,4},{1,5},{2,6},{3,7},{4,8},{5,9},{6,10},{7,11},{8,12},{9,13},{1... | collective-permute-start | bytes 688136 | tf_op jit(solution)/shard_map/ppermute | solution.py:31
  108.0 47.3 %collective-permute-start.39 = (bf16[2,4,224,256]{3,2,1,0:T(8,128)(2,1)S(1)}, bf16[2,4,224,256]{3,2,1,0:T(8,128)(2,1)S(1)}, u32[]{:S(2)}, u32[]{:S(2)}) collective-permute-start(bf16[2,4,224,256]{3,2,1,0:T(8,128)(2,1)S(1)} %pad_maximum_fusion.2.c0), channel_id=1, source_target_pairs={{0,4},{1,5},{2,6},{3,7},{4,8},{5,9},{6,10},{7,11},{8,12},{9,13},{1... | collective-permute-start | bytes 2752520 | tf_op jit(solution)/shard_map/ppermute | solution.py:31
  109.2 51.4 %collective-permute-start.41 = (bf16[2,4,224,256]{3,2,1,0:T(8,128)(2,1)S(1)}, bf16[2,4,224,256]{3,2,1,0:T(8,128)(2,1)S(1)}, u32[]{:S(2)}, u32[]{:S(2)}) collective-permute-start(bf16[2,4,224,256]{3,2,1,0:T(8,128)(2,1)S(1)} %pad_maximum_fusion.2.c0), channel_id=1, source_target_pairs={{0,12},{1,13},{2,14},{3,15},{4,0},{5,1},{6,2},{7,3},{8,4},{9,5},{1... | collective-permute-start | bytes 2752520 | tf_op jit(solution)/shard_map/ppermute | solution.py:31
  111.3 22.9 %collective-permute-start.23 = (f32[128,256]{1,0:T(8,128)S(1)}, f32[128,256]{1,0:T(8,128)S(1)}, u32[]{:S(2)}, u32[]{:S(2)}) collective-permute-start(f32[128,256]{1,0:T(8,128)S(1)} %add_add_fusion.1), channel_id=1, source_target_pairs={{0,8},{1,9},{2,10},{3,11},{4,12},{5,13},{6,14},{7,15},{8,0},{9,1},... | collective-permute-start | bytes 393224 | tf_op jit(solution)/shard_map/ppermute | solution.py:31
  112.2 23.3 %collective-permute-start.22 = (f32[128,256]{1,0:T(8,128)S(1)}, f32[128,256]{1,0:T(8,128)S(1)}, u32[]{:S(2)}, u32[]{:S(2)}) collective-permute-start(f32[128,256]{1,0:T(8,128)S(1)} %add_add_fusion.1), channel_id=1, source_target_pairs={{0,4},{1,5},{2,6},{3,7},{4,8},{5,9},{6,10},{7,11},{8,12},{9,13},{1... | collective-permute-start | bytes 393224 | tf_op jit(solution)/shard_map/ppermute | solution.py:31
  113.8 23.7 %collective-permute-start.21 = (f32[128,256]{1,0:T(8,128)S(1)}, f32[128,256]{1,0:T(8,128)S(1)}, u32[]{:S(2)}, u32[]{:S(2)}) collective-permute-start(f32[128,256]{1,0:T(8,128)S(1)} %add_add_fusion.1), channel_id=1, source_target_pairs={{0,12},{1,13},{2,14},{3,15},{4,0},{5,1},{6,2},{7,3},{8,4},{9,5},{1... | collective-permute-start | bytes 393224 | tf_op jit(solution)/shard_map/ppermute | solution.py:31
  134.2 27.3 %collective-permute-start.31 = (bf16[2,4,224,256]{3,2,1,0:T(8,128)(2,1)S(1)}, bf16[2,4,224,256]{3,2,1,0:T(8,128)(2,1)S(1)}, u32[]{:S(2)}, u32[]{:S(2)}) collective-permute-start(bf16[2,4,224,256]{3,2,1,0:T(8,128)(2,1)S(1)} %pad_maximum_fusion.1.c0), channel_id=1, source_target_pairs={{0,1},{1,2},{2,3},{3,0},{4,5},{5,6},{6,7},{7,4},{8,9},{9,10},{10,1... | collective-permute-start | bytes 2752520 | tf_op jit(solution)/shard_map/ppermute | solution.py:31
  135.6 26.8 %collective-permute-start.33 = (bf16[2,4,224,256]{3,2,1,0:T(8,128)(2,1)S(1)}, bf16[2,4,224,256]{3,2,1,0:T(8,128)(2,1)S(1)}, u32[]{:S(2)}, u32[]{:S(2)}) collective-permute-start(bf16[2,4,224,256]{3,2,1,0:T(8,128)(2,1)S(1)} %pad_maximum_fusion.1.c0), channel_id=1, source_target_pairs={{0,3},{1,0},{2,1},{3,2},{4,7},{5,4},{6,5},{7,6},{8,11},{9,8},{10,9... | collective-permute-start | bytes 2752520 | tf_op jit(solution)/shard_map/ppermute | solution.py:31
  155.2 19.3 %collective-permute-start.27 = (f32[4,128,256]{2,1,0:T(8,128)S(1)}, f32[4,128,256]{2,1,0:T(8,128)}, u32[]{:S(2)}, u32[]{:S(2)}) collective-permute-start(f32[4,128,256]{2,1,0:T(8,128)S(1)} %pad_maximum_fusion.3.own), channel_id=1, source_target_pairs={{0,16},{16,0},{32,48},{48,32},{64,80},{80,64},{96,112},{112,96},{1... | collective-permute-start | bytes 1572872 | tf_op jit(solution)/shard_map/ppermute | solution.py:36
  156.2 31.5 %collective-permute-start.40 = (bf16[1,4,224,256]{3,2,1,0:T(8,128)(2,1)}, bf16[1,4,224,256]{3,2,1,0:T(8,128)(2,1)}, u32[]{:S(2)}, u32[]{:S(2)}) collective-permute-start(bf16[1,4,224,256]{3,2,1,0:T(8,128)(2,1)} %slice.37), channel_id=1, source_target_pairs={{0,4},{1,5},{2,6},{3,7},{4,8},{5,9},{6,10},{7,11},{8,12},{9,13},{1... | collective-permute-start | bytes 1376264 | tf_op jit(solution)/shard_map/ppermute | solution.py:31
  161.4 26.2 %collective-permute-start.42 = (bf16[1,4,224,256]{3,2,1,0:T(8,128)(2,1)}, bf16[1,4,224,256]{3,2,1,0:T(8,128)(2,1)}, u32[]{:S(2)}, u32[]{:S(2)}) collective-permute-start(bf16[1,4,224,256]{3,2,1,0:T(8,128)(2,1)} %slice.38), channel_id=1, source_target_pairs={{0,12},{1,13},{2,14},{3,15},{4,0},{5,1},{6,2},{7,3},{8,4},{9,5},{1... | collective-permute-start | bytes 1376264 | tf_op jit(solution)/shard_map/ppermute | solution.py:31
  162.3 38.1 %collective-permute-start.32 = (bf16[1,4,224,256]{3,2,1,0:T(8,128)(2,1)}, bf16[1,4,224,256]{3,2,1,0:T(8,128)(2,1)}, u32[]{:S(2)}, u32[]{:S(2)}) collective-permute-start(bf16[1,4,224,256]{3,2,1,0:T(8,128)(2,1)} %slice.35), channel_id=1, source_target_pairs={{0,1},{1,2},{2,3},{3,0},{4,5},{5,6},{6,7},{7,4},{8,9},{9,10},{10,1... | collective-permute-start | bytes 1376264 | tf_op jit(solution)/shard_map/ppermute | solution.py:31
  163.7 36.8 %collective-permute-start.34 = (bf16[1,4,224,256]{3,2,1,0:T(8,128)(2,1)}, bf16[1,4,224,256]{3,2,1,0:T(8,128)(2,1)}, u32[]{:S(2)}, u32[]{:S(2)}) collective-permute-start(bf16[1,4,224,256]{3,2,1,0:T(8,128)(2,1)} %slice.36), channel_id=1, source_target_pairs={{0,3},{1,0},{2,1},{3,2},{4,7},{5,4},{6,5},{7,6},{8,11},{9,8},{10,9... | collective-permute-start | bytes 1376264 | tf_op jit(solution)/shard_map/ppermute | solution.py:31
  192.6 13.3 %collective-permute-start.43 = (bf16[2,128,512]{2,1,0:T(8,128)(2,1)S(1)}, bf16[2,128,512]{2,1,0:T(8,128)(2,1)S(1)}, u32[]{:S(2)}, u32[]{:S(2)}) collective-permute-start(bf16[2,128,512]{2,1,0:T(8,128)(2,1)S(1)} %get-tuple-element.37), channel_id=1, source_target_pairs={{0,16},{16,0},{32,48},{48,32},{64,80},{80,64},{96,112},{112,96},{1... | collective-permute-start | bytes 786440 | tf_op jit(solution)/shard_map/ppermute | solution.py:36
  207.4 9.0 %collective-permute-start.45 = (bf16[4,32,512]{2,1,0:T(8,128)(2,1)S(1)}, bf16[4,32,512]{2,1,0:T(8,128)(2,1)S(1)}, u32[]{:S(2)}, u32[]{:S(2)}) collective-permute-start(bf16[4,32,512]{2,1,0:T(8,128)(2,1)S(1)} %get-tuple-element.40), channel_id=1, source_target_pairs={{0,96},{16,112},{32,0},{48,16},{64,32},{80,48},{96,64},{112,80},{1... | collective-permute-start | bytes 393224 | tf_op jit(solution)/shard_map/ppermute | solution.py:36
  (38 other events, 375.5 us)

commit v2 on v1

--- a/solution.py
+++ b/solution.py
@@ -19,6 +19,10 @@
 
 def params():
     return pltpu.CompilerParams(vmem_limit_bytes=52 * 1024 * 1024)
+
+
+def cost(flops, moved):
+    return pl.CostEstimate(flops=int(flops), bytes_accessed=int(moved), transcendentals=0)
 
 
 def shift(value, axis, step):
@@ -60,49 +64,81 @@
     ]
 
 
-def sketch_kernel(tab, g0, g1, g2, g3, sk, *rest):
-    out = rest[-1]
-    for j, g in enumerate((g0, g1, g2, g3)):
-        term = jnp.dot(g[0, 0], sk[...], preferred_element_type=F32)
-        for other in rest[:-1]:
-            term = term + other[0, j].astype(F32)
-        out[0, j] = term.astype(out.dtype)
-
-
-def sketch_chunks(grads, sketch, rows, recv=None):
-    count = len(rows)
-    block = (1, RING, SHARE, RANK)
-    extra = [] if recv is None else [recv]
+def sketch_of(grads, sk):
+    rows = jnp.concatenate([g[0, 0] for g in grads], axis=0)
+    return jnp.dot(rows, sk[...], preferred_element_type=F32)
+
+
+CHUNK = RING * SHARE
+CHUNK_FLOPS = 2 * CHUNK * WIDTH * RANK
+CHUNK_BYTES = 2 * CHUNK * (WIDTH + 2 * RANK)
+CHUNK_BLOCK = (1, CHUNK, RANK)
+
+
+def sketch_kernel(tab, g0, g1, g2, g3, sk, out0, out1):
+    def run(out):
+        out[0] = sketch_of((g0, g1, g2, g3), sk).astype(BF16)
+
+    pl.when(pl.program_id(0) < 2)(lambda: run(out0))
+    pl.when(pl.program_id(0) >= 2)(lambda: run(out1))
+
+
+def sketch_chunks(grads, sketch, rows):
     return pl.pallas_call(
         sketch_kernel,
         grid_spec=pltpu.PrefetchScalarGridSpec(
             num_scalar_prefetch=1,
-            grid=(count,),
+            grid=(4,),
+            in_specs=gradient_specs() + [pl.BlockSpec((WIDTH, RANK), lambda n, t: (0, 0))],
+            out_specs=[
+                pl.BlockSpec(CHUNK_BLOCK, lambda n, t: (jnp.minimum(n, 1), 0, 0)),
+                pl.BlockSpec(CHUNK_BLOCK, lambda n, t: (jnp.maximum(n - 2, 0), 0, 0)),
+            ],
+        ),
+        out_shape=[jax.ShapeDtypeStruct((2, CHUNK, RANK), BF16)] * 2,
+        compiler_params=params(),
+        cost_estimate=cost(4 * CHUNK_FLOPS, 4 * CHUNK_BYTES),
+    )(jnp.stack(rows), grads, grads, grads, grads, sketch)
+
+
+def combine_kernel(tab, g0, g1, g2, g3, sk, recv0, recv1, out0, out1):
+    def run(recv, out):
+        term = sketch_of((g0, g1, g2, g3), sk)
+        out[0] = (term + recv[0].astype(F32)).astype(BF16)
+
+    pl.when(pl.program_id(0) == 0)(lambda: run(recv0, out0))
+    pl.when(pl.program_id(0) == 1)(lambda: run(recv1, out1))
+
+
+def combined_chunks(grads, sketch, rows, recvs):
+    block = pl.BlockSpec(CHUNK_BLOCK, lambda n, t: (0, 0, 0))
+    return pl.pallas_call(
+        combine_kernel,
+        grid_spec=pltpu.PrefetchScalarGridSpec(
+            num_scalar_prefetch=1,
+            grid=(2,),
             in_specs=gradient_specs()
-            + [pl.BlockSpec((WIDTH, RANK), lambda n, t: (0, 0))]
-            + [pl.BlockSpec(block, lambda n, t: (0, 0, 0, 0)) for _ in extra],
-            out_specs=pl.BlockSpec(block, lambda n, t: (n, 0, 0, 0)),
+            + [pl.BlockSpec((WIDTH, RANK), lambda n, t: (0, 0)), block, block],
+            out_specs=[block, block],
         ),
-        out_shape=jax.ShapeDtypeStruct((count,) + block[1:], BF16),
-        compiler_params=params(),
-    )(jnp.stack(rows), grads, grads, grads, grads, sketch, *extra)
+        out_shape=[jax.ShapeDtypeStruct((1, CHUNK, RANK), BF16)] * 2,
+        compiler_params=params(),
+        cost_estimate=cost(2 * CHUNK_FLOPS, 2 * CHUNK_BYTES),
+    )(jnp.stack(rows), grads, grads, grads, grads, sketch, *recvs)
 
 
 def own_kernel(tab, g0, g1, g2, g3, sk, comb0, comb1, near0, near1, own, ahead, behind, across):
-    first = pl.program_id(0) == 0
-
     def run(comb, near):
-        for j, (g, out) in enumerate(zip((g0, g1, g2, g3), (own, ahead, behind, across))):
-            term = jnp.dot(g[0, 0], sk[...], preferred_element_type=F32)
-            term = term + comb[0, j].astype(F32) + near[0, j].astype(F32)
-            out[0] = term.astype(out.dtype)
-
-    pl.when(first)(lambda: run(comb0, near0))
-    pl.when(jnp.logical_not(first))(lambda: run(comb1, near1))
+        term = sketch_of((g0, g1, g2, g3), sk)
+        term = term + comb[0].astype(F32) + near[0].astype(F32)
+        for j, out in enumerate((own, ahead, behind, across)):
+            out[0] = term[j * SHARE : (j + 1) * SHARE].astype(out.dtype)
+
+    pl.when(pl.program_id(0) == 0)(lambda: run(comb0, near0))
+    pl.when(pl.program_id(0) == 1)(lambda: run(comb1, near1))
 
 
 def own_chunks(grads, sketch, rows, combs, nears):
-    block = (1, RING, SHARE, RANK)
     share = pl.BlockSpec((1, SHARE, RANK), lambda n, t: (n, 0, 0))
     return pl.pallas_call(
         own_kernel,
@@ -111,13 +147,14 @@
             grid=(2,),
             in_specs=gradient_specs()
             + [pl.BlockSpec((WIDTH, RANK), lambda n, t: (0, 0))]
-            + [pl.BlockSpec(block, lambda n, t: (0, 0, 0, 0))] * 2
-            + [pl.BlockSpec(block, lambda n, t: (1, 0, 0, 0))] * 2,
+            + [pl.BlockSpec(CHUNK_BLOCK, lambda n, t: (0, 0, 0))] * 2
+            + [pl.BlockSpec(CHUNK_BLOCK, lambda n, t: (1, 0, 0))] * 2,
             out_specs=[share] * 4,
         ),
         out_shape=[jax.ShapeDtypeStruct((2, SHARE, RANK), F32)]
         + [jax.ShapeDtypeStruct((2, SHARE, RANK), BF16)] * 3,
         compiler_params=params(),
+        cost_estimate=cost(2 * CHUNK_FLOPS, 2 * CHUNK_BYTES),
     )(jnp.stack(rows), grads, grads, grads, grads, sketch, *combs, *nears)
 
 
@@ -143,92 +180,45 @@
             jax.ShapeDtypeStruct((2, RANK, RANK), F32),
         ],
         compiler_params=params(),
+        cost_estimate=cost(2 * 12 * SHARE * RANK * RANK, 2 * SHARE * RANK * 16),
     )(own, *parts)
 
 
-def accumulate(chunk, grads):
-    total = None
-    for j, g in enumerate(grads):
-        term = lax.dot_general(
-            chunk[0, j], g[0, 0], (((0,), (0,)), ((), ())), preferred_element_type=F32
-        )
-        total = term if total is None else total + term
-    return total
-
-
-def gather_kernel(tab, g0, g1, g2, g3, c0, c1, c2, out):
-    step = pl.program_id(1)
-    grads = (g0, g1, g2, g3)
-
-    @pl.when(step == 0)
-    def _():
-        out[0] = accumulate(c0, grads)
-
-    @pl.when(step == 1)
-    def _():
-        out[0] += accumulate(c1, grads)
-
-    @pl.when(step == 2)
-    def _():
-        out[0] += accumulate(c2, grads)
-
-
-def project_three(grads, rows, chunks):
-    block = (1, RING, SHARE, RANK)
-    return pl.pallas_call(
-        gather_kernel,
-        grid_spec=pltpu.PrefetchScalarGridSpec(
-            num_scalar_prefetch=1,
-            grid=(2, 3),
-            in_specs=gradient_specs(lambda m, k: m * 3 + k)
-            + [pl.BlockSpec(block, lambda m, k, t: (m, 0, 0, 0))] * 3,
-            out_specs=pl.BlockSpec((1, RANK, WIDTH), lambda m, k, t: (m, 0, 0)),
-        ),
-        out_shape=jax.ShapeDtypeStruct((2, RANK, WIDTH), F32),
-        compiler_params=params(),
-    )(jnp.stack(rows), grads, grads, grads, grads, *chunks)
-
-
-def last_kernel(ranks, tab, g0, g1, g2, g3, c0, c1, part, inv, mine, theirs, rows, whole):
-    first = pl.program_id(0) == 0
-    grads = (g0, g1, g2, g3)
-
-    @pl.when(first)
-    def _():
-        whole[...] = part[0] + accumulate(c0, grads)
-
-    @pl.when(jnp.logical_not(first))
-    def _():
-        whole[...] = part[0] + accumulate(c1, grads)
-
+def project_kernel(ranks, s, g, inv, mine, theirs, rows):
+    whole = lax.dot_general(
+        s[0], g[0], (((0,), (0,)), ((), ())), preferred_element_type=F32
+    )
     for b in range(8):
         start = pl.multiple_of(ranks[b] * BLOCK, BLOCK)
         rows[b * BLOCK : (b + 1) * BLOCK] = inv[0, pl.ds(start, BLOCK), :]
-    out = jnp.dot(rows[...], whole[...], precision=EXACT, preferred_element_type=F32)
+    out = jnp.dot(rows[...], whole, precision=EXACT, preferred_element_type=F32)
     mine[0] = out[:HALF]
     theirs[0] = out[HALF:].astype(BF16)
 
 
-def project_last(grads, rows, chunks, part, inverse, pair, ranks):
-    block = (1, RING, SHARE, RANK)
-    return pl.pallas_call(
-        last_kernel,
+def project(gradients, gathered, inverse, ranks):
+    depth = gradients.shape[1]
+    half = pl.BlockSpec((1, HALF, WIDTH), lambda n, r: (n, 0, 0))
+    return pl.pallas_call(
+        project_kernel,
         grid_spec=pltpu.PrefetchScalarGridSpec(
-            num_scalar_prefetch=2,
-            grid=(2,),
-            in_specs=gradient_specs(lambda n, r: n)
-            + [pl.BlockSpec(block, lambda n, r, t: (0, 0, 0, 0))] * 2
-            + [pl.BlockSpec((1, RANK, WIDTH), lambda n, r, t: (n, 0, 0))]
-            + [pl.BlockSpec((1, RANK, RANK), lambda n, r, t: (pair * 2 + n, 0, 0))],
-            out_specs=[pl.BlockSpec((1, HALF, WIDTH), lambda n, r, t: (n, 0, 0))] * 2,
-            scratch_shapes=[pltpu.VMEM((RANK, RANK), F32), pltpu.VMEM((RANK, WIDTH), F32)],
+            num_scalar_prefetch=1,
+            grid=(MATS,),
+            in_specs=[
+                pl.BlockSpec((1, depth, RANK), lambda n, r: (n, 0, 0)),
+                pl.BlockSpec((1, depth, WIDTH), lambda n, r: (n, 0, 0)),
+                pl.BlockSpec((1, RANK, RANK), lambda n, r: (n, 0, 0)),
+            ],
+            out_specs=[half, half],
+            scratch_shapes=[pltpu.VMEM((RANK, RANK), F32)],
         ),
         out_shape=[
-            jax.ShapeDtypeStruct((2, HALF, WIDTH), F32),
-            jax.ShapeDtypeStruct((2, HALF, WIDTH), BF16),
+            jax.ShapeDtypeStruct((MATS, HALF, WIDTH), F32),
+            jax.ShapeDtypeStruct((MATS, HALF, WIDTH), BF16),
         ],
         compiler_params=params(),
-    )(ranks, jnp.stack(rows), grads, grads, grads, grads, *chunks, part, inverse)
+        cost_estimate=cost(MATS * 2 * RANK * WIDTH * (depth + 6 * RANK), MATS * 2 * depth * (WIDTH + RANK)),
+    )(ranks, gathered, gradients, inverse)
 
 
 def basis_kernel(root, s, inv, out):
@@ -238,15 +228,16 @@
     out[0] = (value * root).astype(BF16)
 
 
-def make_basis(total, inverse, pair, root):
+def make_basis(total, inverse, root):
     share = pl.BlockSpec((1, SHARE, RANK), lambda n: (n, 0, 0))
     return pl.pallas_call(
         functools.partial(basis_kernel, root),
-        grid=(2,),
-        in_specs=[share, pl.BlockSpec((1, RANK, RANK), lambda n: (pair * 2 + n, 0, 0))],
+        grid=(MATS,),
+        in_specs=[share, pl.BlockSpec((1, RANK, RANK), lambda n: (n, 0, 0))],
         out_specs=share,
-        out_shape=jax.ShapeDtypeStruct((2, SHARE, RANK), BF16),
-        compiler_params=params(),
+        out_shape=jax.ShapeDtypeStruct((MATS, SHARE, RANK), BF16),
+        compiler_params=params(),
+        cost_estimate=cost(4 * 12 * SHARE * RANK * RANK, 4 * SHARE * RANK * 10),
     )(total, inverse)
 
 
@@ -352,6 +343,7 @@
         ),
         out_shape=jax.ShapeDtypeStruct((MATS, RANK, RANK), F32),
         compiler_params=params(),
+        cost_estimate=cost(12e9, 4 * MATS * RANK * RANK * 4),
     )(where, own, other)
 
 
@@ -359,11 +351,8 @@
     return [shift(value, axis, -1), shift(value, axis, 1), shift(value, axis, 2)]
 
 
-def sum_and_factor(gram01, gram23):
+def sum_and_factor(send, keep):
     x, core, _, _ = place()
-    first = core == 0
-    keep = jnp.where(first, gram01, gram23)
-    send = jnp.where(first, gram23, gram01)
     pair = (keep + shift(send, "core", 1)).reshape(RING, HALF, RANK)
 
     def piece(off):
@@ -388,60 +377,50 @@
 
     hop1 = {}
     for sign in (1, -1):
+        rows = []
         for p, (ring, _) in enumerate(pairs):
             far, near = (2 * p, 2 * p + 1) if sign == 1 else (2 * p + 1, 2 * p)
-            rows = [
+            rows += [
                 chunk_row(far, ring, here[ring] + 2),
                 chunk_row(near, ring, here[ring] + (sign % RING)),
             ]
-            hop1[p, sign] = shift(sketch_chunks(grads, sketch, rows), ring, sign)
+        for p, sent in enumerate(sketch_chunks(grads, sketch, rows)):
+            hop1[p, sign] = shift(sent, pairs[p][0], sign)
     hop2 = {}
     for sign in (1, -1):
+        rows = []
         for p, (ring, _) in enumerate(pairs):
             far = 2 * p if sign == 1 else 2 * p + 1
-            rows = [chunk_row(far, ring, here[ring] + (sign % RING))]
-            hop2[p, sign] = shift(sketch_chunks(grads, sketch, rows, hop1[p, sign]), ring, sign)
-    total, rounded, gram = [], [], []
+            rows.append(chunk_row(far, ring, here[ring] + (sign % RING)))
+        sums = combined_chunks(grads, sketch, rows, (hop1[0, sign], hop1[1, sign]))
+        for p, sent in enumerate(sums):
+            hop2[p, sign] = shift(sent, pairs[p][0], sign)
+    hop2 = dict(zip(hop2, lax.optimization_barrier(tuple(hop2.values()))))
+    owns, parts = [], []
     for p, (ring, cross) in enumerate(pairs):
         rows = [chunk_row(2 * p + i, ring, here[ring]) for i in range(2)]
         own, ahead, behind, across = own_chunks(
             grads, sketch, rows, (hop2[p, 1], hop2[p, -1]), (hop1[p, -1], hop1[p, 1])
         )
-        parts = [shift(ahead, cross, 1), shift(behind, cross, -1), shift(across, cross, 2)]
-        outs = totals(own, parts)
-        for store, value in zip((total, rounded, gram), outs):
-            store.append(value)
-
-    inverse = sum_and_factor(*gram)
+        owns.append(own)
+        parts.append([shift(ahead, cross, 1), shift(behind, cross, -1), shift(across, cross, 2)])
+    total, rounded, gram = zip(*(totals(own, arrived) for own, arrived in zip(owns, parts)))
+    send = jnp.where(core == 0, gram[1], gram[0])
+    keep = jnp.where(core == 0, gram[0], gram[1])
+
+    gathered = lax.all_gather(jnp.concatenate(rounded, axis=0), "mat", axis=1, tiled=True)
+    inverse = sum_and_factor(send, keep)
 
     ranks = [(x + off) % RING * 2 + core for off in OFFS]
     ranks += [(x + off) % RING * 2 + 1 - core for off in OFFS]
     ranks = jnp.stack(ranks).astype(jnp.int32)
-    chunks, nexts, backs, befores, afters = [], [], [], [], []
-    for p, (ring, cross) in enumerate(pairs):
-        chunks.append(jnp.stack([rounded[p]] + from_others(rounded[p], cross), axis=1))
-    for p, (ring, _) in enumerate(pairs):
-        befores.append(shift(chunks[p], ring, 1))
-        afters.append(shift(chunks[p], ring, -1))
-    for p, (ring, _) in enumerate(pairs):
-        nexts.append(shift(befores[p][0:1], ring, 1))
-        backs.append(shift(afters[p][1:2], ring, -1))
-    mine, theirs, basis = [], [], []
-    for p, (ring, _) in enumerate(pairs):
-        rows = [chunk_row(2 * p + i, ring, here[ring] + off) for i in range(2) for off in (0, 3, 1)]
-        part = project_three(grads, rows, (chunks[p], befores[p], afters[p]))
-        rows = [chunk_row(2 * p + i, ring, here[ring] + 2) for i in range(2)]
-        a, b = project_last(grads, rows, (nexts[p], backs[p]), part, inverse, p, ranks)
-        mine.append(a.reshape(2, RING, BLOCK, WIDTH))
-        theirs.append(shift(b, "core", 1).reshape(2, RING, BLOCK, WIDTH))
-        basis.append(make_basis(total[p], inverse, p, root))
-    both = jnp.concatenate(
-        [m + t.astype(F32) for m, t in zip(mine, theirs)], axis=0
-    )
+    basis = make_basis(jnp.concatenate(total, axis=0), inverse, root)
+    mine, theirs = project(gradients, gathered, inverse, ranks)
+    both = (mine + shift(theirs, "core", 1).astype(F32)).reshape(MATS, RING, BLOCK, WIDTH)
     out = both[:, 0]
     for j, step in ((1, 1), (2, -1), (3, 2)):
         out = out + shift(both[:, j].astype(BF16), "x", step).astype(F32)
-    return jnp.concatenate(basis, axis=0), out
+    return basis, out
 
 
 def solution(mesh):

time: 220 us -> 190 us (0.86)
  Pallas kernels: 74.5 us -> 52.6 us
  starting transfers between devices: 68.7 us -> 52.8 us
  between operations: 1.25 us -> 14.5 us
  local copies, waits for them, and re-layouts: 8.99 us -> 3.39 us
    ppermute x34 -> x20, starting transfers between devices: 57.9 us -> 35.2 us  [shift(): return lax.ppermute(value, 'mat', pairs)]
    pallas_call x8 -> x2, Pallas kernels: 24 us -> 10.6 us  [sketch_chunks(): pl.pallas_call(sketch_kernel, grid_spec=pltpu.PrefetchScalarGridSpec(num_...]
    all_gather x0 -> x1, waiting for transfers between devices: none -> 8.72 us  [local(): lax.all_gather(jnp.concatenate(rounded, axis=0), 'mat', axis=1, tiled=True)]
    ppermute x13 -> x12, starting transfers between devices: 10.8 us -> 17.6 us  [shift(): return lax.ppermute(value, 'row', pairs)]
    pallas_call x6 -> x4, Pallas kernels: 26.9 us -> 20.1 us  [the longest x1 11.1 us: project(): pl.pallas_call(project_kernel, grid_spec=pltpu.PrefetchScalarGridSpec(num...]
    ppermute x13 -> x12, waiting for transfers between devices: 23.4 us -> 16.6 us  [shift(): return lax.ppermute(value, 'row', pairs)]
    slice x4 -> x0, local copies, waits for them, and re-layouts: 3.37 us -> none  [the longest x2 1.7 us: local(): backs.append(shift(afters[p][1:2], ring, -1))]
    unnamed x46 -> x10, local copies, waits for them, and re-layouts: 4.11 us -> 1.88 us
  transfers between devices with their start and end apart: 47 -> 33, of which waited for: 22 -> 27; matrix products, arithmetic and copies ran while one was open for 3% -> 2% of each run, Pallas kernels for 32% -> 16%
where the time goes in v2:
time: 190 us
  waiting for transfers between devices  62.4 us (33%)
  starting transfers between devices  52.8 us (28%)
  Pallas kernels  52.6 us (28%)
  between operations  14.5 us (8%)
  other arithmetic  4.35 us (2%)
  local copies, waits for them, and re-layouts  3.39 us (2%)
    ppermute x20, waiting for transfers between devices, shift(): return lax.ppermute(value, 'mat', pairs)  37 us
    ppermute x20, starting transfers between devices, shift(): return lax.ppermute(value, 'mat', pairs)  35.2 us
    ppermute x12, starting transfers between devices, shift(): return lax.ppermute(value, 'row', pairs)  17.6 us
    ppermute x12, waiting for transfers between devices, shift(): return lax.ppermute(value, 'row', pairs)  16.6 us
    pallas_call x1, Pallas kernels, inverse_factors(): pl.pallas_call(inverse_kernel, grid_spec=pltpu.PrefetchScalarGridSpec(num...  12.1 us
    pallas_call x1, Pallas kernels, project(): pl.pallas_call(project_kernel, grid_spec=pltpu.PrefetchScalarGridSpec(num...  11.1 us
    pallas_call x2, Pallas kernels, sketch_chunks(): pl.pallas_call(sketch_kernel, grid_spec=pltpu.PrefetchScalarGridSpec(num_...  10.6 us
    all_gather x1, waiting for transfers between devices, local(): lax.all_gather(jnp.concatenate(rounded, axis=0), 'mat', axis=1, tiled=True)  8.72 us
  transfers between devices with their start and end apart: 33, of which 27 were waited for; matrix products, arithmetic and copies ran while one was open for 2% of the time, Pallas kernels for 16%

profile of v2, /device:TPU:0, one launch (start us, length us, event | category | flops | bytes accessed | tf_op | source)
XLA Modules:
  0.0 190.0 jit_solution(6429607555548692962)
XLA Ops:
  8.7 5.3 %shard_map.41 = (bf16[2,896,256]{2,1,0:T(8,128)(2,1)S(1)}, bf16[2,896,256]{2,1,0:T(8,128)(2,1)}) custom-call(s32[4,5]{1,0:T(4,128)S(1)} %pad_add_fusion.tab, bf16[4,16,224,512]{3,2,1,0:T(8,128)(2,1)} %bitcast.75, bf16[4,16,224,512]{3,2,1,0:T(8,128)(2,1)} %bitcast.76, bf16[4,16,224,512]{3,2,1,0:T(8,128)(2,1)} %bitcast.77, bf16[4,16,224,512]{3,2,1,0:T(8,128)(2,1)} %bitcast.78, ...), custom_call_target="tpu_custom_call" | custom-call | flops 939524096 | bytes 7340032 | tf_op jit(solution)/shard_map/pallas_call | solution.py:87
  17.9 5.3 %shard_map.43 = (bf16[2,896,256]{2,1,0:T(8,128)(2,1)S(1)}, bf16[2,896,256]{2,1,0:T(8,128)(2,1)}) custom-call(s32[4,5]{1,0:T(4,128)S(1)} %pad_add_fusion.1.tab, bf16[4,16,224,512]{3,2,1,0:T(8,128)(2,1)} %bitcast.79, bf16[4,16,224,512]{3,2,1,0:T(8,128)(2,1)} %bitcast.80, bf16[4,16,224,512]{3,2,1,0:T(8,128)(2,1)} %bitcast.81, ...), custom_call_target="tpu_custom_call" | custom-call | flops 939524096 | bytes 7340032 | tf_op jit(solution)/shard_map/pallas_call | solution.py:87
  24.9 2.1 %collective-permute-start.5 = (bf16[2,896,256]{2,1,0:T(8,128)(2,1)}, bf16[2,896,256]{2,1,0:T(8,128)(2,1)}, u32[]{:S(2)}, u32[]{:S(2)}) collective-permute-start(bf16[2,896,256]{2,1,0:T(8,128)(2,1)} %get-tuple-element.35), channel_id=1, source_target_pairs={{0,12},{1,13},{2,14},{3,15},{4,0},{5,1},{6,2},{7,3},{8,4},{9,5},{1... | collective-permute-start | bytes 2752520 | tf_op jit(solution)/shard_map/ppermute | solution.py:35
  27.3 10.1 %collective-permute-done.recv0.near1 = bf16[2,896,256]{2,1,0:T(8,128)(2,1)S(1)} collective-permute-done((bf16[2,896,256]{2,1,0:T(8,128)(2,1)S(1)}, bf16[2,896,256]{2,1,0:T(8,128)(2,1)S(1)}, u32[]{:S(2)}, u32[]{:S(2)}) %collective-permute-start) | collective-permute-done | bytes 917536 | tf_op jit(solution)/shard_map/ppermute | solution.py:35
  40.0 3.2 %shard_map.42 = (bf16[1,896,256]{2,1,0:T(8,128)(2,1)S(1)}, bf16[1,896,256]{2,1,0:T(8,128)(2,1)S(1)}) custom-call(s32[2,5]{1,0:T(2,128)S(1)} %pad_add_fusion.3.tab, bf16[4,16,224,512]{3,2,1,0:T(8,128)(2,1)} %bitcast.83, bf16[4,16,224,512]{3,2,1,0:T(8,128)(2,1)} %bitcast.84, bf16[4,16,224,512]{3,2,1,0:T(8,128)(2,1)} %bitcast.85, ...), custom_call_target="tpu_custom_call" | custom-call | flops 469762048 | bytes 3670016 | tf_op jit(solution)/shard_map/pallas_call | solution.py:115
  46.7 3.2 %shard_map.44 = (bf16[1,896,256]{2,1,0:T(8,128)(2,1)S(1)}, bf16[1,896,256]{2,1,0:T(8,128)(2,1)S(1)}) custom-call(s32[2,5]{1,0:T(2,128)S(1)} %pad_add_fusion.4.tab, bf16[4,16,224,512]{3,2,1,0:T(8,128)(2,1)} %bitcast.87, bf16[4,16,224,512]{3,2,1,0:T(8,128)(2,1)} %bitcast.88, bf16[4,16,224,512]{3,2,1,0:T(8,128)(2,1)} %bitcast.89, ...), custom_call_target="tpu_custom_call" | custom-call | flops 469762048 | bytes 3670016 | tf_op jit(solution)/shard_map/pallas_call | solution.py:115
  51.7 3.4 %collective-permute-start.7 = (bf16[1,896,256]{2,1,0:T(8,128)(2,1)S(1)}, bf16[1,896,256]{2,1,0:T(8,128)(2,1)}, u32[]{:S(2)}, u32[]{:S(2)}) collective-permute-start(bf16[1,896,256]{2,1,0:T(8,128)(2,1)S(1)} %get-tuple-element.37), channel_id=1, source_target_pairs={{0,12},{1,13},{2,14},{3,15},{4,0},{5,1},{6,2},{7,3},{8,4},{9,5},{1... | collective-permute-start | bytes 1376264 | tf_op jit(solution)/shard_map/ppermute | solution.py:35
  57.2 3.5 %collective-permute-done.6.comb1 = bf16[1,896,256]{2,1,0:T(8,128)(2,1)S(1)} collective-permute-done((bf16[1,896,256]{2,1,0:T(8,128)(2,1)S(1)}, bf16[1,896,256]{2,1,0:T(8,128)(2,1)S(1)}, u32[]{:S(2)}, u32[]{:S(2)}) %collective-permute-start.6) | collective-permute-done | bytes 458784 | tf_op jit(solution)/shard_map/ppermute | solution.py:35
  60.7 2.5 %collective-permute-done.7.comb1 = bf16[1,896,256]{2,1,0:T(8,128)(2,1)} collective-permute-done((bf16[1,896,256]{2,1,0:T(8,128)(2,1)S(1)}, bf16[1,896,256]{2,1,0:T(8,128)(2,1)}, u32[]{:S(2)}, u32[]{:S(2)}) %collective-permute-start.7) | collective-permute-done | bytes 458784 | tf_op jit(solution)/shard_map/ppermute | solution.py:35
  63.1 3.3 %shard_map.47 = (f32[2,224,256]{2,1,0:T(8,128)S(1)}, bf16[2,224,256]{2,1,0:T(8,128)(2,1)S(1)}, bf16[2,224,256]{2,1,0:T(8,128)(2,1)S(1)}, bf16[2,224,256]{2,1,0:T(8,128)(2,1)S(1)}) custom-call(s32[2,5]{1,0:T(2,128)S(1)} %pad_add_fusion.5.tab, bf16[4,16,224,512]{3,2,1,0:T(8,128)(2,1)} %bitcast.91, bf16[4,16,224,512]{3,2,1,0:T(8,128)(2,1)} %bitcast.92, ...), custom_call_target="tpu_custom_call" | custom-call | flops 469762048 | bytes 3670016 | tf_op jit(solution)/shard_map/pallas_call | solution.py:143
  67.1 2.9 %collective-permute-start.12 = (bf16[2,224,256]{2,1,0:T(8,128)(2,1)S(1)}, bf16[2,224,256]{2,1,0:T(8,128)(2,1)S(1)}, u32[]{:S(2)}, u32[]{:S(2)}) collective-permute-start(bf16[2,224,256]{2,1,0:T(8,128)(2,1)S(1)} %get-tuple-element.49), channel_id=1, source_target_pairs={{0,3},{1,0},{2,1},{3,2},{4,7},{5,4},{6,5},{7,6},{8,11},{9,8},{10,9... | collective-permute-start | bytes 688136 | tf_op jit(solution)/shard_map/ppermute | solution.py:35
  70.0 3.3 %shard_map.45 = (f32[2,224,256]{2,1,0:T(8,128)S(1)}, bf16[2,224,256]{2,1,0:T(8,128)(2,1)S(1)}, bf16[2,224,256]{2,1,0:T(8,128)(2,1)S(1)}, bf16[2,224,256]{2,1,0:T(8,128)(2,1)S(1)}) custom-call(s32[2,5]{1,0:T(2,128)S(1)} %pad_add_fusion.2.tab, bf16[4,16,224,512]{3,2,1,0:T(8,128)(2,1)} %bitcast.95, bf16[4,16,224,512]{3,2,1,0:T(8,128)(2,1)} %bitcast.96, ...), custom_call_target="tpu_custom_call" | custom-call | flops 469762048 | bytes 3670016 | tf_op jit(solution)/shard_map/pallas_call | solution.py:143
  74.0 3.2 %collective-permute-start.9 = (bf16[2,224,256]{2,1,0:T(8,128)(2,1)S(1)}, bf16[2,224,256]{2,1,0:T(8,128)(2,1)S(1)}, u32[]{:S(2)}, u32[]{:S(2)}) collective-permute-start(bf16[2,224,256]{2,1,0:T(8,128)(2,1)S(1)} %get-tuple-element.42), channel_id=1, source_target_pairs={{0,12},{1,13},{2,14},{3,15},{4,0},{5,1},{6,2},{7,3},{8,4},{9,5},{1... | collective-permute-start | bytes 688136 | tf_op jit(solution)/shard_map/ppermute | solution.py:35
  78.3 2.0 %collective-permute-start.10 = (bf16[2,224,256]{2,1,0:T(8,128)(2,1)S(1)}, bf16[2,224,256]{2,1,0:T(8,128)(2,1)S(1)}, u32[]{:S(2)}, u32[]{:S(2)}) collective-permute-start(bf16[2,224,256]{2,1,0:T(8,128)(2,1)S(1)} %get-tuple-element.43), channel_id=1, source_target_pairs={{0,8},{1,9},{2,10},{3,11},{4,12},{5,13},{6,14},{7,15},{8,0},{9,1},... | collective-permute-start | bytes 688136 | tf_op jit(solution)/shard_map/ppermute | solution.py:35
  83.1 2.7 %collective-permute-done.10.c = bf16[2,224,256]{2,1,0:T(8,128)(2,1)S(1)} collective-permute-done((bf16[2,224,256]{2,1,0:T(8,128)(2,1)S(1)}, bf16[2,224,256]{2,1,0:T(8,128)(2,1)S(1)}, u32[]{:S(2)}, u32[]{:S(2)}) %collective-permute-start.10) | collective-permute-done | bytes 229408 | tf_op jit(solution)/shard_map/ppermute | solution.py:35
  92.6 3.3 %collective-permute-start.17 = (f32[128,256]{1,0:T(8,128)S(1)}, f32[128,256]{1,0:T(8,128)S(1)}, u32[]{:S(2)}, u32[]{:S(2)}) collective-permute-start(f32[128,256]{1,0:T(8,128)S(1)} %get-tuple-element.62), channel_id=1, source_target_pairs={{0,64},{16,80},{32,96},{48,112},{64,0},{80,16},{96,32},{112,48},{1... | collective-permute-start | bytes 393224 | tf_op jit(solution)/shard_map/ppermute | solution.py:40
  97.9 2.8 %collective-permute-done.17 = f32[128,256]{1,0:T(8,128)S(1)} collective-permute-done((f32[128,256]{1,0:T(8,128)S(1)}, f32[128,256]{1,0:T(8,128)S(1)}, u32[]{:S(2)}, u32[]{:S(2)}) %collective-permute-start.17) | collective-permute-done | bytes 131104 | tf_op jit(solution)/shard_map/ppermute | solution.py:40
  100.7 2.1 %collective-permute-done.16 = f32[128,256]{1,0:T(8,128)S(1)} collective-permute-done((f32[128,256]{1,0:T(8,128)S(1)}, f32[128,256]{1,0:T(8,128)S(1)}, u32[]{:S(2)}, u32[]{:S(2)}) %collective-permute-start.16) | collective-permute-done | bytes 131104 | tf_op jit(solution)/shard_map/ppermute | solution.py:40
  103.4 3.1 %collective-permute-start.20 = (f32[128,256]{1,0:T(8,128)S(1)}, f32[128,256]{1,0:T(8,128)S(1)}, u32[]{:S(2)}, u32[]{:S(2)}) collective-permute-start(f32[128,256]{1,0:T(8,128)S(1)} %fusion.4), channel_id=1, source_target_pairs={{0,2},{1,3},{2,0},{3,1},{4,6},{5,7},{6,4},{7,5},{8,10},{9,11},{10,... | collective-permute-start | bytes 393224 | tf_op jit(solution)/shard_map/ppermute | solution.py:35
  106.5 3.2 %collective-permute-start.18 = (f32[128,256]{1,0:T(8,128)S(1)}, f32[128,256]{1,0:T(8,128)S(1)}, u32[]{:S(2)}, u32[]{:S(2)}) collective-permute-start(f32[128,256]{1,0:T(8,128)S(1)} %fusion.4), channel_id=1, source_target_pairs={{0,3},{1,0},{2,1},{3,2},{4,7},{5,4},{6,5},{7,6},{8,11},{9,8},{10,9... | collective-permute-start | bytes 393224 | tf_op jit(solution)/shard_map/ppermute | solution.py:35
  109.7 4.1 %collective-permute-done.20 = f32[128,256]{1,0:T(8,128)S(1)} collective-permute-done((f32[128,256]{1,0:T(8,128)S(1)}, f32[128,256]{1,0:T(8,128)S(1)}, u32[]{:S(2)}, u32[]{:S(2)}) %collective-permute-start.20) | collective-permute-done | bytes 131104 | tf_op jit(solution)/shard_map/ppermute | solution.py:35
  113.9 2.5 %collective-permute-done.19 = f32[128,256]{1,0:T(8,128)S(1)} collective-permute-done((f32[128,256]{1,0:T(8,128)S(1)}, f32[128,256]{1,0:T(8,128)S(1)}, u32[]{:S(2)}, u32[]{:S(2)}) %collective-permute-start.19) | collective-permute-done | bytes 131104 | tf_op jit(solution)/shard_map/ppermute | solution.py:35
  121.7 2.6 %collective-permute-done.23 = f32[128,256]{1,0:T(8,128)S(1)} collective-permute-done((f32[128,256]{1,0:T(8,128)S(1)}, f32[128,256]{1,0:T(8,128)S(1)}, u32[]{:S(2)}, u32[]{:S(2)}) %collective-permute-start.23) | collective-permute-done | bytes 131104 | tf_op jit(solution)/shard_map/ppermute | solution.py:35
  125.7 3.7 %collective-permute-start.26 = (f32[128,256]{1,0:T(8,128)S(1)}, f32[128,256]{1,0:T(8,128)S(1)}, u32[]{:S(2)}, u32[]{:S(2)}) collective-permute-start(f32[128,256]{1,0:T(8,128)S(1)} %add_add_fusion), channel_id=1, source_target_pairs={{0,64},{16,80},{32,96},{48,112},{64,0},{80,16},{96,32},{112,48},{1... | collective-permute-start | bytes 393224 | tf_op jit(solution)/shard_map/ppermute | solution.py:40
  129.9 2.7 %collective-permute-start.24 = (f32[128,256]{1,0:T(8,128)S(1)}, f32[128,256]{1,0:T(8,128)S(1)}, u32[]{:S(2)}, u32[]{:S(2)}) collective-permute-start(f32[128,256]{1,0:T(8,128)S(1)} %add_add_fusion), channel_id=1, source_target_pairs={{0,96},{16,112},{32,0},{48,16},{64,32},{80,48},{96,64},{112,80},{1... | collective-permute-start | bytes 393224 | tf_op jit(solution)/shard_map/ppermute | solution.py:40
  133.4 2.2 %collective-permute-done.25 = f32[128,256]{1,0:T(8,128)S(1)} collective-permute-done((f32[128,256]{1,0:T(8,128)S(1)}, f32[128,256]{1,0:T(8,128)S(1)}, u32[]{:S(2)}, u32[]{:S(2)}) %collective-permute-start.25) | collective-permute-done | bytes 131104 | tf_op jit(solution)/shard_map/ppermute | solution.py:40
  137.6 12.1 %shard_map.49.inv = f32[4,256,256]{2,1,0:T(8,128)} custom-call(s32[2]{0:T(128)S(1)} %pad_add_fusion.6.where, f32[4,128,256]{2,1,0:T(8,128)S(1)} %pad_maximum_fusion.1.own, f32[4,128,256]{2,1,0:T(8,128)S(1)} %collective-permute-done.27.other), custom_call_target="tpu_custom_call" | custom-call | flops 12000000000 | bytes 4194304 | tf_op jit(solution)/shard_map/pallas_call | solution.py:332
  149.7 8.7 %all-gather.2.cloned.1.call-done.s = bf16[4,3584,256]{2,1,0:T(8,128)(2,1)} async-done(((bf16[4,224,256]{2,1,0:T(8,128)(2,1)}), bf16[4,3584,256]{2,1,0:T(8,128)(2,1)}) %all-gather.2.cloned.1.call-update) | async-done | bytes 7340048 | tf_op jit(solution)/shard_map/all_gather | solution.py:411
  158.5 11.1 %shard_map.51 = (f32[4,128,512]{2,1,0:T(8,128)S(1)}, bf16[4,128,512]{2,1,0:T(8,128)(2,1)S(1)}) custom-call(s32[8]{0:T(128)S(1)} %stack.331.ranks, bf16[4,3584,256]{2,1,0:T(8,128)(2,1)} %all-gather.2.cloned.1.call-done.s, bf16[4,3584,512]{2,1,0:T(8,128)(2,1)} %g.1, f32[4,256,256]{2,1,0:T(8,128)} %shard_map.49.inv), custom_call_target="tpu_custom_call" | custom-call | flops 5368709120 | bytes 22020096 | tf_op jit(solution)/shard_map/pallas_call | solution.py:202
  171.8 3.1 %collective-permute-start.31 = (bf16[4,32,512]{2,1,0:T(8,128)(2,1)S(1)}, bf16[4,32,512]{2,1,0:T(8,128)(2,1)S(1)}, u32[]{:S(2)}, u32[]{:S(2)}) collective-permute-start(bf16[4,32,512]{2,1,0:T(8,128)(2,1)S(1)} %get-tuple-element.59), channel_id=1, source_target_pairs={{0,64},{16,80},{32,96},{48,112},{64,0},{80,16},{96,32},{112,48},{1... | collective-permute-start | bytes 393224 | tf_op jit(solution)/shard_map/ppermute | solution.py:40
  177.0 2.6 %shard_map.50 = bf16[4,224,256]{2,1,0:T(8,128)(2,1)} custom-call(f32[4,224,256]{2,1,0:T(8,128)S(1)} %pad_maximum_fusion.s, f32[4,256,256]{2,1,0:T(8,128)S(1)} %copy-done.2), custom_call_target="tpu_custom_call" | custom-call | flops 704643072 | bytes 2293760 | tf_op jit(solution)/shard_map/pallas_call | solution.py:233
  179.7 2.0 %collective-permute-done.30 = bf16[4,32,512]{2,1,0:T(8,128)(2,1)S(1)} collective-permute-done((bf16[4,32,512]{2,1,0:T(8,128)(2,1)S(1)}, bf16[4,32,512]{2,1,0:T(8,128)(2,1)S(1)}, u32[]{:S(2)}, u32[]{:S(2)}) %collective-permute-start.30) | collective-permute-done | bytes 131104 | tf_op jit(solution)/shard_map/ppermute | solution.py:40
  (92 shorter events, 47.6 us)
Async XLA Ops:
  7.2 151.3 %all-gather.2.cloned.1.call-start = ((), (), s32[]{:S(2)}) async-start(), calls=%async_computation | async-start | bytes 7798784 | tf_op jit(solution)/shard_map/all_gather | solution.py:411
  14.0 23.4 %collective-permute-start = (bf16[2,896,256]{2,1,0:T(8,128)(2,1)S(1)}, bf16[2,896,256]{2,1,0:T(8,128)(2,1)S(1)}, u32[]{:S(2)}, u32[]{:S(2)}) collective-permute-start(bf16[2,896,256]{2,1,0:T(8,128)(2,1)S(1)} %get-tuple-element.30), channel_id=1, source_target_pairs={{0,1},{1,2},{2,3},{3,0},{4,5},{5,6},{6,7},{7,4},{8,9},{9,10},{10,1... | collective-permute-start | bytes 2752520 | tf_op jit(solution)/shard_map/ppermute | solution.py:35
  15.6 24.4 %collective-permute-start.1 = (bf16[2,896,256]{2,1,0:T(8,128)(2,1)}, bf16[2,896,256]{2,1,0:T(8,128)(2,1)}, u32[]{:S(2)}, u32[]{:S(2)}) collective-permute-start(bf16[2,896,256]{2,1,0:T(8,128)(2,1)} %get-tuple-element.31), channel_id=1, source_target_pairs={{0,4},{1,5},{2,6},{3,7},{4,8},{5,9},{6,10},{7,11},{8,12},{9,13},{1... | collective-permute-start | bytes 2752520 | tf_op jit(solution)/shard_map/ppermute | solution.py:35
  23.2 21.7 %collective-permute-start.4 = (bf16[2,896,256]{2,1,0:T(8,128)(2,1)S(1)}, bf16[2,896,256]{2,1,0:T(8,128)(2,1)}, u32[]{:S(2)}, u32[]{:S(2)}) collective-permute-start(bf16[2,896,256]{2,1,0:T(8,128)(2,1)S(1)} %get-tuple-element.34), channel_id=1, source_target_pairs={{0,3},{1,0},{2,1},{3,2},{4,7},{5,4},{6,5},{7,6},{8,11},{9,8},{10,9... | collective-permute-start | bytes 2752520 | tf_op jit(solution)/shard_map/ppermute | solution.py:35
  24.9 21.8 %collective-permute-start.5 = (bf16[2,896,256]{2,1,0:T(8,128)(2,1)}, bf16[2,896,256]{2,1,0:T(8,128)(2,1)}, u32[]{:S(2)}, u32[]{:S(2)}) collective-permute-start(bf16[2,896,256]{2,1,0:T(8,128)(2,1)} %get-tuple-element.35), channel_id=1, source_target_pairs={{0,12},{1,13},{2,14},{3,15},{4,0},{5,1},{6,2},{7,3},{8,4},{9,5},{1... | collective-permute-start | bytes 2752520 | tf_op jit(solution)/shard_map/ppermute | solution.py:35
  43.2 12.7 %collective-permute-start.2 = (bf16[1,896,256]{2,1,0:T(8,128)(2,1)S(1)}, bf16[1,896,256]{2,1,0:T(8,128)(2,1)S(1)}, u32[]{:S(2)}, u32[]{:S(2)}) collective-permute-start(bf16[1,896,256]{2,1,0:T(8,128)(2,1)S(1)} %get-tuple-element.32), channel_id=1, source_target_pairs={{0,1},{1,2},{2,3},{3,0},{4,5},{5,6},{6,7},{7,4},{8,9},{9,10},{10,1... | collective-permute-start | bytes 1376264 | tf_op jit(solution)/shard_map/ppermute | solution.py:35
  44.9 12.3 %collective-permute-start.3 = (bf16[1,896,256]{2,1,0:T(8,128)(2,1)S(1)}, bf16[1,896,256]{2,1,0:T(8,128)(2,1)S(1)}, u32[]{:S(2)}, u32[]{:S(2)}) collective-permute-start(bf16[1,896,256]{2,1,0:T(8,128)(2,1)S(1)} %get-tuple-element.33), channel_id=1, source_target_pairs={{0,4},{1,5},{2,6},{3,7},{4,8},{5,9},{6,10},{7,11},{8,12},{9,13},{1... | collective-permute-start | bytes 1376264 | tf_op jit(solution)/shard_map/ppermute | solution.py:35
  49.9 10.8 %collective-permute-start.6 = (bf16[1,896,256]{2,1,0:T(8,128)(2,1)S(1)}, bf16[1,896,256]{2,1,0:T(8,128)(2,1)S(1)}, u32[]{:S(2)}, u32[]{:S(2)}) collective-permute-start(bf16[1,896,256]{2,1,0:T(8,128)(2,1)S(1)} %get-tuple-element.36), channel_id=1, source_target_pairs={{0,3},{1,0},{2,1},{3,2},{4,7},{5,4},{6,5},{7,6},{8,11},{9,8},{10,9... | collective-permute-start | bytes 1376264 | tf_op jit(solution)/shard_map/ppermute | solution.py:35
  51.7 11.4 %collective-permute-start.7 = (bf16[1,896,256]{2,1,0:T(8,128)(2,1)S(1)}, bf16[1,896,256]{2,1,0:T(8,128)(2,1)}, u32[]{:S(2)}, u32[]{:S(2)}) collective-permute-start(bf16[1,896,256]{2,1,0:T(8,128)(2,1)S(1)} %get-tuple-element.37), channel_id=1, source_target_pairs={{0,12},{1,13},{2,14},{3,15},{4,0},{5,1},{6,2},{7,3},{8,4},{9,5},{1... | collective-permute-start | bytes 1376264 | tf_op jit(solution)/shard_map/ppermute | solution.py:35
  66.4 11.9 %collective-permute-start.11 = (bf16[2,224,256]{2,1,0:T(8,128)(2,1)S(1)}, bf16[2,224,256]{2,1,0:T(8,128)(2,1)S(1)}, u32[]{:S(2)}, u32[]{:S(2)}) collective-permute-start(bf16[2,224,256]{2,1,0:T(8,128)(2,1)S(1)} %get-tuple-element.48), channel_id=1, source_target_pairs={{0,1},{1,2},{2,3},{3,0},{4,5},{5,6},{6,7},{7,4},{8,9},{9,10},{10,1... | collective-permute-start | bytes 688136 | tf_op jit(solution)/shard_map/ppermute | solution.py:35
  67.1 13.3 %collective-permute-start.12 = (bf16[2,224,256]{2,1,0:T(8,128)(2,1)S(1)}, bf16[2,224,256]{2,1,0:T(8,128)(2,1)S(1)}, u32[]{:S(2)}, u32[]{:S(2)}) collective-permute-start(bf16[2,224,256]{2,1,0:T(8,128)(2,1)S(1)} %get-tuple-element.49), channel_id=1, source_target_pairs={{0,3},{1,0},{2,1},{3,2},{4,7},{5,4},{6,5},{7,6},{8,11},{9,8},{10,9... | collective-permute-start | bytes 688136 | tf_op jit(solution)/shard_map/ppermute | solution.py:35
  70.0 10.4 %collective-permute-start.13 = (bf16[2,224,256]{2,1,0:T(8,128)(2,1)S(1)}, bf16[2,224,256]{2,1,0:T(8,128)(2,1)S(1)}, u32[]{:S(2)}, u32[]{:S(2)}) collective-permute-start(bf16[2,224,256]{2,1,0:T(8,128)(2,1)S(1)} %get-tuple-element.50), channel_id=1, source_target_pairs={{0,2},{1,3},{2,0},{3,1},{4,6},{5,7},{6,4},{7,5},{8,10},{9,11},{10,... | collective-permute-start | bytes 688136 | tf_op jit(solution)/shard_map/ppermute | solution.py:35
  73.3 9.9 %collective-permute-start.8 = (bf16[2,224,256]{2,1,0:T(8,128)(2,1)S(1)}, bf16[2,224,256]{2,1,0:T(8,128)(2,1)S(1)}, u32[]{:S(2)}, u32[]{:S(2)}) collective-permute-start(bf16[2,224,256]{2,1,0:T(8,128)(2,1)S(1)} %get-tuple-element.41), channel_id=1, source_target_pairs={{0,4},{1,5},{2,6},{3,7},{4,8},{5,9},{6,10},{7,11},{8,12},{9,13},{1... | collective-permute-start | bytes 688136 | tf_op jit(solution)/shard_map/ppermute | solution.py:35
  74.0 9.2 %collective-permute-start.9 = (bf16[2,224,256]{2,1,0:T(8,128)(2,1)S(1)}, bf16[2,224,256]{2,1,0:T(8,128)(2,1)S(1)}, u32[]{:S(2)}, u32[]{:S(2)}) collective-permute-start(bf16[2,224,256]{2,1,0:T(8,128)(2,1)S(1)} %get-tuple-element.42), channel_id=1, source_target_pairs={{0,12},{1,13},{2,14},{3,15},{4,0},{5,1},{6,2},{7,3},{8,4},{9,5},{1... | collective-permute-start | bytes 688136 | tf_op jit(solution)/shard_map/ppermute | solution.py:35
  78.3 7.5 %collective-permute-start.10 = (bf16[2,224,256]{2,1,0:T(8,128)(2,1)S(1)}, bf16[2,224,256]{2,1,0:T(8,128)(2,1)S(1)}, u32[]{:S(2)}, u32[]{:S(2)}) collective-permute-start(bf16[2,224,256]{2,1,0:T(8,128)(2,1)S(1)} %get-tuple-element.43), channel_id=1, source_target_pairs={{0,8},{1,9},{2,10},{3,11},{4,12},{5,13},{6,14},{7,15},{8,0},{9,1},... | collective-permute-start | bytes 688136 | tf_op jit(solution)/shard_map/ppermute | solution.py:35
  89.4 2.0 %collective-permute-start.14 = (f32[2,256,256]{2,1,0:T(8,128)S(1)}, f32[2,256,256]{2,1,0:T(8,128)S(1)}, u32[]{:S(2)}, u32[]{:S(2)}) collective-permute-start(f32[2,256,256]{2,1,0:T(8,128)S(1)} %broadcast_select_fusion), channel_id=1, source_target_pairs={{0,16},{16,0},{32,48},{48,32},{64,80},{80,64},{96,112},{112,96},{1... | collective-permute-start | bytes 1572872 | tf_op jit(solution)/shard_map/ppermute | solution.py:40
  92.6 8.1 %collective-permute-start.17 = (f32[128,256]{1,0:T(8,128)S(1)}, f32[128,256]{1,0:T(8,128)S(1)}, u32[]{:S(2)}, u32[]{:S(2)}) collective-permute-start(f32[128,256]{1,0:T(8,128)S(1)} %get-tuple-element.62), channel_id=1, source_target_pairs={{0,64},{16,80},{32,96},{48,112},{64,0},{80,16},{96,32},{112,48},{1... | collective-permute-start | bytes 393224 | tf_op jit(solution)/shard_map/ppermute | solution.py:40
  95.9 6.9 %collective-permute-start.16 = (f32[128,256]{1,0:T(8,128)S(1)}, f32[128,256]{1,0:T(8,128)S(1)}, u32[]{:S(2)}, u32[]{:S(2)}) collective-permute-start(f32[128,256]{1,0:T(8,128)S(1)} %get-tuple-element.63), channel_id=1, source_target_pairs={{0,96},{16,112},{32,0},{48,16},{64,32},{80,48},{96,64},{112,80},{1... | collective-permute-start | bytes 393224 | tf_op jit(solution)/shard_map/ppermute | solution.py:40
  97.1 6.3 %collective-permute-start.15 = (f32[128,256]{1,0:T(8,128)S(1)}, f32[128,256]{1,0:T(8,128)S(1)}, u32[]{:S(2)}, u32[]{:S(2)}) collective-permute-start(f32[128,256]{1,0:T(8,128)S(1)} %get-tuple-element.61), channel_id=1, source_target_pairs={{0,32},{16,48},{32,64},{48,80},{64,96},{80,112},{96,0},{112,16},{1... | collective-permute-start | bytes 393224 | tf_op jit(solution)/shard_map/ppermute | solution.py:40
  103.4 10.5 %collective-permute-start.20 = (f32[128,256]{1,0:T(8,128)S(1)}, f32[128,256]{1,0:T(8,128)S(1)}, u32[]{:S(2)}, u32[]{:S(2)}) collective-permute-start(f32[128,256]{1,0:T(8,128)S(1)} %fusion.4), channel_id=1, source_target_pairs={{0,2},{1,3},{2,0},{3,1},{4,6},{5,7},{6,4},{7,5},{8,10},{9,11},{10,... | collective-permute-start | bytes 393224 | tf_op jit(solution)/shard_map/ppermute | solution.py:35
  106.5 9.9 %collective-permute-start.19 = (f32[128,256]{1,0:T(8,128)S(1)}, f32[128,256]{1,0:T(8,128)S(1)}, u32[]{:S(2)}, u32[]{:S(2)}) collective-permute-start(f32[128,256]{1,0:T(8,128)S(1)} %fusion.4), channel_id=1, source_target_pairs={{0,1},{1,2},{2,3},{3,0},{4,5},{5,6},{6,7},{7,4},{8,9},{9,10},{10,1... | collective-permute-start | bytes 393224 | tf_op jit(solution)/shard_map/ppermute | solution.py:35
  106.5 9.9 %collective-permute-start.18 = (f32[128,256]{1,0:T(8,128)S(1)}, f32[128,256]{1,0:T(8,128)S(1)}, u32[]{:S(2)}, u32[]{:S(2)}) collective-permute-start(f32[128,256]{1,0:T(8,128)S(1)} %fusion.4), channel_id=1, source_target_pairs={{0,3},{1,0},{2,1},{3,2},{4,7},{5,4},{6,5},{7,6},{8,11},{9,8},{10,9... | collective-permute-start | bytes 393224 | tf_op jit(solution)/shard_map/ppermute | solution.py:35
  116.4 7.8 %collective-permute-start.23 = (f32[128,256]{1,0:T(8,128)S(1)}, f32[128,256]{1,0:T(8,128)S(1)}, u32[]{:S(2)}, u32[]{:S(2)}) collective-permute-start(f32[128,256]{1,0:T(8,128)S(1)} %add_add_fusion.1), channel_id=1, source_target_pairs={{0,8},{1,9},{2,10},{3,11},{4,12},{5,13},{6,14},{7,15},{8,0},{9,1},... | collective-permute-start | bytes 393224 | tf_op jit(solution)/shard_map/ppermute | solution.py:35
  118.4 6.8 %collective-permute-start.22 = (f32[128,256]{1,0:T(8,128)S(1)}, f32[128,256]{1,0:T(8,128)S(1)}, u32[]{:S(2)}, u32[]{:S(2)}) collective-permute-start(f32[128,256]{1,0:T(8,128)S(1)} %add_add_fusion.1), channel_id=1, source_target_pairs={{0,4},{1,5},{2,6},{3,7},{4,8},{5,9},{6,10},{7,11},{8,12},{9,13},{1... | collective-permute-start | bytes 393224 | tf_op jit(solution)/shard_map/ppermute | solution.py:35
  120.1 5.5 %collective-permute-start.21 = (f32[128,256]{1,0:T(8,128)S(1)}, f32[128,256]{1,0:T(8,128)S(1)}, u32[]{:S(2)}, u32[]{:S(2)}) collective-permute-start(f32[128,256]{1,0:T(8,128)S(1)} %add_add_fusion.1), channel_id=1, source_target_pairs={{0,12},{1,13},{2,14},{3,15},{4,0},{5,1},{6,2},{7,3},{8,4},{9,5},{1... | collective-permute-start | bytes 393224 | tf_op jit(solution)/shard_map/ppermute | solution.py:35
  125.7 7.7 %collective-permute-start.26 = (f32[128,256]{1,0:T(8,128)S(1)}, f32[128,256]{1,0:T(8,128)S(1)}, u32[]{:S(2)}, u32[]{:S(2)}) collective-permute-start(f32[128,256]{1,0:T(8,128)S(1)} %add_add_fusion), channel_id=1, source_target_pairs={{0,64},{16,80},{32,96},{48,112},{64,0},{80,16},{96,32},{112,48},{1... | collective-permute-start | bytes 393224 | tf_op jit(solution)/shard_map/ppermute | solution.py:40
  129.4 6.2 %collective-permute-start.25 = (f32[128,256]{1,0:T(8,128)S(1)}, f32[128,256]{1,0:T(8,128)S(1)}, u32[]{:S(2)}, u32[]{:S(2)}) collective-permute-start(f32[128,256]{1,0:T(8,128)S(1)} %add_add_fusion), channel_id=1, source_target_pairs={{0,32},{16,48},{32,64},{48,80},{64,96},{80,112},{96,0},{112,16},{1... | collective-permute-start | bytes 393224 | tf_op jit(solution)/shard_map/ppermute | solution.py:40
  129.9 5.6 %collective-permute-start.24 = (f32[128,256]{1,0:T(8,128)S(1)}, f32[128,256]{1,0:T(8,128)S(1)}, u32[]{:S(2)}, u32[]{:S(2)}) collective-permute-start(f32[128,256]{1,0:T(8,128)S(1)} %add_add_fusion), channel_id=1, source_target_pairs={{0,96},{16,112},{32,0},{48,16},{64,32},{80,48},{96,64},{112,80},{1... | collective-permute-start | bytes 393224 | tf_op jit(solution)/shard_map/ppermute | solution.py:40
  135.6 2.0 %collective-permute-start.27 = (f32[4,128,256]{2,1,0:T(8,128)S(1)}, f32[4,128,256]{2,1,0:T(8,128)S(1)}, u32[]{:S(2)}, u32[]{:S(2)}) collective-permute-start(f32[4,128,256]{2,1,0:T(8,128)S(1)} %pad_maximum_fusion.1.own), channel_id=1, source_target_pairs={{0,16},{16,0},{32,48},{48,32},{64,80},{80,64},{96,112},{112,96},{1... | collective-permute-start | bytes 1572872 | tf_op jit(solution)/shard_map/ppermute | solution.py:40
  171.8 7.9 %collective-permute-start.31 = (bf16[4,32,512]{2,1,0:T(8,128)(2,1)S(1)}, bf16[4,32,512]{2,1,0:T(8,128)(2,1)S(1)}, u32[]{:S(2)}, u32[]{:S(2)}) collective-permute-start(bf16[4,32,512]{2,1,0:T(8,128)(2,1)S(1)} %get-tuple-element.59), channel_id=1, source_target_pairs={{0,64},{16,80},{32,96},{48,112},{64,0},{80,16},{96,32},{112,48},{1... | collective-permute-start | bytes 393224 | tf_op jit(solution)/shard_map/ppermute | solution.py:40
  174.9 6.9 %collective-permute-start.30 = (bf16[4,32,512]{2,1,0:T(8,128)(2,1)S(1)}, bf16[4,32,512]{2,1,0:T(8,128)(2,1)S(1)}, u32[]{:S(2)}, u32[]{:S(2)}) collective-permute-start(bf16[4,32,512]{2,1,0:T(8,128)(2,1)S(1)} %get-tuple-element.60), channel_id=1, source_target_pairs={{0,96},{16,112},{32,0},{48,16},{64,32},{80,48},{96,64},{112,80},{1... | collective-permute-start | bytes 393224 | tf_op jit(solution)/shard_map/ppermute | solution.py:40
  176.0 6.3 %collective-permute-start.29 = (bf16[4,32,512]{2,1,0:T(8,128)(2,1)S(1)}, bf16[4,32,512]{2,1,0:T(8,128)(2,1)S(1)}, u32[]{:S(2)}, u32[]{:S(2)}) collective-permute-start(bf16[4,32,512]{2,1,0:T(8,128)(2,1)S(1)} %get-tuple-element.58), channel_id=1, source_target_pairs={{0,32},{16,48},{32,64},{48,80},{64,96},{80,112},{96,0},{112,16},{1... | collective-permute-start | bytes 393224 | tf_op jit(solution)/shard_map/ppermute | solution.py:40
  (6 other events, 46.1 us)
Sparse Core Ops, SparseCore 0:
  88.4 70.0 all-gather.1

commit v3 on v2

v3 whole, which is shorter than its diff:
```python
import functools

import jax
import jax.numpy as jnp
from jax import lax
from jax.experimental import pallas as pl
from jax.experimental.pallas import tpu as pltpu
from jax.sharding import PartitionSpec as P

MATS, RANK, SHARE, WIDTH, SHARES, RING = 4, 256, 224, 512, 16, 4
HALF = RANK // 2
BLOCK = RANK // 8
OFFS = (0, 1, 3, 2)
F32, BF16 = jnp.float32, jnp.bfloat16
EXACT = lax.Precision.HIGHEST
NEWTON_TOL = 3e-4
NEWTON_MAX = 10


def params():
    return pltpu.CompilerParams(vmem_limit_bytes=52 * 1024 * 1024)


def cost(flops, moved):
    return pl.CostEstimate(flops=int(flops), bytes_accessed=int(moved), transcendentals=0)


def shift(value, axis, step):
    pairs = []
    if axis in ("y", "z"):
        for z in range(RING):
            for y in range(RING):
                to = z * RING + (y + step) % RING if axis == "y" else (z + step) % RING * RING + y
                pairs.append((z * RING + y, to))
        return lax.ppermute(value, "mat", pairs)
    for x in range(RING):
        for core in range(2):
            to = (x + step) % RING * 2 + core if axis == "x" else x * 2 + (core + step) % 2
            pairs.append((x * 2 + core, to))
    return lax.ppermute(value, "row", pairs)


def place():
    row, mat = lax.axis_index("row"), lax.axis_index("mat")
    return row // 2, row % 2, mat % RING, mat // RING


def chunk_row(index, along, dest):
    _, _, y, z = place()
    if along == "y":
        return [index] + [(z + off) % RING * RING + dest % RING for off in OFFS]
    return [index] + [dest % RING * RING + (y + off) % RING for off in OFFS]


def gradient_specs(base, step=lambda *ids: ids[0]):
    return [
        pl.BlockSpec(
            (1, 1, SHARE, WIDTH),
            lambda *a, j=j: (a[-1][base + step(*a[:-1]), 0], a[-1][base + step(*a[:-1]), 1 + j], 0, 0),
        )
        for j in range(RING)
    ]


def sketch_of(grads, sk):
    rows = jnp.concatenate([g[0, 0] for g in grads], axis=0)
    return jnp.dot(rows, sk[...], preferred_element_type=F32)


CHUNK = RING * SHARE
CHUNK_FLOPS = 2 * CHUNK * WIDTH * RANK
CHUNK_BYTES = 2 * CHUNK * (WIDTH + 2 * RANK)
CHUNK_BLOCK = (1, CHUNK, RANK)


def sketch_kernel(tab, g0, g1, g2, g3, sk, *outs):
    def run(out):
        out[0] = sketch_of((g0, g1, g2, g3), sk).astype(BF16)

    for n, out in enumerate(outs):
        pl.when(pl.program_id(0) == n)(lambda out=out: run(out))


def sketch_chunks(grads, sketch, table, base):
    return pl.pallas_call(
        sketch_kernel,
        grid_spec=pltpu.PrefetchScalarGridSpec(
            num_scalar_prefetch=1,
            grid=(4,),
            in_specs=gradient_specs(base) + [pl.BlockSpec((WIDTH, RANK), lambda n, t: (0, 0))],
            out_specs=[pl.BlockSpec(CHUNK_BLOCK, lambda n, t: (0, 0, 0))] * 4,
        ),
        out_shape=[jax.ShapeDtypeStruct((1, CHUNK, RANK), BF16)] * 4,
        compiler_params=params(),
        cost_estimate=cost(4 * CHUNK_FLOPS, 4 * CHUNK_BYTES),
    )(table, grads, grads, grads, grads, sketch)


def combine_kernel(tab, g0, g1, g2, g3, sk, recv0, recv1, out0, out1):
    def run(recv, out):
        term = sketch_of((g0, g1, g2, g3), sk)
        out[0] = (term + recv[0].astype(F32)).astype(BF16)

    pl.when(pl.program_id(0) == 0)(lambda: run(recv0, out0))
    pl.when(pl.program_id(0) == 1)(lambda: run(recv1, out1))


def combined_chunks(grads, sketch, table, base, recvs):
    block = pl.BlockSpec(CHUNK_BLOCK, lambda n, t: (0, 0, 0))
    return pl.pallas_call(
        combine_kernel,
        grid_spec=pltpu.PrefetchScalarGridSpec(
            num_scalar_prefetch=1,
            grid=(2,),
            in_specs=gradient_specs(base)
            + [pl.BlockSpec((WIDTH, RANK), lambda n, t: (0, 0)), block, block],
            out_specs=[block, block],
        ),
        out_shape=[jax.ShapeDtypeStruct((1, CHUNK, RANK), BF16)] * 2,
        compiler_params=params(),
        cost_estimate=cost(2 * CHUNK_FLOPS, 2 * CHUNK_BYTES),
    )(table, grads, grads, grads, grads, sketch, *recvs)


def near_kernel(tab, g0, g1, g2, g3, sk, near0, near1, out):
    def run(near):
        out[0] = sketch_of((g0, g1, g2, g3), sk) + near[0].astype(F32)

    pl.when(pl.program_id(0) == 0)(lambda: run(near0))
    pl.when(pl.program_id(0) == 1)(lambda: run(near1))


def own_and_near(grads, sketch, table, base, nears):
    return pl.pallas_call(
        near_kernel,
        grid_spec=pltpu.PrefetchScalarGridSpec(
            num_scalar_prefetch=1,
            grid=(2,),
            in_specs=gradient_specs(base)
            + [pl.BlockSpec((WIDTH, RANK), lambda n, t: (0, 0))]
            + [pl.BlockSpec(CHUNK_BLOCK, lambda n, t: (0, 0, 0))] * 2,
            out_specs=pl.BlockSpec(CHUNK_BLOCK, lambda n, t: (n, 0, 0)),
        ),
        out_shape=jax.ShapeDtypeStruct((2, CHUNK, RANK), F32),
        compiler_params=params(),
        cost_estimate=cost(2 * CHUNK_FLOPS, 2 * CHUNK_BYTES),
    )(table, grads, grads, grads, grads, sketch, *nears)


def own_kernel(part, comb0, comb1, own, ahead, behind, across):
    def run(comb):
        for j, out in enumerate((own, ahead, behind, across)):
            rows = slice(j * SHARE, (j + 1) * SHARE)
            out[0] = (part[0, rows] + comb[0, rows].astype(F32)).astype(out.dtype)

    pl.when(pl.program_id(0) == 0)(lambda: run(comb0))
    pl.when(pl.program_id(0) == 1)(lambda: run(comb1))


def own_chunks(part, combs):
    share = pl.BlockSpec((1, SHARE, RANK), lambda n: (n, 0, 0))
    return pl.pallas_call(
        own_kernel,
        grid=(2,),
        in_specs=[pl.BlockSpec(CHUNK_BLOCK, lambda n: (n, 0, 0))]
        + [pl.BlockSpec(CHUNK_BLOCK, lambda n: (0, 0, 0))] * 2,
        out_specs=[share] * 4,
        out_shape=[jax.ShapeDtypeStruct((2, SHARE, RANK), F32)]
        + [jax.ShapeDtypeStruct((2, SHARE, RANK), BF16)] * 3,
        compiler_params=params(),
        cost_estimate=cost(2 * CHUNK * RANK, 16 * CHUNK * RANK),
    )(part, *combs)


def total_kernel(own, a, b, c, total, rounded):
    value = own[0] + a[0].astype(F32) + b[0].astype(F32) + c[0].astype(F32)
    total[0] = value
    rounded[0] = value.astype(BF16)


def totals(own, parts):
    share = pl.BlockSpec((1, SHARE, RANK), lambda n: (n, 0, 0))
    return pl.pallas_call(
        total_kernel,
        grid=(2,),
        in_specs=[share] * 4,
        out_specs=[share, share],
        out_shape=[
            jax.ShapeDtypeStruct((2, SHARE, RANK), F32),
            jax.ShapeDtypeStruct((2, SHARE, RANK), BF16),
        ],
        compiler_params=params(),
        cost_estimate=cost(2 * SHARE * RANK, 2 * SHARE * RANK * 16),
    )(own, *parts)


TRI = 3


def gram_kernel(s, out):
    left = jnp.transpose(s[0])
    out[0, 0] = jnp.dot(left[:HALF], s[0, :, :HALF], precision=EXACT, preferred_element_type=F32)
    low = jnp.dot(left[HALF:], s[0], precision=EXACT, preferred_element_type=F32)
    out[0, 1] = low[:, :HALF]
    out[0, 2] = low[:, HALF:]


def gram_parts(total):
    return pl.pallas_call(
        gram_kernel,
        grid=(MATS,),
        in_specs=[pl.BlockSpec((1, SHARE, RANK), lambda n: (n, 0, 0))],
        out_specs=pl.BlockSpec((1, TRI, HALF, HALF), lambda n: (n, 0, 0, 0)),
        out_shape=jax.ShapeDtypeStruct((MATS, TRI, HALF, HALF), F32),
        compiler_params=params(),
        cost_estimate=cost(MATS * 12 * SHARE * RANK * RANK, 16 * SHARE * RANK),
    )(total)


def finish(ranks, inv, whole, rows, mine, theirs):
    for b in range(8):
        start = pl.multiple_of(ranks[b] * BLOCK, BLOCK)
        rows[b * BLOCK : (b + 1) * BLOCK] = inv[0, pl.ds(start, BLOCK), :]
    out = jnp.dot(rows[...], whole, precision=EXACT, preferred_element_type=F32)
    mine[0] = out[:HALF]
    theirs[0] = out[HALF:].astype(BF16)


def project_kernel(ranks, s, g, inv, mine, theirs, rows):
    whole = lax.dot_general(s[0], g[0], (((0,), (0,)), ((), ())), preferred_element_type=F32)
    finish(ranks, inv, whole, rows, mine, theirs)


def project(gradients, gathered, inverse, ranks):
    depth = gradients.shape[1]
    half = pl.BlockSpec((1, HALF, WIDTH), lambda n, r: (n, 0, 0))
    return pl.pallas_call(
        project_kernel,
        grid_spec=pltpu.PrefetchScalarGridSpec(
            num_scalar_prefetch=1,
            grid=(MATS,),
            in_specs=[
                pl.BlockSpec((1, depth, RANK), lambda n, r: (n, 0, 0)),
                pl.BlockSpec((1, depth, WIDTH), lambda n, r: (n, 0, 0)),
                pl.BlockSpec((1, RANK, RANK), lambda n, r: (n, 0, 0)),
            ],
            out_specs=[half, half],
            scratch_shapes=[pltpu.VMEM((RANK, RANK), F32)],
        ),
        out_shape=[
            jax.ShapeDtypeStruct((MATS, HALF, WIDTH), F32),
            jax.ShapeDtypeStruct((MATS, HALF, WIDTH), BF16),
        ],
        compiler_params=params(),
        cost_estimate=cost(MATS * 2 * RANK * WIDTH * (depth + 6 * RANK), MATS * 2 * depth * (WIDTH + RANK)),
    )(ranks, gathered, gradients, inverse)


def basis_kernel(root, s, inv, out):
    value = lax.dot_general(
        s[0], inv[0], (((1,), (1,)), ((), ())), precision=EXACT, preferred_element_type=F32
    )
    out[0] = (value * root).astype(BF16)


def make_basis(total, inverse, root):
    share = pl.BlockSpec((1, SHARE, RANK), lambda n: (n, 0, 0))
    return pl.pallas_call(
        functools.partial(basis_kernel, root),
        grid=(MATS,),
        in_specs=[share, pl.BlockSpec((1, RANK, RANK), lambda n: (n, 0, 0))],
        out_specs=share,
        out_shape=jax.ShapeDtypeStruct((MATS, SHARE, RANK), BF16),
        compiler_params=params(),
        cost_estimate=cost(4 * 12 * SHARE * RANK * RANK, 4 * SHARE * RANK * 10),
    )(total, inverse)


def inverse_kernel(where, own, other, out, gram, scaled, blocks):
    x, core = where[0], where[1]
    piece = own.shape[1]
    for j, off in enumerate(OFFS):
        start = pl.multiple_of(lax.rem(x + off, RING) * piece, piece)
        blocks[core, pl.ds(start, piece), :] = own[j]
        blocks[1 - core, pl.ds(start, piece), :] = other[j]
    for m in range(MATS):
        corner, side, last = (
            blocks[m // 2, ((m % 2) * TRI + i) * HALF : ((m % 2) * TRI + i + 1) * HALF] for i in range(TRI)
        )
        gram[m, :HALF, :HALF] = corner
        gram[m, HALF:, :HALF] = side
        gram[m, :HALF, HALF:] = jnp.transpose(side)
        gram[m, HALF:, HALF:] = last
    rows = lax.broadcasted_iota(jnp.int32, (RANK, RANK), 0)
    cols = lax.broadcasted_iota(jnp.int32, (RANK, RANK), 1)
    eye = (rows == cols).astype(F32)
    weight = jnp.where(rows > cols, 1.0, 0.5 * eye)

    def diagonal(a, axis):
        return jnp.sum(jnp.where(rows == cols, a, 0.0), axis=axis, keepdims=True)

    def halves(v):
        high = v.astype(BF16)
        return high, (v - high.astype(F32)).astype(BF16)

    def product(u, v, last=False):
        dims = (((1,), (1 if last else 0,)), ((), ()))
        return lax.dot_general(u, v, dims, preferred_element_type=F32)

    def product3(u, v, last=False):
        (a, b), (c, d) = halves(u), halves(v)
        return product(a, c, last) + (product(a, d, last) + product(b, c, last))

    def rough(value, a):
        value = value.astype(BF16)
        return product(product(value, a.astype(BF16)).astype(BF16), value, True) - eye

    def fine(value, a):
        return product3(product3(value, a), value, True) - eye

    def less(value, error):
        return value - product((weight * error).astype(BF16), value.astype(BF16))

    for m in range(MATS):
        a = gram[m]
        scaled[m] = a * lax.rsqrt(diagonal(a, 1)) * lax.rsqrt(diagonal(a, 0))
    for m in range(MATS):
        out[m] = eye - weight * (scaled[m] - eye)
    for _ in range(2):
        for m in range(MATS):
            value = out[m]
            out[m] = less(value, rough(value, scaled[m]))

    def exact_step(carry):
        count, _ = carry
        large = jnp.zeros((RANK, RANK), F32)
        for m in range(MATS):
            value = out[m]
            error = fine(value, scaled[m])
            large = jnp.maximum(large, jnp.where(error == error, jnp.abs(error), 1e9))
            large = jnp.maximum(large, jnp.where((rows == cols) & (value <= 0.0), 1e9, 0.0))
            out[m] = less(value, error)
        return count + 1, jnp.max(large)

    _, left = lax.while_loop(
        lambda c: (c[0] < NEWTON_MAX) & (c[1] > NEWTON_TOL) & (c[1] < 1e8),
        exact_step,
        (jnp.int32(0), jnp.float32(1.0)),
    )
    done = left <= NEWTON_TOL

    @pl.when(done)
    def _():
        for m in range(MATS):
            out[m] = out[m] * lax.rsqrt(diagonal(gram[m], 0))

    @pl.when(jnp.logical_not(done))
    def _():
        row_ids = lax.broadcasted_iota(jnp.int32, (RANK, 1), 0)
        col_ids = lax.broadcasted_iota(jnp.int32, (1, RANK), 1)

        def matrix(m, _):
            out[m] = eye

            def column(j, _):
                pivot_row = gram[m, pl.ds(j, 1), :]
                pivot = jnp.sum(jnp.where(col_ids == j, pivot_row, 0.0), axis=1, keepdims=True)
                values = jnp.sum(jnp.where(cols == j, gram[m], 0.0), axis=1, keepdims=True)
                factor = jnp.where(row_ids > j, values / pivot, 0.0)
                known = out[m, pl.ds(j, 1), :]
                gram[m] = gram[m] - factor * pivot_row
                out[m] = out[m] - factor * known
                out[m, pl.ds(j, 1), :] = known / jnp.sqrt(pivot)
                return 0

            return lax.fori_loop(0, RANK, column, 0)

        lax.fori_loop(0, MATS, matrix, 0)


def inverse_factors(where, own, other):
    piece = own.shape[1]
    return pl.pallas_call(
        inverse_kernel,
        grid_spec=pltpu.PrefetchScalarGridSpec(
            num_scalar_prefetch=1,
            grid=(1,),
            in_specs=[pl.BlockSpec((RING, piece, HALF), lambda n, w: (0, 0, 0))] * 2,
            out_specs=pl.BlockSpec((MATS, RANK, RANK), lambda n, w: (0, 0, 0)),
            scratch_shapes=[
                pltpu.VMEM((MATS, RANK, RANK), F32),
                pltpu.VMEM((MATS, RANK, RANK), F32),
                pltpu.VMEM((2, RING * piece, HALF), F32),
            ],
        ),
        out_shape=jax.ShapeDtypeStruct((MATS, RANK, RANK), F32),
        compiler_params=params(),
        cost_estimate=cost(8e9, 4 * MATS * RANK * RANK * 4),
    )(where, own, other)


def from_others(value, axis):
    return [shift(value, axis, -1), shift(value, axis, 1), shift(value, axis, 2)]


def x_pieces(whole):
    x = place()[0]

    def piece(off):
        return lax.dynamic_index_in_dim(whole, (x + off) % RING, 0, keepdims=False)

    def sent(off, step):
        return piece(off), "x", step

    return piece, [sent(1, 1), sent(3, -1), sent(2, 2)]


def summed_grams(grams):
    core = place()[1]
    send = lax.dynamic_slice_in_dim(grams, 2 * (1 - core), 2, 0)
    keep = lax.dynamic_slice_in_dim(grams, 2 * core, 2, 0)
    whole = (keep + shift(send, "core", 1)).reshape(RING, 2 * TRI * HALF // RING, HALF)
    piece, outgoing = x_pieces(whole)
    part = piece(0)
    for arrived in [shift(*args) for args in outgoing]:
        part = part + arrived
    for axis in ("y", "z"):
        for arrived in from_others(part, axis):
            part = part + arrived
    own = jnp.stack([part] + from_others(part, "x"))
    return own, shift(own, "core", 1)


def local(gradients, sketch):
    root = float(gradients.shape[1] * lax.axis_size("row")) ** 0.5
    grads = gradients.reshape(MATS, SHARES, SHARE, WIDTH)
    x, core, y, z = place()
    here = {"y": y, "z": z}
    pairs = (("y", "z"), ("z", "y"))

    listed, base = [], {}

    def enlist(name, rows):
        base[name] = len(listed)
        listed.extend(rows)

    links = [(sign, p) for sign in (1, -1) for p in range(2)]
    moving = {link: 2 * link[1] + (link[0] < 0) for link in links}
    enlist("far", [chunk_row(moving[link], pairs[link[1]][0], here[pairs[link[1]][0]] + 2) for link in links])
    enlist(
        "near",
        [chunk_row(moving[-s, p], pairs[p][0], here[pairs[p][0]] + s % RING) for s, p in links],
    )
    for sign in (1, -1):
        fars = [2 * p if sign == 1 else 2 * p + 1 for p in range(2)]
        enlist(("hop2", sign), [chunk_row(m, r[0], here[r[0]] + sign % RING) for m, r in zip(fars, pairs)])
    for p, (ring, _) in enumerate(pairs):
        enlist(("own", p), [chunk_row(2 * p + i, ring, here[ring]) for i in range(2)])
    table = jnp.stack([jnp.asarray(v, jnp.int32) for row in listed for v in row]).reshape(-1, 5)

    hop1, near, hop2 = {}, {}, {}
    sent = sketch_chunks(grads, sketch, table, base["far"])
    for (sign, p), value in zip(links, sent):
        hop1[p, sign] = shift(value, pairs[p][0], sign)
    table, *_ = lax.optimization_barrier((table, *sent))
    sent = sketch_chunks(grads, sketch, table, base["near"])
    for (sign, p), value in zip(links, sent):
        near[p, sign] = shift(value, pairs[p][0], sign)
    table, *_ = lax.optimization_barrier((table, *sent))
    for sign in (1, -1):
        recvs = (hop1[0, sign], hop1[1, sign])
        for p, value in enumerate(combined_chunks(grads, sketch, table, base["hop2", sign], recvs)):
            hop2[p, sign] = shift(value, pairs[p][0], sign)
    part = [
        own_and_near(grads, sketch, table, base["own", p], (near[p, -1], near[p, 1])) for p in range(2)
    ]
    held = lax.optimization_barrier((*part, *hop2.values()))
    part, hop2 = held[:2], dict(zip(hop2, held[2:]))
    owns, parts = [], []
    for p, (_, cross) in enumerate(pairs):
        own, ahead, behind, across = own_chunks(part[p], (hop2[p, 1], hop2[p, -1]))
        owns.append(own)
        parts.append([shift(ahead, cross, 1), shift(behind, cross, -1), shift(across, cross, 2)])
    total, rounded = zip(*(totals(own, arrived) for own, arrived in zip(owns, parts)))
    gathered = lax.all_gather(jnp.concatenate(rounded, axis=0), "mat", axis=1, tiled=True)
    total = jnp.concatenate(total, axis=0)

    where = jnp.stack([x, core]).astype(jnp.int32)
    inverse = inverse_factors(where, *summed_grams(gram_parts(total)))

    ranks = [(x + off) % RING * 2 + core for off in OFFS]
    ranks += [(x + off) % RING * 2 + 1 - core for off in OFFS]
    ranks = jnp.stack(ranks).astype(jnp.int32)
    basis = make_basis(total, inverse, root)
    mine, theirs = project(gradients, gathered, inverse, ranks)
    both = (mine + shift(theirs, "core", 1).astype(F32)).reshape(MATS, RING, BLOCK, WIDTH)
    out = both[:, 0]
    for j, step in ((1, 1), (2, -1), (3, 2)):
        out = out + shift(both[:, j].astype(BF16), "x", step).astype(F32)
    return basis, out


def solution(mesh):
    placed = (P(None, "row", "mat"), P("mat", None))
    return jax.shard_map(
        local,
        mesh=mesh,
        in_specs=placed,
        out_specs=(P(None, ("row", "mat"), None), P(None, "row", "mat")),
        check_vma=False,
    )
```

time: 190 us -> 182 us (0.958)
  waiting for transfers between devices: 62.4 us -> 56.4 us
  other arithmetic: 4.35 us -> 1.96 us
    ppermute x20 -> x24, waiting for transfers between devices: 37 us -> 23.7 us  [shift(): return lax.ppermute(value, 'mat', pairs)]
    all_gather x1, waiting for transfers between devices: 8.72 us -> 17 us  [local(): lax.all_gather(jnp.concatenate(rounded, axis=0), 'mat', axis=1, tiled=True)]
    pallas_call x2 -> x5, Pallas kernels: 6.57 us -> 13 us  [the longest x2 7.64 us: own_and_near(): pl.pallas_call(near_kernel, grid_spec=pltpu.PrefetchScalarGridSpec(num_sc...]
    pallas_call x1, Pallas kernels: 12.1 us -> 7.13 us  [inverse_factors(): pl.pallas_call(inverse_kernel, grid_spec=pltpu.PrefetchScalarGridSpec(num...]
    pallas_call x2, Pallas kernels: 3.21 us -> 0.27 us  [totals(): pl.pallas_call(total_kernel, grid=(2,), in_specs=[share] * 4, out_specs=[...]
    ppermute x20 -> x24, starting transfers between devices: 35.2 us -> 36.5 us  [shift(): return lax.ppermute(value, 'mat', pairs)]
  transfers between devices with their start and end apart: 33 -> 37, of which waited for: 27 -> 21; matrix products, arithmetic and copies ran while one was open for 2% -> 0% of each run, Pallas kernels for 16% -> 18%
where the time goes in v3:
time: 182 us
  waiting for transfers between devices  56.4 us (31%)
  starting transfers between devices  52.7 us (29%)
  Pallas kernels  52.7 us (29%)
  between operations  14.6 us (8%)
  local copies, waits for them, and re-layouts  3.3 us (2%)
  other arithmetic  1.96 us (1%)
    ppermute x24, starting transfers between devices, shift(): return lax.ppermute(value, 'mat', pairs)  36.5 us
    ppermute x24, waiting for transfers between devices, shift(): return lax.ppermute(value, 'mat', pairs)  23.7 us
    all_gather x1, waiting for transfers between devices, local(): lax.all_gather(jnp.concatenate(rounded, axis=0), 'mat', axis=1, tiled=True)  17 us
    ppermute x12, starting transfers between devices, shift(): return lax.ppermute(value, 'row', pairs)  16.2 us
    ppermute x12, waiting for transfers between devices, shift(): return lax.ppermute(value, 'row', pairs)  15.7 us
    pallas_call x1, Pallas kernels, project(): pl.pallas_call(project_kernel, grid_spec=pltpu.PrefetchScalarGridSpec(num...  12.7 us
    pallas_call x2, Pallas kernels, sketch_chunks(): pl.pallas_call(sketch_kernel, grid_spec=pltpu.PrefetchScalarGridSpec(num_...  10.7 us
    pallas_call x2, Pallas kernels, own_and_near(): pl.pallas_call(near_kernel, grid_spec=pltpu.PrefetchScalarGridSpec(num_sc...  7.64 us
  transfers between devices with their start and end apart: 37, of which 21 were waited for; matrix products, arithmetic and copies ran while one was open for 0% of the time, Pallas kernels for 18%

profile of v3, /device:TPU:0, one launch (start us, length us, event | category | flops | bytes accessed | tf_op | source)
XLA Modules:
  0.0 181.6 jit_solution(13318095028662140531)
XLA Ops:
  8.6 5.4 %shard_map.41 = (bf16[1,896,256]{2,1,0:T(8,128)(2,1)S(1)}, bf16[1,896,256]{2,1,0:T(8,128)(2,1)S(1)}, bf16[1,896,256]{2,1,0:T(8,128)(2,1)S(1)}, bf16[1,896,256]{2,1,0:T(8,128)(2,1)}) custom-call(s32[16,5]{1,0:T(8,128)S(1)} %reshape.19.tab, bf16[4,16,224,512]{3,2,1,0:T(8,128)(2,1)} %bitcast.59, bf16[4,16,224,512]{3,2,1,0:T(8,128)(2,1)} %bitcast.60, ...), custom_call_target="tpu_custom_call" | custom-call | flops 939524096 | bytes 7340032 | tf_op jit(solution)/shard_map/pallas_call | solution.py:85
  15.6 1.9 %collective-permute-start.5 = (bf16[1,896,256]{2,1,0:T(8,128)(2,1)S(1)}, bf16[1,896,256]{2,1,0:T(8,128)(2,1)S(1)}, u32[]{:S(2)}, u32[]{:S(2)}) collective-permute-start(bf16[1,896,256]{2,1,0:T(8,128)(2,1)S(1)} %get-tuple-element.37), channel_id=1, source_target_pairs={{0,4},{1,5},{2,6},{3,7},{4,8},{5,9},{6,10},{7,11},{8,12},{9,13},{1... | collective-permute-start | bytes 1376264 | tf_op jit(solution)/shard_map/ppermute | solution.py:35
  19.2 2.1 %collective-permute-start.9 = (bf16[1,896,256]{2,1,0:T(8,128)(2,1)}, bf16[1,896,256]{2,1,0:T(8,128)(2,1)S(1)}, u32[]{:S(2)}, u32[]{:S(2)}) collective-permute-start(bf16[1,896,256]{2,1,0:T(8,128)(2,1)} %get-tuple-element.39), channel_id=1, source_target_pairs={{0,12},{1,13},{2,14},{3,15},{4,0},{5,1},{6,2},{7,3},{8,4},{9,5},{1... | collective-permute-start | bytes 1376264 | tf_op jit(solution)/shard_map/ppermute | solution.py:35
  21.3 5.4 %shard_map.42 = (bf16[1,896,256]{2,1,0:T(8,128)(2,1)S(1)}, bf16[1,896,256]{2,1,0:T(8,128)(2,1)S(1)}, bf16[1,896,256]{2,1,0:T(8,128)(2,1)S(1)}, bf16[1,896,256]{2,1,0:T(8,128)(2,1)}) custom-call(s32[16,5]{1,0:T(8,128)S(1)} %reshape.19.tab, bf16[4,16,224,512]{3,2,1,0:T(8,128)(2,1)} %bitcast.63, bf16[4,16,224,512]{3,2,1,0:T(8,128)(2,1)} %bitcast.64, ...), custom_call_target="tpu_custom_call" | custom-call | flops 939524096 | bytes 7340032 | tf_op jit(solution)/shard_map/pallas_call | solution.py:85
  29.9 2.0 %collective-permute-start.2 = (bf16[1,896,256]{2,1,0:T(8,128)(2,1)}, bf16[1,896,256]{2,1,0:T(8,128)(2,1)S(1)}, u32[]{:S(2)}, u32[]{:S(2)}) collective-permute-start(bf16[1,896,256]{2,1,0:T(8,128)(2,1)} %get-tuple-element.44), channel_id=1, source_target_pairs={{0,12},{1,13},{2,14},{3,15},{4,0},{5,1},{6,2},{7,3},{8,4},{9,5},{1... | collective-permute-start | bytes 1376264 | tf_op jit(solution)/shard_map/ppermute | solution.py:35
  31.9 3.2 %shard_map.45 = (bf16[1,896,256]{2,1,0:T(8,128)(2,1)S(1)}, bf16[1,896,256]{2,1,0:T(8,128)(2,1)S(1)}) custom-call(s32[16,5]{1,0:T(8,128)S(1)} %reshape.19.tab, bf16[4,16,224,512]{3,2,1,0:T(8,128)(2,1)} %bitcast.67, bf16[4,16,224,512]{3,2,1,0:T(8,128)(2,1)} %bitcast.68, bf16[4,16,224,512]{3,2,1,0:T(8,128)(2,1)} %bitcast.69, ...), custom_call_target="tpu_custom_call" | custom-call | flops 469762048 | bytes 3670016 | tf_op jit(solution)/shard_map/pallas_call | solution.py:110
  36.9 3.2 %shard_map.46 = (bf16[1,896,256]{2,1,0:T(8,128)(2,1)S(1)}, bf16[1,896,256]{2,1,0:T(8,128)(2,1)S(1)}) custom-call(s32[16,5]{1,0:T(8,128)S(1)} %reshape.19.tab, bf16[4,16,224,512]{3,2,1,0:T(8,128)(2,1)} %bitcast.71, bf16[4,16,224,512]{3,2,1,0:T(8,128)(2,1)} %bitcast.72, bf16[4,16,224,512]{3,2,1,0:T(8,128)(2,1)} %bitcast.73, ...), custom_call_target="tpu_custom_call" | custom-call | flops 469762048 | bytes 3670016 | tf_op jit(solution)/shard_map/pallas_call | solution.py:110
  41.0 2.2 %collective-permute-done.1.near1 = bf16[1,896,256]{2,1,0:T(8,128)(2,1)S(1)} collective-permute-done((bf16[1,896,256]{2,1,0:T(8,128)(2,1)S(1)}, bf16[1,896,256]{2,1,0:T(8,128)(2,1)S(1)}, u32[]{:S(2)}, u32[]{:S(2)}) %collective-permute-start.1) | collective-permute-done | bytes 458784 | tf_op jit(solution)/shard_map/ppermute | solution.py:35
  43.9 2.9 %collective-permute-start.11 = (bf16[1,896,256]{2,1,0:T(8,128)(2,1)S(1)}, bf16[1,896,256]{2,1,0:T(8,128)(2,1)S(1)}, u32[]{:S(2)}, u32[]{:S(2)}) collective-permute-start(bf16[1,896,256]{2,1,0:T(8,128)(2,1)S(1)} %get-tuple-element.49), channel_id=1, source_target_pairs={{0,12},{1,13},{2,14},{3,15},{4,0},{5,1},{6,2},{7,3},{8,4},{9,5},{1... | collective-permute-start | bytes 1376264 | tf_op jit(solution)/shard_map/ppermute | solution.py:35
  46.8 3.8 %shard_map.43.part = f32[2,896,256]{2,1,0:T(8,128)} custom-call(s32[16,5]{1,0:T(8,128)S(1)} %reshape.19.tab, bf16[4,16,224,512]{3,2,1,0:T(8,128)(2,1)} %bitcast.75, bf16[4,16,224,512]{3,2,1,0:T(8,128)(2,1)} %bitcast.76, bf16[4,16,224,512]{3,2,1,0:T(8,128)(2,1)} %bitcast.77, bf16[4,16,224,512]{3,2,1,0:T(8,128)(2,1)} %bitcast.78, ...), custom_call_target="tpu_custom_call" | custom-call | flops 469762048 | bytes 3670016 | tf_op jit(solution)/shard_map/pallas_call | solution.py:134
  50.6 3.8 %shard_map.44.part = f32[2,896,256]{2,1,0:T(8,128)} custom-call(s32[16,5]{1,0:T(8,128)S(1)} %reshape.19.tab, bf16[4,16,224,512]{3,2,1,0:T(8,128)(2,1)} %bitcast.79, bf16[4,16,224,512]{3,2,1,0:T(8,128)(2,1)} %bitcast.80, bf16[4,16,224,512]{3,2,1,0:T(8,128)(2,1)} %bitcast.81, bf16[4,16,224,512]{3,2,1,0:T(8,128)(2,1)} %bitcast.82, ...), custom_call_target="tpu_custom_call" | custom-call | flops 469762048 | bytes 3670016 | tf_op jit(solution)/shard_map/pallas_call | solution.py:134
  54.4 2.7 %collective-permute-done.7.comb0 = bf16[1,896,256]{2,1,0:T(8,128)(2,1)S(1)} collective-permute-done((bf16[1,896,256]{2,1,0:T(8,128)(2,1)S(1)}, bf16[1,896,256]{2,1,0:T(8,128)(2,1)S(1)}, u32[]{:S(2)}, u32[]{:S(2)}) %collective-permute-start.7) | collective-permute-done | bytes 458784 | tf_op jit(solution)/shard_map/ppermute | solution.py:35
  59.9 3.2 %collective-permute-start.13 = (bf16[2,224,256]{2,1,0:T(8,128)(2,1)S(1)}, bf16[2,224,256]{2,1,0:T(8,128)(2,1)S(1)}, u32[]{:S(2)}, u32[]{:S(2)}) collective-permute-start(bf16[2,224,256]{2,1,0:T(8,128)(2,1)S(1)} %get-tuple-element.55), channel_id=1, source_target_pairs={{0,12},{1,13},{2,14},{3,15},{4,0},{5,1},{6,2},{7,3},{8,4},{9,5},{1... | collective-permute-start | bytes 688136 | tf_op jit(solution)/shard_map/ppermute | solution.py:35
  68.1 3.7 %collective-permute-done.12.a = bf16[2,224,256]{2,1,0:T(8,128)(2,1)S(1)} collective-permute-done((bf16[2,224,256]{2,1,0:T(8,128)(2,1)S(1)}, bf16[2,224,256]{2,1,0:T(8,128)(2,1)S(1)}, u32[]{:S(2)}, u32[]{:S(2)}) %collective-permute-start.12) | collective-permute-done | bytes 229408 | tf_op jit(solution)/shard_map/ppermute | solution.py:35
  71.8 2.7 %collective-permute-start.17 = (bf16[2,224,256]{2,1,0:T(8,128)(2,1)S(1)}, bf16[2,224,256]{2,1,0:T(8,128)(2,1)S(1)}, u32[]{:S(2)}, u32[]{:S(2)}) collective-permute-start(bf16[2,224,256]{2,1,0:T(8,128)(2,1)S(1)} %get-tuple-element.64), channel_id=1, source_target_pairs={{0,2},{1,3},{2,0},{3,1},{4,6},{5,7},{6,4},{7,5},{8,10},{9,11},{10,... | collective-permute-start | bytes 688136 | tf_op jit(solution)/shard_map/ppermute | solution.py:35
  74.7 4.7 %collective-permute-done.17.c = bf16[2,224,256]{2,1,0:T(8,128)(2,1)S(1)} collective-permute-done((bf16[2,224,256]{2,1,0:T(8,128)(2,1)S(1)}, bf16[2,224,256]{2,1,0:T(8,128)(2,1)S(1)}, u32[]{:S(2)}, u32[]{:S(2)}) %collective-permute-start.17) | collective-permute-done | bytes 229408 | tf_op jit(solution)/shard_map/ppermute | solution.py:35
  84.2 3.1 %collective-permute-start.21 = (f32[192,128]{1,0:T(8,128)S(1)}, f32[192,128]{1,0:T(8,128)S(1)}, u32[]{:S(2)}, u32[]{:S(2)}) collective-permute-start(f32[192,128]{1,0:T(8,128)S(1)} %get-tuple-element.74), channel_id=1, source_target_pairs={{0,64},{16,80},{32,96},{48,112},{64,0},{80,16},{96,32},{112,48},{1... | collective-permute-start | bytes 294920 | tf_op jit(solution)/shard_map/ppermute | solution.py:40
  90.8 2.0 %collective-permute-done.20 = f32[192,128]{1,0:T(8,128)S(1)} collective-permute-done((f32[192,128]{1,0:T(8,128)S(1)}, f32[192,128]{1,0:T(8,128)S(1)}, u32[]{:S(2)}, u32[]{:S(2)}) %collective-permute-start.20) | collective-permute-done | bytes 98336 | tf_op jit(solution)/shard_map/ppermute | solution.py:40
  94.3 2.8 %collective-permute-start.24 = (f32[192,128]{1,0:T(8,128)S(1)}, f32[192,128]{1,0:T(8,128)S(1)}, u32[]{:S(2)}, u32[]{:S(2)}) collective-permute-start(f32[192,128]{1,0:T(8,128)S(1)} %fusion.4), channel_id=1, source_target_pairs={{0,2},{1,3},{2,0},{3,1},{4,6},{5,7},{6,4},{7,5},{8,10},{9,11},{10,... | collective-permute-start | bytes 294920 | tf_op jit(solution)/shard_map/ppermute | solution.py:35
  98.1 2.3 %collective-permute-start.22 = (f32[192,128]{1,0:T(8,128)S(1)}, f32[192,128]{1,0:T(8,128)S(1)}, u32[]{:S(2)}, u32[]{:S(2)}) collective-permute-start(f32[192,128]{1,0:T(8,128)S(1)} %fusion.4), channel_id=1, source_target_pairs={{0,3},{1,0},{2,1},{3,2},{4,7},{5,4},{6,5},{7,6},{8,11},{9,8},{10,9... | collective-permute-start | bytes 294920 | tf_op jit(solution)/shard_map/ppermute | solution.py:35
  100.3 2.5 %collective-permute-done.24 = f32[192,128]{1,0:T(8,128)S(1)} collective-permute-done((f32[192,128]{1,0:T(8,128)S(1)}, f32[192,128]{1,0:T(8,128)S(1)}, u32[]{:S(2)}, u32[]{:S(2)}) %collective-permute-start.24) | collective-permute-done | bytes 98336 | tf_op jit(solution)/shard_map/ppermute | solution.py:35
  102.8 2.6 %collective-permute-done.23 = f32[192,128]{1,0:T(8,128)S(1)} collective-permute-done((f32[192,128]{1,0:T(8,128)S(1)}, f32[192,128]{1,0:T(8,128)S(1)}, u32[]{:S(2)}, u32[]{:S(2)}) %collective-permute-start.23) | collective-permute-done | bytes 98336 | tf_op jit(solution)/shard_map/ppermute | solution.py:35
  106.4 2.5 %collective-permute-start.25 = (f32[192,128]{1,0:T(8,128)S(1)}, f32[192,128]{1,0:T(8,128)S(1)}, u32[]{:S(2)}, u32[]{:S(2)}) collective-permute-start(f32[192,128]{1,0:T(8,128)S(1)} %add_add_fusion.1), channel_id=1, source_target_pairs={{0,12},{1,13},{2,14},{3,15},{4,0},{5,1},{6,2},{7,3},{8,4},{9,5},{1... | collective-permute-start | bytes 294920 | tf_op jit(solution)/shard_map/ppermute | solution.py:35
  108.8 3.4 %collective-permute-done.27 = f32[192,128]{1,0:T(8,128)S(1)} collective-permute-done((f32[192,128]{1,0:T(8,128)S(1)}, f32[192,128]{1,0:T(8,128)S(1)}, u32[]{:S(2)}, u32[]{:S(2)}) %collective-permute-start.27) | collective-permute-done | bytes 98336 | tf_op jit(solution)/shard_map/ppermute | solution.py:35
  113.0 2.5 %collective-permute-start.30 = (f32[192,128]{1,0:T(8,128)S(1)}, f32[192,128]{1,0:T(8,128)S(1)}, u32[]{:S(2)}, u32[]{:S(2)}) collective-permute-start(f32[192,128]{1,0:T(8,128)S(1)} %add_add_fusion), channel_id=1, source_target_pairs={{0,64},{16,80},{32,96},{48,112},{64,0},{80,16},{96,32},{112,48},{1... | collective-permute-start | bytes 294920 | tf_op jit(solution)/shard_map/ppermute | solution.py:40
  116.1 2.7 %collective-permute-start.28 = (f32[192,128]{1,0:T(8,128)S(1)}, f32[192,128]{1,0:T(8,128)S(1)}, u32[]{:S(2)}, u32[]{:S(2)}) collective-permute-start(f32[192,128]{1,0:T(8,128)S(1)} %add_add_fusion), channel_id=1, source_target_pairs={{0,96},{16,112},{32,0},{48,16},{64,32},{80,48},{96,64},{112,80},{1... | collective-permute-start | bytes 294920 | tf_op jit(solution)/shard_map/ppermute | solution.py:40
  123.3 7.1 %shard_map.52.inv = f32[4,256,256]{2,1,0:T(8,128)S(1)} custom-call(s32[2]{0:T(128)S(1)} %pad_add_fusion.where, f32[4,192,128]{2,1,0:T(8,128)S(1)} %pad_maximum_fusion.1.own, f32[4,192,128]{2,1,0:T(8,128)S(1)} %collective-permute-done.31.other), custom_call_target="tpu_custom_call" | custom-call | flops 8000000000 | bytes 4194304 | tf_op jit(solution)/shard_map/pallas_call | solution.py:383
  131.5 17.0 %all-gather.2.cloned.1.call-done.s = bf16[4,3584,256]{2,1,0:T(8,128)(2,1)} async-done(((bf16[4,224,256]{2,1,0:T(8,128)(2,1)}), bf16[4,3584,256]{2,1,0:T(8,128)(2,1)}) %all-gather.2.cloned.1.call-update) | async-done | bytes 7340048 | tf_op jit(solution)/shard_map/all_gather | solution.py:485
  148.6 12.7 %shard_map.54 = (f32[4,128,512]{2,1,0:T(8,128)S(1)}, bf16[4,128,512]{2,1,0:T(8,128)(2,1)S(1)}) custom-call(s32[8]{0:T(128)S(1)} %stack.183.ranks, bf16[4,3584,256]{2,1,0:T(8,128)(2,1)} %all-gather.2.cloned.1.call-done.s, bf16[4,3584,512]{2,1,0:T(8,128)(2,1)} %g.1, f32[4,256,256]{2,1,0:T(8,128)} %copy-done.1), custom_call_target="tpu_custom_call" | custom-call | flops 5368709120 | bytes 22020096 | tf_op jit(solution)/shard_map/pallas_call | solution.py:237
  163.5 3.0 %collective-permute-start.35 = (bf16[4,32,512]{2,1,0:T(8,128)(2,1)S(1)}, bf16[4,32,512]{2,1,0:T(8,128)(2,1)S(1)}, u32[]{:S(2)}, u32[]{:S(2)}) collective-permute-start(bf16[4,32,512]{2,1,0:T(8,128)(2,1)S(1)} %get-tuple-element.71), channel_id=1, source_target_pairs={{0,64},{16,80},{32,96},{48,112},{64,0},{80,16},{96,32},{112,48},{1... | collective-permute-start | bytes 393224 | tf_op jit(solution)/shard_map/ppermute | solution.py:40
  168.5 2.5 %shard_map.53 = bf16[4,224,256]{2,1,0:T(8,128)(2,1)} custom-call(f32[4,224,256]{2,1,0:T(8,128)S(1)} %constant_dynamic-update-slice_fusion.s, f32[4,256,256]{2,1,0:T(8,128)S(1)} %copy-done.2), custom_call_target="tpu_custom_call" | custom-call | flops 704643072 | bytes 2293760 | tf_op jit(solution)/shard_map/pallas_call | solution.py:268
  171.4 2.0 %collective-permute-done.34 = bf16[4,32,512]{2,1,0:T(8,128)(2,1)S(1)} collective-permute-done((bf16[4,32,512]{2,1,0:T(8,128)(2,1)S(1)}, bf16[4,32,512]{2,1,0:T(8,128)(2,1)S(1)}, u32[]{:S(2)}, u32[]{:S(2)}) %collective-permute-start.34) | collective-permute-done | bytes 131104 | tf_op jit(solution)/shard_map/ppermute | solution.py:40
  (88 shorter events, 43.5 us)
Async XLA Ops:
  7.2 141.4 %all-gather.2.cloned.1.call-start = ((), (), s32[]{:S(2)}) async-start(), calls=%async_computation | async-start | bytes 7798784 | tf_op jit(solution)/shard_map/all_gather | solution.py:485
  13.9 14.5 %collective-permute-start.4 = (bf16[1,896,256]{2,1,0:T(8,128)(2,1)S(1)}, bf16[1,896,256]{2,1,0:T(8,128)(2,1)S(1)}, u32[]{:S(2)}, u32[]{:S(2)}) collective-permute-start(bf16[1,896,256]{2,1,0:T(8,128)(2,1)S(1)} %get-tuple-element.36), channel_id=1, source_target_pairs={{0,1},{1,2},{2,3},{3,0},{4,5},{5,6},{6,7},{7,4},{8,9},{9,10},{10,1... | collective-permute-start | bytes 1376264 | tf_op jit(solution)/shard_map/ppermute | solution.py:35
  15.6 14.3 %collective-permute-start.5 = (bf16[1,896,256]{2,1,0:T(8,128)(2,1)S(1)}, bf16[1,896,256]{2,1,0:T(8,128)(2,1)S(1)}, u32[]{:S(2)}, u32[]{:S(2)}) collective-permute-start(bf16[1,896,256]{2,1,0:T(8,128)(2,1)S(1)} %get-tuple-element.37), channel_id=1, source_target_pairs={{0,4},{1,5},{2,6},{3,7},{4,8},{5,9},{6,10},{7,11},{8,12},{9,13},{1... | collective-permute-start | bytes 1376264 | tf_op jit(solution)/shard_map/ppermute | solution.py:35
  17.5 17.6 %collective-permute-start.8 = (bf16[1,896,256]{2,1,0:T(8,128)(2,1)S(1)}, bf16[1,896,256]{2,1,0:T(8,128)(2,1)S(1)}, u32[]{:S(2)}, u32[]{:S(2)}) collective-permute-start(bf16[1,896,256]{2,1,0:T(8,128)(2,1)S(1)} %get-tuple-element.38), channel_id=1, source_target_pairs={{0,3},{1,0},{2,1},{3,2},{4,7},{5,4},{6,5},{7,6},{8,11},{9,8},{10,9... | collective-permute-start | bytes 1376264 | tf_op jit(solution)/shard_map/ppermute | solution.py:35
  19.2 16.0 %collective-permute-start.9 = (bf16[1,896,256]{2,1,0:T(8,128)(2,1)}, bf16[1,896,256]{2,1,0:T(8,128)(2,1)S(1)}, u32[]{:S(2)}, u32[]{:S(2)}) collective-permute-start(bf16[1,896,256]{2,1,0:T(8,128)(2,1)} %get-tuple-element.39), channel_id=1, source_target_pairs={{0,12},{1,13},{2,14},{3,15},{4,0},{5,1},{6,2},{7,3},{8,4},{9,5},{1... | collective-permute-start | bytes 1376264 | tf_op jit(solution)/shard_map/ppermute | solution.py:35
  26.7 13.4 %collective-permute-start = (bf16[1,896,256]{2,1,0:T(8,128)(2,1)S(1)}, bf16[1,896,256]{2,1,0:T(8,128)(2,1)S(1)}, u32[]{:S(2)}, u32[]{:S(2)}) collective-permute-start(bf16[1,896,256]{2,1,0:T(8,128)(2,1)S(1)} %get-tuple-element.43), channel_id=1, source_target_pairs={{0,3},{1,0},{2,1},{3,2},{4,7},{5,4},{6,5},{7,6},{8,11},{9,8},{10,9... | collective-permute-start | bytes 1376264 | tf_op jit(solution)/shard_map/ppermute | solution.py:35
  28.5 14.7 %collective-permute-start.1 = (bf16[1,896,256]{2,1,0:T(8,128)(2,1)S(1)}, bf16[1,896,256]{2,1,0:T(8,128)(2,1)S(1)}, u32[]{:S(2)}, u32[]{:S(2)}) collective-permute-start(bf16[1,896,256]{2,1,0:T(8,128)(2,1)S(1)} %get-tuple-element.41), channel_id=1, source_target_pairs={{0,1},{1,2},{2,3},{3,0},{4,5},{5,6},{6,7},{7,4},{8,9},{9,10},{10,1... | collective-permute-start | bytes 1376264 | tf_op jit(solution)/shard_map/ppermute | solution.py:35
  29.9 14.0 %collective-permute-start.2 = (bf16[1,896,256]{2,1,0:T(8,128)(2,1)}, bf16[1,896,256]{2,1,0:T(8,128)(2,1)S(1)}, u32[]{:S(2)}, u32[]{:S(2)}) collective-permute-start(bf16[1,896,256]{2,1,0:T(8,128)(2,1)} %get-tuple-element.44), channel_id=1, source_target_pairs={{0,12},{1,13},{2,14},{3,15},{4,0},{5,1},{6,2},{7,3},{8,4},{9,5},{1... | collective-permute-start | bytes 1376264 | tf_op jit(solution)/shard_map/ppermute | solution.py:35
  35.1 15.5 %collective-permute-start.3 = (bf16[1,896,256]{2,1,0:T(8,128)(2,1)S(1)}, bf16[1,896,256]{2,1,0:T(8,128)(2,1)S(1)}, u32[]{:S(2)}, u32[]{:S(2)}) collective-permute-start(bf16[1,896,256]{2,1,0:T(8,128)(2,1)S(1)} %get-tuple-element.42), channel_id=1, source_target_pairs={{0,4},{1,5},{2,6},{3,7},{4,8},{5,9},{6,10},{7,11},{8,12},{9,13},{1... | collective-permute-start | bytes 1376264 | tf_op jit(solution)/shard_map/ppermute | solution.py:35
  35.2 19.2 %collective-permute-start.6 = (bf16[1,896,256]{2,1,0:T(8,128)(2,1)S(1)}, bf16[1,896,256]{2,1,0:T(8,128)(2,1)S(1)}, u32[]{:S(2)}, u32[]{:S(2)}) collective-permute-start(bf16[1,896,256]{2,1,0:T(8,128)(2,1)S(1)} %get-tuple-element.46), channel_id=1, source_target_pairs={{0,1},{1,2},{2,3},{3,0},{4,5},{5,6},{6,7},{7,4},{8,9},{9,10},{10,1... | collective-permute-start | bytes 1376264 | tf_op jit(solution)/shard_map/ppermute | solution.py:35
  40.0 17.1 %collective-permute-start.7 = (bf16[1,896,256]{2,1,0:T(8,128)(2,1)S(1)}, bf16[1,896,256]{2,1,0:T(8,128)(2,1)S(1)}, u32[]{:S(2)}, u32[]{:S(2)}) collective-permute-start(bf16[1,896,256]{2,1,0:T(8,128)(2,1)S(1)} %get-tuple-element.47), channel_id=1, source_target_pairs={{0,4},{1,5},{2,6},{3,7},{4,8},{5,9},{6,10},{7,11},{8,12},{9,13},{1... | collective-permute-start | bytes 1376264 | tf_op jit(solution)/shard_map/ppermute | solution.py:35
  43.2 14.0 %collective-permute-start.10 = (bf16[1,896,256]{2,1,0:T(8,128)(2,1)S(1)}, bf16[1,896,256]{2,1,0:T(8,128)(2,1)S(1)}, u32[]{:S(2)}, u32[]{:S(2)}) collective-permute-start(bf16[1,896,256]{2,1,0:T(8,128)(2,1)S(1)} %get-tuple-element.48), channel_id=1, source_target_pairs={{0,3},{1,0},{2,1},{3,2},{4,7},{5,4},{6,5},{7,6},{8,11},{9,8},{10,9... | collective-permute-start | bytes 1376264 | tf_op jit(solution)/shard_map/ppermute | solution.py:35
  43.9 13.3 %collective-permute-start.11 = (bf16[1,896,256]{2,1,0:T(8,128)(2,1)S(1)}, bf16[1,896,256]{2,1,0:T(8,128)(2,1)S(1)}, u32[]{:S(2)}, u32[]{:S(2)}) collective-permute-start(bf16[1,896,256]{2,1,0:T(8,128)(2,1)S(1)} %get-tuple-element.49), channel_id=1, source_target_pairs={{0,12},{1,13},{2,14},{3,15},{4,0},{5,1},{6,2},{7,3},{8,4},{9,5},{1... | collective-permute-start | bytes 1376264 | tf_op jit(solution)/shard_map/ppermute | solution.py:35
  59.8 12.1 %collective-permute-start.12 = (bf16[2,224,256]{2,1,0:T(8,128)(2,1)S(1)}, bf16[2,224,256]{2,1,0:T(8,128)(2,1)S(1)}, u32[]{:S(2)}, u32[]{:S(2)}) collective-permute-start(bf16[2,224,256]{2,1,0:T(8,128)(2,1)S(1)} %get-tuple-element.54), channel_id=1, source_target_pairs={{0,4},{1,5},{2,6},{3,7},{4,8},{5,9},{6,10},{7,11},{8,12},{9,13},{1... | collective-permute-start | bytes 688136 | tf_op jit(solution)/shard_map/ppermute | solution.py:35
  59.9 14.7 %collective-permute-start.13 = (bf16[2,224,256]{2,1,0:T(8,128)(2,1)S(1)}, bf16[2,224,256]{2,1,0:T(8,128)(2,1)S(1)}, u32[]{:S(2)}, u32[]{:S(2)}) collective-permute-start(bf16[2,224,256]{2,1,0:T(8,128)(2,1)S(1)} %get-tuple-element.55), channel_id=1, source_target_pairs={{0,12},{1,13},{2,14},{3,15},{4,0},{5,1},{6,2},{7,3},{8,4},{9,5},{1... | collective-permute-start | bytes 688136 | tf_op jit(solution)/shard_map/ppermute | solution.py:35
  63.1 11.5 %collective-permute-start.14 = (bf16[2,224,256]{2,1,0:T(8,128)(2,1)S(1)}, bf16[2,224,256]{2,1,0:T(8,128)(2,1)S(1)}, u32[]{:S(2)}, u32[]{:S(2)}) collective-permute-start(bf16[2,224,256]{2,1,0:T(8,128)(2,1)S(1)} %get-tuple-element.56), channel_id=1, source_target_pairs={{0,8},{1,9},{2,10},{3,11},{4,12},{5,13},{6,14},{7,15},{8,0},{9,1},... | collective-permute-start | bytes 688136 | tf_op jit(solution)/shard_map/ppermute | solution.py:35
  64.8 9.9 %collective-permute-start.15 = (bf16[2,224,256]{2,1,0:T(8,128)(2,1)S(1)}, bf16[2,224,256]{2,1,0:T(8,128)(2,1)S(1)}, u32[]{:S(2)}, u32[]{:S(2)}) collective-permute-start(bf16[2,224,256]{2,1,0:T(8,128)(2,1)S(1)} %get-tuple-element.62), channel_id=1, source_target_pairs={{0,1},{1,2},{2,3},{3,0},{4,5},{5,6},{6,7},{7,4},{8,9},{9,10},{10,1... | collective-permute-start | bytes 688136 | tf_op jit(solution)/shard_map/ppermute | solution.py:35
  66.3 8.4 %collective-permute-start.16 = (bf16[2,224,256]{2,1,0:T(8,128)(2,1)S(1)}, bf16[2,224,256]{2,1,0:T(8,128)(2,1)S(1)}, u32[]{:S(2)}, u32[]{:S(2)}) collective-permute-start(bf16[2,224,256]{2,1,0:T(8,128)(2,1)S(1)} %get-tuple-element.63), channel_id=1, source_target_pairs={{0,3},{1,0},{2,1},{3,2},{4,7},{5,4},{6,5},{7,6},{8,11},{9,8},{10,9... | collective-permute-start | bytes 688136 | tf_op jit(solution)/shard_map/ppermute | solution.py:35
  71.8 7.5 %collective-permute-start.17 = (bf16[2,224,256]{2,1,0:T(8,128)(2,1)S(1)}, bf16[2,224,256]{2,1,0:T(8,128)(2,1)S(1)}, u32[]{:S(2)}, u32[]{:S(2)}) collective-permute-start(bf16[2,224,256]{2,1,0:T(8,128)(2,1)S(1)} %get-tuple-element.64), channel_id=1, source_target_pairs={{0,2},{1,3},{2,0},{3,1},{4,6},{5,7},{6,4},{7,5},{8,10},{9,11},{10,... | collective-permute-start | bytes 688136 | tf_op jit(solution)/shard_map/ppermute | solution.py:35
  84.2 6.6 %collective-permute-start.21 = (f32[192,128]{1,0:T(8,128)S(1)}, f32[192,128]{1,0:T(8,128)S(1)}, u32[]{:S(2)}, u32[]{:S(2)}) collective-permute-start(f32[192,128]{1,0:T(8,128)S(1)} %get-tuple-element.74), channel_id=1, source_target_pairs={{0,64},{16,80},{32,96},{48,112},{64,0},{80,16},{96,32},{112,48},{1... | collective-permute-start | bytes 294920 | tf_op jit(solution)/shard_map/ppermute | solution.py:40
  88.4 5.8 %collective-permute-start.19 = (f32[192,128]{1,0:T(8,128)S(1)}, f32[192,128]{1,0:T(8,128)S(1)}, u32[]{:S(2)}, u32[]{:S(2)}) collective-permute-start(f32[192,128]{1,0:T(8,128)S(1)} %get-tuple-element.73), channel_id=1, source_target_pairs={{0,32},{16,48},{32,64},{48,80},{64,96},{80,112},{96,0},{112,16},{1... | collective-permute-start | bytes 294920 | tf_op jit(solution)/shard_map/ppermute | solution.py:40
  94.3 8.6 %collective-permute-start.24 = (f32[192,128]{1,0:T(8,128)S(1)}, f32[192,128]{1,0:T(8,128)S(1)}, u32[]{:S(2)}, u32[]{:S(2)}) collective-permute-start(f32[192,128]{1,0:T(8,128)S(1)} %fusion.4), channel_id=1, source_target_pairs={{0,2},{1,3},{2,0},{3,1},{4,6},{5,7},{6,4},{7,5},{8,10},{9,11},{10,... | collective-permute-start | bytes 294920 | tf_op jit(solution)/shard_map/ppermute | solution.py:35
  97.1 8.3 %collective-permute-start.23 = (f32[192,128]{1,0:T(8,128)S(1)}, f32[192,128]{1,0:T(8,128)S(1)}, u32[]{:S(2)}, u32[]{:S(2)}) collective-permute-start(f32[192,128]{1,0:T(8,128)S(1)} %fusion.4), channel_id=1, source_target_pairs={{0,1},{1,2},{2,3},{3,0},{4,5},{5,6},{6,7},{7,4},{8,9},{9,10},{10,1... | collective-permute-start | bytes 294920 | tf_op jit(solution)/shard_map/ppermute | solution.py:35
  98.1 7.4 %collective-permute-start.22 = (f32[192,128]{1,0:T(8,128)S(1)}, f32[192,128]{1,0:T(8,128)S(1)}, u32[]{:S(2)}, u32[]{:S(2)}) collective-permute-start(f32[192,128]{1,0:T(8,128)S(1)} %fusion.4), channel_id=1, source_target_pairs={{0,3},{1,0},{2,1},{3,2},{4,7},{5,4},{6,5},{7,6},{8,11},{9,8},{10,9... | collective-permute-start | bytes 294920 | tf_op jit(solution)/shard_map/ppermute | solution.py:35
  105.4 6.8 %collective-permute-start.27 = (f32[192,128]{1,0:T(8,128)S(1)}, f32[192,128]{1,0:T(8,128)S(1)}, u32[]{:S(2)}, u32[]{:S(2)}) collective-permute-start(f32[192,128]{1,0:T(8,128)S(1)} %add_add_fusion.1), channel_id=1, source_target_pairs={{0,8},{1,9},{2,10},{3,11},{4,12},{5,13},{6,14},{7,15},{8,0},{9,1},... | collective-permute-start | bytes 294920 | tf_op jit(solution)/shard_map/ppermute | solution.py:35
  105.5 7.4 %collective-permute-start.26 = (f32[192,128]{1,0:T(8,128)S(1)}, f32[192,128]{1,0:T(8,128)S(1)}, u32[]{:S(2)}, u32[]{:S(2)}) collective-permute-start(f32[192,128]{1,0:T(8,128)S(1)} %add_add_fusion.1), channel_id=1, source_target_pairs={{0,4},{1,5},{2,6},{3,7},{4,8},{5,9},{6,10},{7,11},{8,12},{9,13},{1... | collective-permute-start | bytes 294920 | tf_op jit(solution)/shard_map/ppermute | solution.py:35
  106.4 6.6 %collective-permute-start.25 = (f32[192,128]{1,0:T(8,128)S(1)}, f32[192,128]{1,0:T(8,128)S(1)}, u32[]{:S(2)}, u32[]{:S(2)}) collective-permute-start(f32[192,128]{1,0:T(8,128)S(1)} %add_add_fusion.1), channel_id=1, source_target_pairs={{0,12},{1,13},{2,14},{3,15},{4,0},{5,1},{6,2},{7,3},{8,4},{9,5},{1... | collective-permute-start | bytes 294920 | tf_op jit(solution)/shard_map/ppermute | solution.py:35
  113.0 6.9 %collective-permute-start.30 = (f32[192,128]{1,0:T(8,128)S(1)}, f32[192,128]{1,0:T(8,128)S(1)}, u32[]{:S(2)}, u32[]{:S(2)}) collective-permute-start(f32[192,128]{1,0:T(8,128)S(1)} %add_add_fusion), channel_id=1, source_target_pairs={{0,64},{16,80},{32,96},{48,112},{64,0},{80,16},{96,32},{112,48},{1... | collective-permute-start | bytes 294920 | tf_op jit(solution)/shard_map/ppermute | solution.py:40
  115.5 6.0 %collective-permute-start.29 = (f32[192,128]{1,0:T(8,128)S(1)}, f32[192,128]{1,0:T(8,128)S(1)}, u32[]{:S(2)}, u32[]{:S(2)}) collective-permute-start(f32[192,128]{1,0:T(8,128)S(1)} %add_add_fusion), channel_id=1, source_target_pairs={{0,32},{16,48},{32,64},{48,80},{64,96},{80,112},{96,0},{112,16},{1... | collective-permute-start | bytes 294920 | tf_op jit(solution)/shard_map/ppermute | solution.py:40
  163.5 7.9 %collective-permute-start.35 = (bf16[4,32,512]{2,1,0:T(8,128)(2,1)S(1)}, bf16[4,32,512]{2,1,0:T(8,128)(2,1)S(1)}, u32[]{:S(2)}, u32[]{:S(2)}) collective-permute-start(bf16[4,32,512]{2,1,0:T(8,128)(2,1)S(1)} %get-tuple-element.71), channel_id=1, source_target_pairs={{0,64},{16,80},{32,96},{48,112},{64,0},{80,16},{96,32},{112,48},{1... | collective-permute-start | bytes 393224 | tf_op jit(solution)/shard_map/ppermute | solution.py:40
  166.5 6.9 %collective-permute-start.34 = (bf16[4,32,512]{2,1,0:T(8,128)(2,1)S(1)}, bf16[4,32,512]{2,1,0:T(8,128)(2,1)S(1)}, u32[]{:S(2)}, u32[]{:S(2)}) collective-permute-start(bf16[4,32,512]{2,1,0:T(8,128)(2,1)S(1)} %get-tuple-element.72), channel_id=1, source_target_pairs={{0,96},{16,112},{32,0},{48,16},{64,32},{80,48},{96,64},{112,80},{1... | collective-permute-start | bytes 393224 | tf_op jit(solution)/shard_map/ppermute | solution.py:40
  167.7 6.4 %collective-permute-start.33 = (bf16[4,32,512]{2,1,0:T(8,128)(2,1)S(1)}, bf16[4,32,512]{2,1,0:T(8,128)(2,1)S(1)}, u32[]{:S(2)}, u32[]{:S(2)}) collective-permute-start(bf16[4,32,512]{2,1,0:T(8,128)(2,1)S(1)} %get-tuple-element.70), channel_id=1, source_target_pairs={{0,32},{16,48},{32,64},{48,80},{64,96},{80,112},{96,0},{112,16},{1... | collective-permute-start | bytes 393224 | tf_op jit(solution)/shard_map/ppermute | solution.py:40
  (12 other events, 48.1 us)
Sparse Core Ops, SparseCore 0:
  80.5 68.0 all-gather.1

commit v4 on v3

--- a/solution.py
+++ b/solution.py
@@ -96,13 +96,13 @@
     )(table, grads, grads, grads, grads, sketch)
 
 
-def combine_kernel(tab, g0, g1, g2, g3, sk, recv0, recv1, out0, out1):
+def combine_kernel(tab, g0, g1, g2, g3, sk, *rest):
     def run(recv, out):
         term = sketch_of((g0, g1, g2, g3), sk)
         out[0] = (term + recv[0].astype(F32)).astype(BF16)
 
-    pl.when(pl.program_id(0) == 0)(lambda: run(recv0, out0))
-    pl.when(pl.program_id(0) == 1)(lambda: run(recv1, out1))
+    for n, (recv, out) in enumerate(zip(rest[:MATS], rest[MATS:])):
+        pl.when(pl.program_id(0) == n)(lambda recv=recv, out=out: run(recv, out))
 
 
 def combined_chunks(grads, sketch, table, base, recvs):
@@ -111,23 +111,26 @@
         combine_kernel,
         grid_spec=pltpu.PrefetchScalarGridSpec(
             num_scalar_prefetch=1,
-            grid=(2,),
+            grid=(MATS,),
             in_specs=gradient_specs(base)
-            + [pl.BlockSpec((WIDTH, RANK), lambda n, t: (0, 0)), block, block],
-            out_specs=[block, block],
+            + [pl.BlockSpec((WIDTH, RANK), lambda n, t: (0, 0))]
+            + [block] * MATS,
+            out_specs=[block] * MATS,
         ),
-        out_shape=[jax.ShapeDtypeStruct((1, CHUNK, RANK), BF16)] * 2,
-        compiler_params=params(),
-        cost_estimate=cost(2 * CHUNK_FLOPS, 2 * CHUNK_BYTES),
+        out_shape=[jax.ShapeDtypeStruct((1, CHUNK, RANK), BF16)] * MATS,
+        compiler_params=params(),
+        cost_estimate=cost(4 * CHUNK_FLOPS, 4 * CHUNK_BYTES),
     )(table, grads, grads, grads, grads, sketch, *recvs)
 
 
-def near_kernel(tab, g0, g1, g2, g3, sk, near0, near1, out):
+def near_kernel(tab, g0, g1, g2, g3, sk, *rest):
+    out = rest[-1]
+
     def run(near):
         out[0] = sketch_of((g0, g1, g2, g3), sk) + near[0].astype(F32)
 
-    pl.when(pl.program_id(0) == 0)(lambda: run(near0))
-    pl.when(pl.program_id(0) == 1)(lambda: run(near1))
+    for n, near in enumerate(rest[:-1]):
+        pl.when(pl.program_id(0) == n)(lambda near=near: run(near))
 
 
 def own_and_near(grads, sketch, table, base, nears):
@@ -135,15 +138,15 @@
         near_kernel,
         grid_spec=pltpu.PrefetchScalarGridSpec(
             num_scalar_prefetch=1,
-            grid=(2,),
+            grid=(MATS,),
             in_specs=gradient_specs(base)
             + [pl.BlockSpec((WIDTH, RANK), lambda n, t: (0, 0))]
-            + [pl.BlockSpec(CHUNK_BLOCK, lambda n, t: (0, 0, 0))] * 2,
+            + [pl.BlockSpec(CHUNK_BLOCK, lambda n, t: (0, 0, 0))] * MATS,
             out_specs=pl.BlockSpec(CHUNK_BLOCK, lambda n, t: (n, 0, 0)),
         ),
-        out_shape=jax.ShapeDtypeStruct((2, CHUNK, RANK), F32),
-        compiler_params=params(),
-        cost_estimate=cost(2 * CHUNK_FLOPS, 2 * CHUNK_BYTES),
+        out_shape=jax.ShapeDtypeStruct((MATS, CHUNK, RANK), F32),
+        compiler_params=params(),
+        cost_estimate=cost(4 * CHUNK_FLOPS, 4 * CHUNK_BYTES),
     )(table, grads, grads, grads, grads, sketch, *nears)
 
 
@@ -157,12 +160,12 @@
     pl.when(pl.program_id(0) == 1)(lambda: run(comb1))
 
 
-def own_chunks(part, combs):
+def own_chunks(part, pair, combs):
     share = pl.BlockSpec((1, SHARE, RANK), lambda n: (n, 0, 0))
     return pl.pallas_call(
         own_kernel,
         grid=(2,),
-        in_specs=[pl.BlockSpec(CHUNK_BLOCK, lambda n: (n, 0, 0))]
+        in_specs=[pl.BlockSpec(CHUNK_BLOCK, lambda n: (2 * pair + n, 0, 0))]
         + [pl.BlockSpec(CHUNK_BLOCK, lambda n: (0, 0, 0))] * 2,
         out_specs=[share] * 4,
         out_shape=[jax.ShapeDtypeStruct((2, SHARE, RANK), F32)]
@@ -172,26 +175,29 @@
     )(part, *combs)
 
 
-def total_kernel(own, a, b, c, total, rounded):
+def total_kernel(own, a, b, c, *rest):
+    total, rounded = rest[-2:]
     value = own[0] + a[0].astype(F32) + b[0].astype(F32) + c[0].astype(F32)
     total[0] = value
     rounded[0] = value.astype(BF16)
 
 
-def totals(own, parts):
+def totals(pair, own, parts, done=()):
     share = pl.BlockSpec((1, SHARE, RANK), lambda n: (n, 0, 0))
+    placed = pl.BlockSpec((1, SHARE, RANK), lambda n: (2 * pair + n, 0, 0))
     return pl.pallas_call(
         total_kernel,
         grid=(2,),
-        in_specs=[share] * 4,
-        out_specs=[share, share],
+        in_specs=[share] * 4 + [pl.BlockSpec(memory_space=pl.ANY) for _ in done],
+        out_specs=[placed, placed],
         out_shape=[
-            jax.ShapeDtypeStruct((2, SHARE, RANK), F32),
-            jax.ShapeDtypeStruct((2, SHARE, RANK), BF16),
+            jax.ShapeDtypeStruct((MATS, SHARE, RANK), F32),
+            jax.ShapeDtypeStruct((MATS, SHARE, RANK), BF16),
         ],
+        input_output_aliases={4 + i: i for i in range(len(done))},
         compiler_params=params(),
         cost_estimate=cost(2 * SHARE * RANK, 2 * SHARE * RANK * 16),
-    )(own, *parts)
+    )(own, *parts, *done)
 
 
 TRI = 3
@@ -217,42 +223,79 @@
     )(total)
 
 
-def finish(ranks, inv, whole, rows, mine, theirs):
-    for b in range(8):
-        start = pl.multiple_of(ranks[b] * BLOCK, BLOCK)
-        rows[b * BLOCK : (b + 1) * BLOCK] = inv[0, pl.ds(start, BLOCK), :]
-    out = jnp.dot(rows[...], whole, precision=EXACT, preferred_element_type=F32)
-    mine[0] = out[:HALF]
-    theirs[0] = out[HALF:].astype(BF16)
-
-
-def project_kernel(ranks, s, g, inv, mine, theirs, rows):
-    whole = lax.dot_general(s[0], g[0], (((0,), (0,)), ((), ())), preferred_element_type=F32)
-    finish(ranks, inv, whole, rows, mine, theirs)
+def halves(v):
+    high = v.astype(BF16)
+    return high, (v - high.astype(F32)).astype(BF16)
+
+
+def product(u, v, last=False):
+    dims = (((1,), (1 if last else 0,)), ((), ()))
+    return lax.dot_general(u, v, dims, preferred_element_type=F32)
+
+
+def product3(u, v, last=False):
+    (a, b), (c, d) = halves(u), halves(v)
+    return product(a, c, last) + (product(a, d, last) + product(b, c, last))
+
+
+PARTS = 2
+
+
+def project_kernel(ranks, s_hbm, g_hbm, inv, mine, theirs, s, g, rows, s_sems, g_sems):
+    depth = s.shape[1] // PARTS
+    copies = {}
+    for m in range(MATS):
+        for k in range(PARTS):
+            piece = (m, pl.ds(k * depth, depth))
+            copies[m, k] = (
+                pltpu.make_async_copy(s_hbm.at[piece], s.at[piece], s_sems.at[m, k]),
+                pltpu.make_async_copy(g_hbm.at[piece], g.at[piece], g_sems.at[m, k]),
+            )
+            for copy in copies[m, k]:
+                copy.start()
+    for m in range(MATS):
+        whole = None
+        for k in range(PARTS):
+            for copy in copies[m, k]:
+                copy.wait()
+            piece = slice(k * depth, (k + 1) * depth)
+            term = lax.dot_general(
+                s[m, piece], g[m, piece], (((0,), (0,)), ((), ())), preferred_element_type=F32
+            )
+            whole = term if whole is None else whole + term
+        for b in range(8):
+            start = pl.multiple_of(ranks[b] * BLOCK, BLOCK)
+            rows[b * BLOCK : (b + 1) * BLOCK] = inv[m, pl.ds(start, BLOCK), :]
+        out = product3(rows[...], whole)
+        mine[m] = out[:HALF]
+        theirs[m] = out[HALF:].astype(BF16)
 
 
 def project(gradients, gathered, inverse, ranks):
     depth = gradients.shape[1]
-    half = pl.BlockSpec((1, HALF, WIDTH), lambda n, r: (n, 0, 0))
+    half = pl.BlockSpec((MATS, HALF, WIDTH), lambda n, r: (0, 0, 0))
+    kept = pl.BlockSpec(memory_space=pl.ANY)
     return pl.pallas_call(
         project_kernel,
         grid_spec=pltpu.PrefetchScalarGridSpec(
             num_scalar_prefetch=1,
-            grid=(MATS,),
-            in_specs=[
-                pl.BlockSpec((1, depth, RANK), lambda n, r: (n, 0, 0)),
-                pl.BlockSpec((1, depth, WIDTH), lambda n, r: (n, 0, 0)),
-                pl.BlockSpec((1, RANK, RANK), lambda n, r: (n, 0, 0)),
+            grid=(1,),
+            in_specs=[kept, kept, pl.BlockSpec((MATS, RANK, RANK), lambda n, r: (0, 0, 0))],
+            out_specs=[half, half],
+            scratch_shapes=[
+                pltpu.VMEM((MATS, depth, RANK), BF16),
+                pltpu.VMEM((MATS, depth, WIDTH), BF16),
+                pltpu.VMEM((RANK, RANK), F32),
+                pltpu.SemaphoreType.DMA((MATS, PARTS)),
+                pltpu.SemaphoreType.DMA((MATS, PARTS)),
             ],
-            out_specs=[half, half],
-            scratch_shapes=[pltpu.VMEM((RANK, RANK), F32)],
         ),
         out_shape=[
             jax.ShapeDtypeStruct((MATS, HALF, WIDTH), F32),
             jax.ShapeDtypeStruct((MATS, HALF, WIDTH), BF16),
         ],
         compiler_params=params(),
-        cost_estimate=cost(MATS * 2 * RANK * WIDTH * (depth + 6 * RANK), MATS * 2 * depth * (WIDTH + RANK)),
+        cost_estimate=cost(MATS * 2 * RANK * WIDTH * (depth + 3 * RANK), MATS * 2 * depth * (WIDTH + RANK)),
     )(ranks, gathered, gradients, inverse)
 
 
@@ -299,18 +342,6 @@
     def diagonal(a, axis):
         return jnp.sum(jnp.where(rows == cols, a, 0.0), axis=axis, keepdims=True)
 
-    def halves(v):
-        high = v.astype(BF16)
-        return high, (v - high.astype(F32)).astype(BF16)
-
-    def product(u, v, last=False):
-        dims = (((1,), (1 if last else 0,)), ((), ()))
-        return lax.dot_general(u, v, dims, preferred_element_type=F32)
-
-    def product3(u, v, last=False):
-        (a, b), (c, d) = halves(u), halves(v)
-        return product(a, c, last) + (product(a, d, last) + product(b, c, last))
-
     def rough(value, a):
         value = value.astype(BF16)
         return product(product(value, a.astype(BF16)).astype(BF16), value, True) - eye
@@ -467,23 +498,21 @@
     for (sign, p), value in zip(links, sent):
         near[p, sign] = shift(value, pairs[p][0], sign)
     table, *_ = lax.optimization_barrier((table, *sent))
-    for sign in (1, -1):
-        recvs = (hop1[0, sign], hop1[1, sign])
-        for p, value in enumerate(combined_chunks(grads, sketch, table, base["hop2", sign], recvs)):
-            hop2[p, sign] = shift(value, pairs[p][0], sign)
-    part = [
-        own_and_near(grads, sketch, table, base["own", p], (near[p, -1], near[p, 1])) for p in range(2)
-    ]
-    held = lax.optimization_barrier((*part, *hop2.values()))
-    part, hop2 = held[:2], dict(zip(hop2, held[2:]))
+    recvs = [hop1[p, sign] for sign, p in links]
+    for (sign, p), value in zip(links, combined_chunks(grads, sketch, table, base["hop2", 1], recvs)):
+        hop2[p, sign] = shift(value, pairs[p][0], sign)
+    nears = (near[0, -1], near[0, 1], near[1, -1], near[1, 1])
+    part = own_and_near(grads, sketch, table, base["own", 0], nears)
+    held = lax.optimization_barrier((part, *hop2.values()))
+    part, hop2 = held[0], dict(zip(hop2, held[1:]))
     owns, parts = [], []
     for p, (_, cross) in enumerate(pairs):
-        own, ahead, behind, across = own_chunks(part[p], (hop2[p, 1], hop2[p, -1]))
+        own, ahead, behind, across = own_chunks(part, p, (hop2[p, 1], hop2[p, -1]))
         owns.append(own)
         parts.append([shift(ahead, cross, 1), shift(behind, cross, -1), shift(across, cross, 2)])
-    total, rounded = zip(*(totals(own, arrived) for own, arrived in zip(owns, parts)))
-    gathered = lax.all_gather(jnp.concatenate(rounded, axis=0), "mat", axis=1, tiled=True)
-    total = jnp.concatenate(total, axis=0)
+    done = totals(0, owns[0], parts[0])
+    total, rounded = totals(1, owns[1], parts[1], done)
+    gathered = lax.all_gather(rounded, "mat", axis=1, tiled=True)
 
     where = jnp.stack([x, core]).astype(jnp.int32)
     inverse = inverse_factors(where, *summed_grams(gram_parts(total)))

time: 182 us -> 177 us (0.973)
  waiting for transfers between devices: 56.4 us -> 50.6 us
  local copies, waits for them, and re-layouts: 3.3 us -> 5.48 us
    ppermute x24, waiting for transfers between devices: 23.7 us -> 17.9 us  [shift(): return lax.ppermute(value, 'mat', pairs)]
    unnamed x15 -> x24, local copies, waits for them, and re-layouts: 2.81 us -> 5.03 us
    pallas_call x2 -> x1, Pallas kernels: 7.64 us -> 6.41 us  [own_and_near(): pl.pallas_call(near_kernel, grid_spec=pltpu.PrefetchScalarGridSpec(num_sc...]
    pallas_call x2 -> x1, Pallas kernels: 6.34 us -> 6.06 us  [combined_chunks(): pl.pallas_call(combine_kernel, grid_spec=pltpu.PrefetchScalarGridSpec(num...]
  transfers between devices with their start and end apart: 37 -> 37, of which waited for: 21 -> 23; matrix products, arithmetic and copies ran while one was open for 0% -> 0% of each run, Pallas kernels for 18% -> 18%
where the time goes in v4:
time: 177 us
  starting transfers between devices  53.7 us (30%)
  Pallas kernels  51.2 us (29%)
  waiting for transfers between devices  50.6 us (29%)
  between operations  14.5 us (8%)
  local copies, waits for them, and re-layouts  5.48 us (3%)
    ppermute x24, starting transfers between devices, shift(): return lax.ppermute(value, 'mat', pairs)  37.3 us
    ppermute x24, waiting for transfers between devices, shift(): return lax.ppermute(value, 'mat', pairs)  17.9 us
    all_gather x1, waiting for transfers between devices, local(): gathered = lax.all_gather(rounded, 'mat', axis=1, tiled=True)  17.1 us
    ppermute x12, starting transfers between devices, shift(): return lax.ppermute(value, 'row', pairs)  16.4 us
    ppermute x12, waiting for transfers between devices, shift(): return lax.ppermute(value, 'row', pairs)  15.5 us
    pallas_call x1, Pallas kernels, project(): pl.pallas_call(project_kernel, grid_spec=pltpu.PrefetchScalarGridSpec(num...  11 us
    pallas_call x2, Pallas kernels, sketch_chunks(): pl.pallas_call(sketch_kernel, grid_spec=pltpu.PrefetchScalarGridSpec(num_...  10.7 us
    pallas_call x1, Pallas kernels, inverse_factors(): pl.pallas_call(inverse_kernel, grid_spec=pltpu.PrefetchScalarGridSpec(num...  7.35 us
  transfers between devices with their start and end apart: 37, of which 23 were waited for; matrix products, arithmetic and copies ran while one was open for 0% of the time, Pallas kernels for 18%

profile of v4, /device:TPU:0, one launch (start us, length us, event | category | flops | bytes accessed | tf_op | source)
XLA Modules:
  0.0 176.7 jit_solution(4703900430682300415)
XLA Ops:
  8.6 5.4 %shard_map.41 = (bf16[1,896,256]{2,1,0:T(8,128)(2,1)S(1)}, bf16[1,896,256]{2,1,0:T(8,128)(2,1)S(1)}, bf16[1,896,256]{2,1,0:T(8,128)(2,1)S(1)}, bf16[1,896,256]{2,1,0:T(8,128)(2,1)}) custom-call(s32[16,5]{1,0:T(8,128)S(1)} %reshape.19.tab, bf16[4,16,224,512]{3,2,1,0:T(8,128)(2,1)} %bitcast.59, bf16[4,16,224,512]{3,2,1,0:T(8,128)(2,1)} %bitcast.60, ...), custom_call_target="tpu_custom_call" | custom-call | flops 939524096 | bytes 7340032 | tf_op jit(solution)/shard_map/pallas_call | solution.py:85
  15.6 1.9 %collective-permute-start.5 = (bf16[1,896,256]{2,1,0:T(8,128)(2,1)S(1)}, bf16[1,896,256]{2,1,0:T(8,128)(2,1)S(1)}, u32[]{:S(2)}, u32[]{:S(2)}) collective-permute-start(bf16[1,896,256]{2,1,0:T(8,128)(2,1)S(1)} %get-tuple-element.36), channel_id=1, source_target_pairs={{0,4},{1,5},{2,6},{3,7},{4,8},{5,9},{6,10},{7,11},{8,12},{9,13},{1... | collective-permute-start | bytes 1376264 | tf_op jit(solution)/shard_map/ppermute | solution.py:35
  17.5 1.7 collective-permute-start.6
  19.2 2.1 %collective-permute-start.7 = (bf16[1,896,256]{2,1,0:T(8,128)(2,1)}, bf16[1,896,256]{2,1,0:T(8,128)(2,1)S(1)}, u32[]{:S(2)}, u32[]{:S(2)}) collective-permute-start(bf16[1,896,256]{2,1,0:T(8,128)(2,1)} %get-tuple-element.38), channel_id=1, source_target_pairs={{0,12},{1,13},{2,14},{3,15},{4,0},{5,1},{6,2},{7,3},{8,4},{9,5},{1... | collective-permute-start | bytes 1376264 | tf_op jit(solution)/shard_map/ppermute | solution.py:35
  21.3 5.4 %shard_map.42 = (bf16[1,896,256]{2,1,0:T(8,128)(2,1)S(1)}, bf16[1,896,256]{2,1,0:T(8,128)(2,1)S(1)}, bf16[1,896,256]{2,1,0:T(8,128)(2,1)S(1)}, bf16[1,896,256]{2,1,0:T(8,128)(2,1)}) custom-call(s32[16,5]{1,0:T(8,128)S(1)} %reshape.19.tab, bf16[4,16,224,512]{3,2,1,0:T(8,128)(2,1)} %bitcast.63, bf16[4,16,224,512]{3,2,1,0:T(8,128)(2,1)} %bitcast.64, ...), custom_call_target="tpu_custom_call" | custom-call | flops 939524096 | bytes 7340032 | tf_op jit(solution)/shard_map/pallas_call | solution.py:85
  26.7 1.8 %collective-permute-start = (bf16[1,896,256]{2,1,0:T(8,128)(2,1)S(1)}, bf16[1,896,256]{2,1,0:T(8,128)(2,1)S(1)}, u32[]{:S(2)}, u32[]{:S(2)}) collective-permute-start(bf16[1,896,256]{2,1,0:T(8,128)(2,1)S(1)} %get-tuple-element.42), channel_id=1, source_target_pairs={{0,3},{1,0},{2,1},{3,2},{4,7},{5,4},{6,5},{7,6},{8,11},{9,8},{10,9... | collective-permute-start | bytes 1376264 | tf_op jit(solution)/shard_map/ppermute | solution.py:35
  29.9 2.0 %collective-permute-start.2 = (bf16[1,896,256]{2,1,0:T(8,128)(2,1)}, bf16[1,896,256]{2,1,0:T(8,128)(2,1)S(1)}, u32[]{:S(2)}, u32[]{:S(2)}) collective-permute-start(bf16[1,896,256]{2,1,0:T(8,128)(2,1)} %get-tuple-element.43), channel_id=1, source_target_pairs={{0,12},{1,13},{2,14},{3,15},{4,0},{5,1},{6,2},{7,3},{8,4},{9,5},{1... | collective-permute-start | bytes 1376264 | tf_op jit(solution)/shard_map/ppermute | solution.py:35
  33.7 6.1 %shard_map.44 = (bf16[1,896,256]{2,1,0:T(8,128)(2,1)S(1)}, bf16[1,896,256]{2,1,0:T(8,128)(2,1)S(1)}, bf16[1,896,256]{2,1,0:T(8,128)(2,1)S(1)}, bf16[1,896,256]{2,1,0:T(8,128)(2,1)}) custom-call(s32[16,5]{1,0:T(8,128)S(1)} %reshape.19.tab, bf16[4,16,224,512]{3,2,1,0:T(8,128)(2,1)} %bitcast.67, bf16[4,16,224,512]{3,2,1,0:T(8,128)(2,1)} %bitcast.68, ...), custom_call_target="tpu_custom_call" | custom-call | flops 939524096 | bytes 7340032 | tf_op jit(solution)/shard_map/pallas_call | solution.py:110
  47.0 6.4 %shard_map.43.part = f32[4,896,256]{2,1,0:T(8,128)} custom-call(s32[16,5]{1,0:T(8,128)S(1)} %reshape.19.tab, bf16[4,16,224,512]{3,2,1,0:T(8,128)(2,1)} %bitcast.71, bf16[4,16,224,512]{3,2,1,0:T(8,128)(2,1)} %bitcast.72, bf16[4,16,224,512]{3,2,1,0:T(8,128)(2,1)} %bitcast.73, bf16[4,16,224,512]{3,2,1,0:T(8,128)(2,1)} %bitcast.74, ...), custom_call_target="tpu_custom_call" | custom-call | flops 939524096 | bytes 7340032 | tf_op jit(solution)/shard_map/pallas_call | solution.py:137
  54.7 1.9 %shard_map.46 = (f32[2,224,256]{2,1,0:T(8,128)S(1)}, bf16[2,224,256]{2,1,0:T(8,128)(2,1)S(1)}, bf16[2,224,256]{2,1,0:T(8,128)(2,1)S(1)}, bf16[2,224,256]{2,1,0:T(8,128)(2,1)S(1)}) custom-call(f32[4,896,256]{2,1,0:T(8,128)} %shard_map.43.part, bf16[1,896,256]{2,1,0:T(8,128)(2,1)S(1)} %collective-permute-done.8.comb0, bf16[1,896,256]{2,1,0:T(8,128)(2,1)} %copy-done.6), custom_call_target="tpu_custom_call" | custom-call | flops 458752 | bytes 3670016 | tf_op jit(solution)/shard_map/pallas_call | solution.py:165
  58.0 1.7 shard_map.45
  59.9 3.2 %collective-permute-start.16 = (bf16[2,224,256]{2,1,0:T(8,128)(2,1)S(1)}, bf16[2,224,256]{2,1,0:T(8,128)(2,1)S(1)}, u32[]{:S(2)}, u32[]{:S(2)}) collective-permute-start(bf16[2,224,256]{2,1,0:T(8,128)(2,1)S(1)} %get-tuple-element.60), channel_id=1, source_target_pairs={{0,12},{1,13},{2,14},{3,15},{4,0},{5,1},{6,2},{7,3},{8,4},{9,5},{1... | collective-permute-start | bytes 688136 | tf_op jit(solution)/shard_map/ppermute | solution.py:35
  63.2 2.8 %collective-permute-start.13 = (bf16[2,224,256]{2,1,0:T(8,128)(2,1)S(1)}, bf16[2,224,256]{2,1,0:T(8,128)(2,1)S(1)}, u32[]{:S(2)}, u32[]{:S(2)}) collective-permute-start(bf16[2,224,256]{2,1,0:T(8,128)(2,1)S(1)} %get-tuple-element.54), channel_id=1, source_target_pairs={{0,3},{1,0},{2,1},{3,2},{4,7},{5,4},{6,5},{7,6},{8,11},{9,8},{10,9... | collective-permute-start | bytes 688136 | tf_op jit(solution)/shard_map/ppermute | solution.py:35
  66.6 4.0 %collective-permute-done.16.b = bf16[2,224,256]{2,1,0:T(8,128)(2,1)S(1)} collective-permute-done((bf16[2,224,256]{2,1,0:T(8,128)(2,1)S(1)}, bf16[2,224,256]{2,1,0:T(8,128)(2,1)S(1)}, u32[]{:S(2)}, u32[]{:S(2)}) %collective-permute-start.16) | collective-permute-done | bytes 229408 | tf_op jit(solution)/shard_map/ppermute | solution.py:35
  75.7 1.8 %shard_map.49 = f32[4,3,128,128]{3,2,1,0:T(8,128)S(1)} custom-call(f32[4,224,256]{2,1,0:T(8,128)S(1)} %copy-done.3), custom_call_target="tpu_custom_call" | custom-call | flops 704643072 | bytes 917504 | tf_op jit(solution)/shard_map/pallas_call | solution.py:215
  79.4 3.1 %collective-permute-start.21 = (f32[192,128]{1,0:T(8,128)S(1)}, f32[192,128]{1,0:T(8,128)S(1)}, u32[]{:S(2)}, u32[]{:S(2)}) collective-permute-start(f32[192,128]{1,0:T(8,128)S(1)} %get-tuple-element.72), channel_id=1, source_target_pairs={{0,64},{16,80},{32,96},{48,112},{64,0},{80,16},{96,32},{112,48},{1... | collective-permute-start | bytes 294920 | tf_op jit(solution)/shard_map/ppermute | solution.py:40
  86.0 2.0 %collective-permute-done.20 = f32[192,128]{1,0:T(8,128)S(1)} collective-permute-done((f32[192,128]{1,0:T(8,128)S(1)}, f32[192,128]{1,0:T(8,128)S(1)}, u32[]{:S(2)}, u32[]{:S(2)}) %collective-permute-start.20) | collective-permute-done | bytes 98336 | tf_op jit(solution)/shard_map/ppermute | solution.py:40
  90.5 2.7 %collective-permute-start.23 = (f32[192,128]{1,0:T(8,128)S(1)}, f32[192,128]{1,0:T(8,128)S(1)}, u32[]{:S(2)}, u32[]{:S(2)}) collective-permute-start(f32[192,128]{1,0:T(8,128)S(1)} %fusion.4), channel_id=1, source_target_pairs={{0,1},{1,2},{2,3},{3,0},{4,5},{5,6},{6,7},{7,4},{8,9},{9,10},{10,1... | collective-permute-start | bytes 294920 | tf_op jit(solution)/shard_map/ppermute | solution.py:35
  93.7 4.0 %collective-permute-done.24 = f32[192,128]{1,0:T(8,128)S(1)} collective-permute-done((f32[192,128]{1,0:T(8,128)S(1)}, f32[192,128]{1,0:T(8,128)S(1)}, u32[]{:S(2)}, u32[]{:S(2)}) %collective-permute-start.24) | collective-permute-done | bytes 98336 | tf_op jit(solution)/shard_map/ppermute | solution.py:35
  100.9 2.6 %collective-permute-start.27 = (f32[192,128]{1,0:T(8,128)S(1)}, f32[192,128]{1,0:T(8,128)S(1)}, u32[]{:S(2)}, u32[]{:S(2)}) collective-permute-start(f32[192,128]{1,0:T(8,128)S(1)} %add_add_fusion.1), channel_id=1, source_target_pairs={{0,8},{1,9},{2,10},{3,11},{4,12},{5,13},{6,14},{7,15},{8,0},{9,1},... | collective-permute-start | bytes 294920 | tf_op jit(solution)/shard_map/ppermute | solution.py:35
  103.8 3.0 %collective-permute-start.25 = (f32[192,128]{1,0:T(8,128)S(1)}, f32[192,128]{1,0:T(8,128)S(1)}, u32[]{:S(2)}, u32[]{:S(2)}) collective-permute-start(f32[192,128]{1,0:T(8,128)S(1)} %add_add_fusion.1), channel_id=1, source_target_pairs={{0,12},{1,13},{2,14},{3,15},{4,0},{5,1},{6,2},{7,3},{8,4},{9,5},{1... | collective-permute-start | bytes 294920 | tf_op jit(solution)/shard_map/ppermute | solution.py:35
  107.3 2.1 %collective-permute-done.26 = f32[192,128]{1,0:T(8,128)S(1)} collective-permute-done((f32[192,128]{1,0:T(8,128)S(1)}, f32[192,128]{1,0:T(8,128)S(1)}, u32[]{:S(2)}, u32[]{:S(2)}) %collective-permute-start.26) | collective-permute-done | bytes 98336 | tf_op jit(solution)/shard_map/ppermute | solution.py:35
  109.4 2.7 %collective-permute-start.30 = (f32[192,128]{1,0:T(8,128)S(1)}, f32[192,128]{1,0:T(8,128)S(1)}, u32[]{:S(2)}, u32[]{:S(2)}) collective-permute-start(f32[192,128]{1,0:T(8,128)S(1)} %add_add_fusion), channel_id=1, source_target_pairs={{0,64},{16,80},{32,96},{48,112},{64,0},{80,16},{96,32},{112,48},{1... | collective-permute-start | bytes 294920 | tf_op jit(solution)/shard_map/ppermute | solution.py:40
  112.8 2.5 %collective-permute-start.28 = (f32[192,128]{1,0:T(8,128)S(1)}, f32[192,128]{1,0:T(8,128)S(1)}, u32[]{:S(2)}, u32[]{:S(2)}) collective-permute-start(f32[192,128]{1,0:T(8,128)S(1)} %add_add_fusion), channel_id=1, source_target_pairs={{0,96},{16,112},{32,0},{48,16},{64,32},{80,48},{96,64},{112,80},{1... | collective-permute-start | bytes 294920 | tf_op jit(solution)/shard_map/ppermute | solution.py:40
  116.0 1.9 %collective-permute-done.29 = f32[192,128]{1,0:T(8,128)S(1)} collective-permute-done((f32[192,128]{1,0:T(8,128)S(1)}, f32[192,128]{1,0:T(8,128)S(1)}, u32[]{:S(2)}, u32[]{:S(2)}) %collective-permute-start.29) | collective-permute-done | bytes 98336 | tf_op jit(solution)/shard_map/ppermute | solution.py:40
  119.7 7.4 %shard_map.50.inv = f32[4,256,256]{2,1,0:T(8,128)S(1)} custom-call(s32[2]{0:T(128)S(1)} %pad_add_fusion.where, f32[4,192,128]{2,1,0:T(8,128)S(1)} %pad_maximum_fusion.own, f32[4,192,128]{2,1,0:T(8,128)S(1)} %collective-permute-done.31.other), custom_call_target="tpu_custom_call" | custom-call | flops 8000000000 | bytes 4194304 | tf_op jit(solution)/shard_map/pallas_call | solution.py:414
  128.1 17.1 %all-gather.2.cloned.1.call-done.s_hbm = bf16[4,3584,256]{2,1,0:T(8,128)(2,1)} async-done(((bf16[4,224,256]{2,1,0:T(8,128)(2,1)}), bf16[4,3584,256]{2,1,0:T(8,128)(2,1)}) %all-gather.2.cloned.1.call-update) | async-done | bytes 7340048 | tf_op jit(solution)/shard_map/all_gather | solution.py:515
  145.3 11.0 %shard_map.52 = (f32[4,128,512]{2,1,0:T(8,128)S(1)}, bf16[4,128,512]{2,1,0:T(8,128)(2,1)S(1)}) custom-call(s32[8]{0:T(128)S(1)} %stack.183.ranks, bf16[4,3584,256]{2,1,0:T(8,128)(2,1)} %all-gather.2.cloned.1.call-done.s_hbm, bf16[4,3584,512]{2,1,0:T(8,128)(2,1)} %g_hbm.1, f32[4,256,256]{2,1,0:T(8,128)} %copy-done.1), custom_call_target="tpu_custom_call" | custom-call | flops 4563402752 | bytes 22020096 | tf_op jit(solution)/shard_map/pallas_call | solution.py:278
  156.3 1.9 %collective-permute-done.32 = bf16[4,128,512]{2,1,0:T(8,128)(2,1)S(1)} collective-permute-done((bf16[4,128,512]{2,1,0:T(8,128)(2,1)S(1)}, bf16[4,128,512]{2,1,0:T(8,128)(2,1)S(1)}, u32[]{:S(2)}, u32[]{:S(2)}) %collective-permute-start.32) | collective-permute-done | bytes 524320 | tf_op jit(solution)/shard_map/ppermute | solution.py:40
  158.5 3.1 %collective-permute-start.35 = (bf16[4,32,512]{2,1,0:T(8,128)(2,1)S(1)}, bf16[4,32,512]{2,1,0:T(8,128)(2,1)S(1)}, u32[]{:S(2)}, u32[]{:S(2)}) collective-permute-start(bf16[4,32,512]{2,1,0:T(8,128)(2,1)S(1)} %get-tuple-element.69), channel_id=1, source_target_pairs={{0,64},{16,80},{32,96},{48,112},{64,0},{80,16},{96,32},{112,48},{1... | collective-permute-start | bytes 393224 | tf_op jit(solution)/shard_map/ppermute | solution.py:40
  163.6 2.5 %shard_map.51 = bf16[4,224,256]{2,1,0:T(8,128)(2,1)} custom-call(f32[4,224,256]{2,1,0:T(8,128)S(1)} %copy-done.4, f32[4,256,256]{2,1,0:T(8,128)S(1)} %copy-done.2), custom_call_target="tpu_custom_call" | custom-call | flops 704643072 | bytes 2293760 | tf_op jit(solution)/shard_map/pallas_call | solution.py:311
  166.4 2.0 %collective-permute-done.34 = bf16[4,32,512]{2,1,0:T(8,128)(2,1)S(1)} collective-permute-done((bf16[4,32,512]{2,1,0:T(8,128)(2,1)S(1)}, bf16[4,32,512]{2,1,0:T(8,128)(2,1)S(1)}, u32[]{:S(2)}, u32[]{:S(2)}) %collective-permute-start.34) | collective-permute-done | bytes 131104 | tf_op jit(solution)/shard_map/ppermute | solution.py:40
  (93 shorter events, 42.6 us)
Async XLA Ops:
  7.2 138.1 %all-gather.2.cloned.1.call-start = ((), (), s32[]{:S(2)}) async-start(), calls=%async_computation | async-start | bytes 7798784 | tf_op jit(solution)/shard_map/all_gather | solution.py:515
  14.0 14.5 %collective-permute-start.4 = (bf16[1,896,256]{2,1,0:T(8,128)(2,1)S(1)}, bf16[1,896,256]{2,1,0:T(8,128)(2,1)S(1)}, u32[]{:S(2)}, u32[]{:S(2)}) collective-permute-start(bf16[1,896,256]{2,1,0:T(8,128)(2,1)S(1)} %get-tuple-element.35), channel_id=1, source_target_pairs={{0,1},{1,2},{2,3},{3,0},{4,5},{5,6},{6,7},{7,4},{8,9},{9,10},{10,1... | collective-permute-start | bytes 1376264 | tf_op jit(solution)/shard_map/ppermute | solution.py:35
  15.6 14.3 %collective-permute-start.5 = (bf16[1,896,256]{2,1,0:T(8,128)(2,1)S(1)}, bf16[1,896,256]{2,1,0:T(8,128)(2,1)S(1)}, u32[]{:S(2)}, u32[]{:S(2)}) collective-permute-start(bf16[1,896,256]{2,1,0:T(8,128)(2,1)S(1)} %get-tuple-element.36), channel_id=1, source_target_pairs={{0,4},{1,5},{2,6},{3,7},{4,8},{5,9},{6,10},{7,11},{8,12},{9,13},{1... | collective-permute-start | bytes 1376264 | tf_op jit(solution)/shard_map/ppermute | solution.py:35
  17.5 14.4 %collective-permute-start.6 = (bf16[1,896,256]{2,1,0:T(8,128)(2,1)S(1)}, bf16[1,896,256]{2,1,0:T(8,128)(2,1)S(1)}, u32[]{:S(2)}, u32[]{:S(2)}) collective-permute-start(bf16[1,896,256]{2,1,0:T(8,128)(2,1)S(1)} %get-tuple-element.37), channel_id=1, source_target_pairs={{0,3},{1,0},{2,1},{3,2},{4,7},{5,4},{6,5},{7,6},{8,11},{9,8},{10,9... | collective-permute-start | bytes 1376264 | tf_op jit(solution)/shard_map/ppermute | solution.py:35
  19.2 13.7 %collective-permute-start.7 = (bf16[1,896,256]{2,1,0:T(8,128)(2,1)}, bf16[1,896,256]{2,1,0:T(8,128)(2,1)S(1)}, u32[]{:S(2)}, u32[]{:S(2)}) collective-permute-start(bf16[1,896,256]{2,1,0:T(8,128)(2,1)} %get-tuple-element.38), channel_id=1, source_target_pairs={{0,12},{1,13},{2,14},{3,15},{4,0},{5,1},{6,2},{7,3},{8,4},{9,5},{1... | collective-permute-start | bytes 1376264 | tf_op jit(solution)/shard_map/ppermute | solution.py:35
  26.7 14.7 %collective-permute-start = (bf16[1,896,256]{2,1,0:T(8,128)(2,1)S(1)}, bf16[1,896,256]{2,1,0:T(8,128)(2,1)S(1)}, u32[]{:S(2)}, u32[]{:S(2)}) collective-permute-start(bf16[1,896,256]{2,1,0:T(8,128)(2,1)S(1)} %get-tuple-element.42), channel_id=1, source_target_pairs={{0,3},{1,0},{2,1},{3,2},{4,7},{5,4},{6,5},{7,6},{8,11},{9,8},{10,9... | collective-permute-start | bytes 1376264 | tf_op jit(solution)/shard_map/ppermute | solution.py:35
  28.5 14.5 %collective-permute-start.1 = (bf16[1,896,256]{2,1,0:T(8,128)(2,1)S(1)}, bf16[1,896,256]{2,1,0:T(8,128)(2,1)S(1)}, u32[]{:S(2)}, u32[]{:S(2)}) collective-permute-start(bf16[1,896,256]{2,1,0:T(8,128)(2,1)S(1)} %get-tuple-element.40), channel_id=1, source_target_pairs={{0,1},{1,2},{2,3},{3,0},{4,5},{5,6},{6,7},{7,4},{8,9},{9,10},{10,1... | collective-permute-start | bytes 1376264 | tf_op jit(solution)/shard_map/ppermute | solution.py:35
  29.9 14.8 %collective-permute-start.2 = (bf16[1,896,256]{2,1,0:T(8,128)(2,1)}, bf16[1,896,256]{2,1,0:T(8,128)(2,1)S(1)}, u32[]{:S(2)}, u32[]{:S(2)}) collective-permute-start(bf16[1,896,256]{2,1,0:T(8,128)(2,1)} %get-tuple-element.43), channel_id=1, source_target_pairs={{0,12},{1,13},{2,14},{3,15},{4,0},{5,1},{6,2},{7,3},{8,4},{9,5},{1... | collective-permute-start | bytes 1376264 | tf_op jit(solution)/shard_map/ppermute | solution.py:35
  31.9 14.3 %collective-permute-start.3 = (bf16[1,896,256]{2,1,0:T(8,128)(2,1)S(1)}, bf16[1,896,256]{2,1,0:T(8,128)(2,1)S(1)}, u32[]{:S(2)}, u32[]{:S(2)}) collective-permute-start(bf16[1,896,256]{2,1,0:T(8,128)(2,1)S(1)} %get-tuple-element.41), channel_id=1, source_target_pairs={{0,4},{1,5},{2,6},{3,7},{4,8},{5,9},{6,10},{7,11},{8,12},{9,13},{1... | collective-permute-start | bytes 1376264 | tf_op jit(solution)/shard_map/ppermute | solution.py:35
  39.8 13.7 %collective-permute-start.8 = (bf16[1,896,256]{2,1,0:T(8,128)(2,1)S(1)}, bf16[1,896,256]{2,1,0:T(8,128)(2,1)S(1)}, u32[]{:S(2)}, u32[]{:S(2)}) collective-permute-start(bf16[1,896,256]{2,1,0:T(8,128)(2,1)S(1)} %get-tuple-element.45), channel_id=1, source_target_pairs={{0,1},{1,2},{2,3},{3,0},{4,5},{5,6},{6,7},{7,4},{8,9},{9,10},{10,1... | collective-permute-start | bytes 1376264 | tf_op jit(solution)/shard_map/ppermute | solution.py:35
  41.4 12.6 %collective-permute-start.9 = (bf16[1,896,256]{2,1,0:T(8,128)(2,1)S(1)}, bf16[1,896,256]{2,1,0:T(8,128)(2,1)S(1)}, u32[]{:S(2)}, u32[]{:S(2)}) collective-permute-start(bf16[1,896,256]{2,1,0:T(8,128)(2,1)S(1)} %get-tuple-element.46), channel_id=1, source_target_pairs={{0,4},{1,5},{2,6},{3,7},{4,8},{5,9},{6,10},{7,11},{8,12},{9,13},{1... | collective-permute-start | bytes 1376264 | tf_op jit(solution)/shard_map/ppermute | solution.py:35
  43.0 10.9 %collective-permute-start.10 = (bf16[1,896,256]{2,1,0:T(8,128)(2,1)S(1)}, bf16[1,896,256]{2,1,0:T(8,128)(2,1)S(1)}, u32[]{:S(2)}, u32[]{:S(2)}) collective-permute-start(bf16[1,896,256]{2,1,0:T(8,128)(2,1)S(1)} %get-tuple-element.47), channel_id=1, source_target_pairs={{0,3},{1,0},{2,1},{3,2},{4,7},{5,4},{6,5},{7,6},{8,11},{9,8},{10,9... | collective-permute-start | bytes 1376264 | tf_op jit(solution)/shard_map/ppermute | solution.py:35
  44.6 9.8 %collective-permute-start.11 = (bf16[1,896,256]{2,1,0:T(8,128)(2,1)}, bf16[1,896,256]{2,1,0:T(8,128)(2,1)S(1)}, u32[]{:S(2)}, u32[]{:S(2)}) collective-permute-start(bf16[1,896,256]{2,1,0:T(8,128)(2,1)} %get-tuple-element.48), channel_id=1, source_target_pairs={{0,12},{1,13},{2,14},{3,15},{4,0},{5,1},{6,2},{7,3},{8,4},{9,5},{1... | collective-permute-start | bytes 1376264 | tf_op jit(solution)/shard_map/ppermute | solution.py:35
  56.6 9.5 %collective-permute-start.15 = (bf16[2,224,256]{2,1,0:T(8,128)(2,1)S(1)}, bf16[2,224,256]{2,1,0:T(8,128)(2,1)S(1)}, u32[]{:S(2)}, u32[]{:S(2)}) collective-permute-start(bf16[2,224,256]{2,1,0:T(8,128)(2,1)S(1)} %get-tuple-element.59), channel_id=1, source_target_pairs={{0,4},{1,5},{2,6},{3,7},{4,8},{5,9},{6,10},{7,11},{8,12},{9,13},{1... | collective-permute-start | bytes 688136 | tf_op jit(solution)/shard_map/ppermute | solution.py:35
  59.7 11.9 %collective-permute-start.12 = (bf16[2,224,256]{2,1,0:T(8,128)(2,1)S(1)}, bf16[2,224,256]{2,1,0:T(8,128)(2,1)S(1)}, u32[]{:S(2)}, u32[]{:S(2)}) collective-permute-start(bf16[2,224,256]{2,1,0:T(8,128)(2,1)S(1)} %get-tuple-element.53), channel_id=1, source_target_pairs={{0,1},{1,2},{2,3},{3,0},{4,5},{5,6},{6,7},{7,4},{8,9},{9,10},{10,1... | collective-permute-start | bytes 688136 | tf_op jit(solution)/shard_map/ppermute | solution.py:35
  59.9 10.8 %collective-permute-start.16 = (bf16[2,224,256]{2,1,0:T(8,128)(2,1)S(1)}, bf16[2,224,256]{2,1,0:T(8,128)(2,1)S(1)}, u32[]{:S(2)}, u32[]{:S(2)}) collective-permute-start(bf16[2,224,256]{2,1,0:T(8,128)(2,1)S(1)} %get-tuple-element.60), channel_id=1, source_target_pairs={{0,12},{1,13},{2,14},{3,15},{4,0},{5,1},{6,2},{7,3},{8,4},{9,5},{1... | collective-permute-start | bytes 688136 | tf_op jit(solution)/shard_map/ppermute | solution.py:35
  63.1 7.6 %collective-permute-start.17 = (bf16[2,224,256]{2,1,0:T(8,128)(2,1)S(1)}, bf16[2,224,256]{2,1,0:T(8,128)(2,1)S(1)}, u32[]{:S(2)}, u32[]{:S(2)}) collective-permute-start(bf16[2,224,256]{2,1,0:T(8,128)(2,1)S(1)} %get-tuple-element.61), channel_id=1, source_target_pairs={{0,8},{1,9},{2,10},{3,11},{4,12},{5,13},{6,14},{7,15},{8,0},{9,1},... | collective-permute-start | bytes 688136 | tf_op jit(solution)/shard_map/ppermute | solution.py:35
  63.2 9.4 %collective-permute-start.13 = (bf16[2,224,256]{2,1,0:T(8,128)(2,1)S(1)}, bf16[2,224,256]{2,1,0:T(8,128)(2,1)S(1)}, u32[]{:S(2)}, u32[]{:S(2)}) collective-permute-start(bf16[2,224,256]{2,1,0:T(8,128)(2,1)S(1)} %get-tuple-element.54), channel_id=1, source_target_pairs={{0,3},{1,0},{2,1},{3,2},{4,7},{5,4},{6,5},{7,6},{8,11},{9,8},{10,9... | collective-permute-start | bytes 688136 | tf_op jit(solution)/shard_map/ppermute | solution.py:35
  66.0 7.5 %collective-permute-start.14 = (bf16[2,224,256]{2,1,0:T(8,128)(2,1)S(1)}, bf16[2,224,256]{2,1,0:T(8,128)(2,1)S(1)}, u32[]{:S(2)}, u32[]{:S(2)}) collective-permute-start(bf16[2,224,256]{2,1,0:T(8,128)(2,1)S(1)} %get-tuple-element.55), channel_id=1, source_target_pairs={{0,2},{1,3},{2,0},{3,1},{4,6},{5,7},{6,4},{7,5},{8,10},{9,11},{10,... | collective-permute-start | bytes 688136 | tf_op jit(solution)/shard_map/ppermute | solution.py:35
  79.4 6.6 %collective-permute-start.21 = (f32[192,128]{1,0:T(8,128)S(1)}, f32[192,128]{1,0:T(8,128)S(1)}, u32[]{:S(2)}, u32[]{:S(2)}) collective-permute-start(f32[192,128]{1,0:T(8,128)S(1)} %get-tuple-element.72), channel_id=1, source_target_pairs={{0,64},{16,80},{32,96},{48,112},{64,0},{80,16},{96,32},{112,48},{1... | collective-permute-start | bytes 294920 | tf_op jit(solution)/shard_map/ppermute | solution.py:40
  83.6 5.8 %collective-permute-start.19 = (f32[192,128]{1,0:T(8,128)S(1)}, f32[192,128]{1,0:T(8,128)S(1)}, u32[]{:S(2)}, u32[]{:S(2)}) collective-permute-start(f32[192,128]{1,0:T(8,128)S(1)} %get-tuple-element.71), channel_id=1, source_target_pairs={{0,32},{16,48},{32,64},{48,80},{64,96},{80,112},{96,0},{112,16},{1... | collective-permute-start | bytes 294920 | tf_op jit(solution)/shard_map/ppermute | solution.py:40
  89.5 8.3 %collective-permute-start.24 = (f32[192,128]{1,0:T(8,128)S(1)}, f32[192,128]{1,0:T(8,128)S(1)}, u32[]{:S(2)}, u32[]{:S(2)}) collective-permute-start(f32[192,128]{1,0:T(8,128)S(1)} %fusion.4), channel_id=1, source_target_pairs={{0,2},{1,3},{2,0},{3,1},{4,6},{5,7},{6,4},{7,5},{8,10},{9,11},{10,... | collective-permute-start | bytes 294920 | tf_op jit(solution)/shard_map/ppermute | solution.py:35
  90.5 8.9 %collective-permute-start.23 = (f32[192,128]{1,0:T(8,128)S(1)}, f32[192,128]{1,0:T(8,128)S(1)}, u32[]{:S(2)}, u32[]{:S(2)}) collective-permute-start(f32[192,128]{1,0:T(8,128)S(1)} %fusion.4), channel_id=1, source_target_pairs={{0,1},{1,2},{2,3},{3,0},{4,5},{5,6},{6,7},{7,4},{8,9},{9,10},{10,1... | collective-permute-start | bytes 294920 | tf_op jit(solution)/shard_map/ppermute | solution.py:35
  93.1 7.8 %collective-permute-start.22 = (f32[192,128]{1,0:T(8,128)S(1)}, f32[192,128]{1,0:T(8,128)S(1)}, u32[]{:S(2)}, u32[]{:S(2)}) collective-permute-start(f32[192,128]{1,0:T(8,128)S(1)} %fusion.4), channel_id=1, source_target_pairs={{0,3},{1,0},{2,1},{3,2},{4,7},{5,4},{6,5},{7,6},{8,11},{9,8},{10,9... | collective-permute-start | bytes 294920 | tf_op jit(solution)/shard_map/ppermute | solution.py:35
  100.9 6.3 %collective-permute-start.27 = (f32[192,128]{1,0:T(8,128)S(1)}, f32[192,128]{1,0:T(8,128)S(1)}, u32[]{:S(2)}, u32[]{:S(2)}) collective-permute-start(f32[192,128]{1,0:T(8,128)S(1)} %add_add_fusion.1), channel_id=1, source_target_pairs={{0,8},{1,9},{2,10},{3,11},{4,12},{5,13},{6,14},{7,15},{8,0},{9,1},... | collective-permute-start | bytes 294920 | tf_op jit(solution)/shard_map/ppermute | solution.py:35
  103.5 5.8 %collective-permute-start.26 = (f32[192,128]{1,0:T(8,128)S(1)}, f32[192,128]{1,0:T(8,128)S(1)}, u32[]{:S(2)}, u32[]{:S(2)}) collective-permute-start(f32[192,128]{1,0:T(8,128)S(1)} %add_add_fusion.1), channel_id=1, source_target_pairs={{0,4},{1,5},{2,6},{3,7},{4,8},{5,9},{6,10},{7,11},{8,12},{9,13},{1... | collective-permute-start | bytes 294920 | tf_op jit(solution)/shard_map/ppermute | solution.py:35
  103.8 5.6 %collective-permute-start.25 = (f32[192,128]{1,0:T(8,128)S(1)}, f32[192,128]{1,0:T(8,128)S(1)}, u32[]{:S(2)}, u32[]{:S(2)}) collective-permute-start(f32[192,128]{1,0:T(8,128)S(1)} %add_add_fusion.1), channel_id=1, source_target_pairs={{0,12},{1,13},{2,14},{3,15},{4,0},{5,1},{6,2},{7,3},{8,4},{9,5},{1... | collective-permute-start | bytes 294920 | tf_op jit(solution)/shard_map/ppermute | solution.py:35
  109.4 6.6 %collective-permute-start.30 = (f32[192,128]{1,0:T(8,128)S(1)}, f32[192,128]{1,0:T(8,128)S(1)}, u32[]{:S(2)}, u32[]{:S(2)}) collective-permute-start(f32[192,128]{1,0:T(8,128)S(1)} %add_add_fusion), channel_id=1, source_target_pairs={{0,64},{16,80},{32,96},{48,112},{64,0},{80,16},{96,32},{112,48},{1... | collective-permute-start | bytes 294920 | tf_op jit(solution)/shard_map/ppermute | solution.py:40
  112.0 5.8 %collective-permute-start.29 = (f32[192,128]{1,0:T(8,128)S(1)}, f32[192,128]{1,0:T(8,128)S(1)}, u32[]{:S(2)}, u32[]{:S(2)}) collective-permute-start(f32[192,128]{1,0:T(8,128)S(1)} %add_add_fusion), channel_id=1, source_target_pairs={{0,32},{16,48},{32,64},{48,80},{64,96},{80,112},{96,0},{112,16},{1... | collective-permute-start | bytes 294920 | tf_op jit(solution)/shard_map/ppermute | solution.py:40
  158.5 7.9 %collective-permute-start.35 = (bf16[4,32,512]{2,1,0:T(8,128)(2,1)S(1)}, bf16[4,32,512]{2,1,0:T(8,128)(2,1)S(1)}, u32[]{:S(2)}, u32[]{:S(2)}) collective-permute-start(bf16[4,32,512]{2,1,0:T(8,128)(2,1)S(1)} %get-tuple-element.69), channel_id=1, source_target_pairs={{0,64},{16,80},{32,96},{48,112},{64,0},{80,16},{96,32},{112,48},{1... | collective-permute-start | bytes 393224 | tf_op jit(solution)/shard_map/ppermute | solution.py:40
  161.5 6.9 %collective-permute-start.34 = (bf16[4,32,512]{2,1,0:T(8,128)(2,1)S(1)}, bf16[4,32,512]{2,1,0:T(8,128)(2,1)S(1)}, u32[]{:S(2)}, u32[]{:S(2)}) collective-permute-start(bf16[4,32,512]{2,1,0:T(8,128)(2,1)S(1)} %get-tuple-element.70), channel_id=1, source_target_pairs={{0,96},{16,112},{32,0},{48,16},{64,32},{80,48},{96,64},{112,80},{1... | collective-permute-start | bytes 393224 | tf_op jit(solution)/shard_map/ppermute | solution.py:40
  162.7 6.3 %collective-permute-start.33 = (bf16[4,32,512]{2,1,0:T(8,128)(2,1)S(1)}, bf16[4,32,512]{2,1,0:T(8,128)(2,1)S(1)}, u32[]{:S(2)}, u32[]{:S(2)}) collective-permute-start(bf16[4,32,512]{2,1,0:T(8,128)(2,1)S(1)} %get-tuple-element.68), channel_id=1, source_target_pairs={{0,32},{16,48},{32,64},{48,80},{64,96},{80,112},{96,0},{112,16},{1... | collective-permute-start | bytes 393224 | tf_op jit(solution)/shard_map/ppermute | solution.py:40
  (17 other events, 87.2 us)
Sparse Core Ops, SparseCore 0:
  74.6 70.6 all-gather.1

commit v5 on v4

--- a/solution.py
+++ b/solution.py
@@ -434,30 +434,29 @@
     return [shift(value, axis, -1), shift(value, axis, 1), shift(value, axis, 2)]
 
 
-def x_pieces(whole):
-    x = place()[0]
+def quarter(whole, axis):
+    here = dict(zip(("x", "core", "y", "z"), place()))[axis]
 
     def piece(off):
-        return lax.dynamic_index_in_dim(whole, (x + off) % RING, 0, keepdims=False)
-
-    def sent(off, step):
-        return piece(off), "x", step
-
-    return piece, [sent(1, 1), sent(3, -1), sent(2, 2)]
+        return lax.dynamic_index_in_dim(whole, (here + off) % RING, 0, keepdims=False)
+
+    part = piece(0)
+    for off, step in ((1, 1), (3, -1), (2, 2)):
+        part = part + shift(piece(off), axis, step)
+    return part
 
 
 def summed_grams(grams):
-    core = place()[1]
+    _, core, y, _ = place()
     send = lax.dynamic_slice_in_dim(grams, 2 * (1 - core), 2, 0)
     keep = lax.dynamic_slice_in_dim(grams, 2 * core, 2, 0)
     whole = (keep + shift(send, "core", 1)).reshape(RING, 2 * TRI * HALF // RING, HALF)
-    piece, outgoing = x_pieces(whole)
-    part = piece(0)
-    for arrived in [shift(*args) for args in outgoing]:
-        part = part + arrived
-    for axis in ("y", "z"):
-        for arrived in from_others(part, axis):
-            part = part + arrived
+    part = quarter(whole, "x")
+    small = quarter(part.reshape(RING, part.shape[0] // RING, HALF), "y")
+    for arrived in from_others(small, "z"):
+        small = small + arrived
+    after, before, opposite = from_others(small, "y")
+    part = jnp.roll(jnp.stack([small, after, opposite, before]), y, axis=0).reshape(part.shape)
     own = jnp.stack([part] + from_others(part, "x"))
     return own, shift(own, "core", 1)
 

time: 177 us -> 174 us (0.983)
  waiting for transfers between devices: 50.6 us -> 46.8 us
    all_gather x1, waiting for transfers between devices: 17.1 us -> 10.9 us  [local(): gathered = lax.all_gather(rounded, 'mat', axis=1, tiled=True)]
    ppermute x24 -> x27, starting transfers between devices: 37.3 us -> 40.1 us  [shift(): return lax.ppermute(value, 'mat', pairs)]
    ppermute x24 -> x27, waiting for transfers between devices: 17.9 us -> 20 us  [shift(): return lax.ppermute(value, 'mat', pairs)]
    ppermute x12, starting transfers between devices: 16.4 us -> 14.5 us  [shift(): return lax.ppermute(value, 'row', pairs)]
    unnamed x24 -> x30, local copies, waits for them, and re-layouts: 5.03 us -> 5.04 us
  transfers between devices with their start and end apart: 37 -> 40, of which waited for: 23 -> 25; matrix products, arithmetic and copies ran while one was open for 0% -> 0% of each run, Pallas kernels for 18% -> 18%
where the time goes in v5:
time: 174 us
  starting transfers between devices  54.7 us (31%)
  Pallas kernels  51.3 us (29%)
  waiting for transfers between devices  46.8 us (27%)
  between operations  14.6 us (8%)
  local copies, waits for them, and re-layouts  5.53 us (3%)
    ppermute x27, starting transfers between devices, shift(): return lax.ppermute(value, 'mat', pairs)  40.1 us
    ppermute x27, waiting for transfers between devices, shift(): return lax.ppermute(value, 'mat', pairs)  20 us
    ppermute x12, waiting for transfers between devices, shift(): return lax.ppermute(value, 'row', pairs)  16 us
    ppermute x12, starting transfers between devices, shift(): return lax.ppermute(value, 'row', pairs)  14.5 us
    pallas_call x1, Pallas kernels, project(): pl.pallas_call(project_kernel, grid_spec=pltpu.PrefetchScalarGridSpec(num...  11 us
    all_gather x1, waiting for transfers between devices, local(): gathered = lax.all_gather(rounded, 'mat', axis=1, tiled=True)  10.9 us
    pallas_call x2, Pallas kernels, sketch_chunks(): pl.pallas_call(sketch_kernel, grid_spec=pltpu.PrefetchScalarGridSpec(num_...  10.7 us
    pallas_call x1, Pallas kernels, inverse_factors(): pl.pallas_call(inverse_kernel, grid_spec=pltpu.PrefetchScalarGridSpec(num...  7.35 us
  transfers between devices with their start and end apart: 40, of which 25 were waited for; matrix products, arithmetic and copies ran while one was open for 0% of the time, Pallas kernels for 18%

profile of v5, /device:TPU:0, one launch (start us, length us, event | category | flops | bytes accessed | tf_op | source)
XLA Modules:
  0.0 174.0 jit_solution(10402617108382708863)
XLA Ops:
  8.6 5.4 %shard_map.41 = (bf16[1,896,256]{2,1,0:T(8,128)(2,1)S(1)}, bf16[1,896,256]{2,1,0:T(8,128)(2,1)S(1)}, bf16[1,896,256]{2,1,0:T(8,128)(2,1)S(1)}, bf16[1,896,256]{2,1,0:T(8,128)(2,1)}) custom-call(s32[16,5]{1,0:T(8,128)S(1)} %reshape.25.tab, bf16[4,16,224,512]{3,2,1,0:T(8,128)(2,1)} %bitcast.85, bf16[4,16,224,512]{3,2,1,0:T(8,128)(2,1)} %bitcast.86, ...), custom_call_target="tpu_custom_call" | custom-call | flops 939524096 | bytes 7340032 | tf_op jit(solution)/shard_map/pallas_call | solution.py:85
  14.0 1.7 collective-permute-start.4
  15.6 1.9 %collective-permute-start.5 = (bf16[1,896,256]{2,1,0:T(8,128)(2,1)S(1)}, bf16[1,896,256]{2,1,0:T(8,128)(2,1)S(1)}, u32[]{:S(2)}, u32[]{:S(2)}) collective-permute-start(bf16[1,896,256]{2,1,0:T(8,128)(2,1)S(1)} %get-tuple-element.36), channel_id=1, source_target_pairs={{0,4},{1,5},{2,6},{3,7},{4,8},{5,9},{6,10},{7,11},{8,12},{9,13},{1... | collective-permute-start | bytes 1376264 | tf_op jit(solution)/shard_map/ppermute | solution.py:35
  19.2 2.1 %collective-permute-start.7 = (bf16[1,896,256]{2,1,0:T(8,128)(2,1)}, bf16[1,896,256]{2,1,0:T(8,128)(2,1)S(1)}, u32[]{:S(2)}, u32[]{:S(2)}) collective-permute-start(bf16[1,896,256]{2,1,0:T(8,128)(2,1)} %get-tuple-element.38), channel_id=1, source_target_pairs={{0,12},{1,13},{2,14},{3,15},{4,0},{5,1},{6,2},{7,3},{8,4},{9,5},{1... | collective-permute-start | bytes 1376264 | tf_op jit(solution)/shard_map/ppermute | solution.py:35
  21.3 5.4 %shard_map.42 = (bf16[1,896,256]{2,1,0:T(8,128)(2,1)S(1)}, bf16[1,896,256]{2,1,0:T(8,128)(2,1)S(1)}, bf16[1,896,256]{2,1,0:T(8,128)(2,1)S(1)}, bf16[1,896,256]{2,1,0:T(8,128)(2,1)}) custom-call(s32[16,5]{1,0:T(8,128)S(1)} %reshape.25.tab, bf16[4,16,224,512]{3,2,1,0:T(8,128)(2,1)} %bitcast.89, bf16[4,16,224,512]{3,2,1,0:T(8,128)(2,1)} %bitcast.90, ...), custom_call_target="tpu_custom_call" | custom-call | flops 939524096 | bytes 7340032 | tf_op jit(solution)/shard_map/pallas_call | solution.py:85
  26.7 1.8 %collective-permute-start = (bf16[1,896,256]{2,1,0:T(8,128)(2,1)S(1)}, bf16[1,896,256]{2,1,0:T(8,128)(2,1)S(1)}, u32[]{:S(2)}, u32[]{:S(2)}) collective-permute-start(bf16[1,896,256]{2,1,0:T(8,128)(2,1)S(1)} %get-tuple-element.42), channel_id=1, source_target_pairs={{0,3},{1,0},{2,1},{3,2},{4,7},{5,4},{6,5},{7,6},{8,11},{9,8},{10,9... | collective-permute-start | bytes 1376264 | tf_op jit(solution)/shard_map/ppermute | solution.py:35
  29.9 2.0 %collective-permute-start.2 = (bf16[1,896,256]{2,1,0:T(8,128)(2,1)}, bf16[1,896,256]{2,1,0:T(8,128)(2,1)S(1)}, u32[]{:S(2)}, u32[]{:S(2)}) collective-permute-start(bf16[1,896,256]{2,1,0:T(8,128)(2,1)} %get-tuple-element.43), channel_id=1, source_target_pairs={{0,12},{1,13},{2,14},{3,15},{4,0},{5,1},{6,2},{7,3},{8,4},{9,5},{1... | collective-permute-start | bytes 1376264 | tf_op jit(solution)/shard_map/ppermute | solution.py:35
  33.7 6.1 %shard_map.44 = (bf16[1,896,256]{2,1,0:T(8,128)(2,1)S(1)}, bf16[1,896,256]{2,1,0:T(8,128)(2,1)S(1)}, bf16[1,896,256]{2,1,0:T(8,128)(2,1)S(1)}, bf16[1,896,256]{2,1,0:T(8,128)(2,1)}) custom-call(s32[16,5]{1,0:T(8,128)S(1)} %reshape.25.tab, bf16[4,16,224,512]{3,2,1,0:T(8,128)(2,1)} %bitcast.93, bf16[4,16,224,512]{3,2,1,0:T(8,128)(2,1)} %bitcast.94, ...), custom_call_target="tpu_custom_call" | custom-call | flops 939524096 | bytes 7340032 | tf_op jit(solution)/shard_map/pallas_call | solution.py:110
  47.0 6.4 %shard_map.43.part = f32[4,896,256]{2,1,0:T(8,128)} custom-call(s32[16,5]{1,0:T(8,128)S(1)} %reshape.25.tab, bf16[4,16,224,512]{3,2,1,0:T(8,128)(2,1)} %bitcast.97, bf16[4,16,224,512]{3,2,1,0:T(8,128)(2,1)} %bitcast.98, bf16[4,16,224,512]{3,2,1,0:T(8,128)(2,1)} %bitcast.99, bf16[4,16,224,512]{3,2,1,0:T(8,128)(2,1)} %bitcast.100, ...), custom_call_target="tpu_custom_call" | custom-call | flops 939524096 | bytes 7340032 | tf_op jit(solution)/shard_map/pallas_call | solution.py:137
  54.7 1.9 %shard_map.46 = (f32[2,224,256]{2,1,0:T(8,128)S(1)}, bf16[2,224,256]{2,1,0:T(8,128)(2,1)S(1)}, bf16[2,224,256]{2,1,0:T(8,128)(2,1)S(1)}, bf16[2,224,256]{2,1,0:T(8,128)(2,1)S(1)}) custom-call(f32[4,896,256]{2,1,0:T(8,128)} %shard_map.43.part, bf16[1,896,256]{2,1,0:T(8,128)(2,1)S(1)} %collective-permute-done.8.comb0, bf16[1,896,256]{2,1,0:T(8,128)(2,1)} %copy-done.6), custom_call_target="tpu_custom_call" | custom-call | flops 458752 | bytes 3670016 | tf_op jit(solution)/shard_map/pallas_call | solution.py:165
  58.0 1.7 shard_map.45
  59.9 3.2 %collective-permute-start.16 = (bf16[2,224,256]{2,1,0:T(8,128)(2,1)S(1)}, bf16[2,224,256]{2,1,0:T(8,128)(2,1)S(1)}, u32[]{:S(2)}, u32[]{:S(2)}) collective-permute-start(bf16[2,224,256]{2,1,0:T(8,128)(2,1)S(1)} %get-tuple-element.60), channel_id=1, source_target_pairs={{0,12},{1,13},{2,14},{3,15},{4,0},{5,1},{6,2},{7,3},{8,4},{9,5},{1... | collective-permute-start | bytes 688136 | tf_op jit(solution)/shard_map/ppermute | solution.py:35
  63.1 2.8 %collective-permute-start.13 = (bf16[2,224,256]{2,1,0:T(8,128)(2,1)S(1)}, bf16[2,224,256]{2,1,0:T(8,128)(2,1)S(1)}, u32[]{:S(2)}, u32[]{:S(2)}) collective-permute-start(bf16[2,224,256]{2,1,0:T(8,128)(2,1)S(1)} %get-tuple-element.54), channel_id=1, source_target_pairs={{0,3},{1,0},{2,1},{3,2},{4,7},{5,4},{6,5},{7,6},{8,11},{9,8},{10,9... | collective-permute-start | bytes 688136 | tf_op jit(solution)/shard_map/ppermute | solution.py:35
  66.6 4.0 %collective-permute-done.16.b = bf16[2,224,256]{2,1,0:T(8,128)(2,1)S(1)} collective-permute-done((bf16[2,224,256]{2,1,0:T(8,128)(2,1)S(1)}, bf16[2,224,256]{2,1,0:T(8,128)(2,1)S(1)}, u32[]{:S(2)}, u32[]{:S(2)}) %collective-permute-start.16) | collective-permute-done | bytes 229408 | tf_op jit(solution)/shard_map/ppermute | solution.py:35
  75.6 1.8 %shard_map.49 = f32[4,3,128,128]{3,2,1,0:T(8,128)S(1)} custom-call(f32[4,224,256]{2,1,0:T(8,128)S(1)} %copy-done.3), custom_call_target="tpu_custom_call" | custom-call | flops 704643072 | bytes 917504 | tf_op jit(solution)/shard_map/pallas_call | solution.py:215
  79.4 3.1 %collective-permute-start.21 = (f32[192,128]{1,0:T(8,128)S(1)}, f32[192,128]{1,0:T(8,128)S(1)}, u32[]{:S(2)}, u32[]{:S(2)}) collective-permute-start(f32[192,128]{1,0:T(8,128)S(1)} %get-tuple-element.74), channel_id=1, source_target_pairs={{0,64},{16,80},{32,96},{48,112},{64,0},{80,16},{96,32},{112,48},{1... | collective-permute-start | bytes 294920 | tf_op jit(solution)/shard_map/ppermute | solution.py:40
  86.0 2.0 %collective-permute-done.20 = f32[192,128]{1,0:T(8,128)S(1)} collective-permute-done((f32[192,128]{1,0:T(8,128)S(1)}, f32[192,128]{1,0:T(8,128)S(1)}, u32[]{:S(2)}, u32[]{:S(2)}) %collective-permute-start.20) | collective-permute-done | bytes 98336 | tf_op jit(solution)/shard_map/ppermute | solution.py:40
  90.5 3.3 %collective-permute-start.23 = (f32[48,128]{1,0:T(8,128)S(1)}, f32[48,128]{1,0:T(8,128)S(1)}, u32[]{:S(2)}, u32[]{:S(2)}) collective-permute-start(f32[48,128]{1,0:T(8,128)S(1)} %get-tuple-element.78), channel_id=1, source_target_pairs={{0,3},{1,0},{2,1},{3,2},{4,7},{5,4},{6,5},{7,6},{8,11},{9,8},{10,9... | collective-permute-start | bytes 73736 | tf_op jit(solution)/shard_map/ppermute | solution.py:35
  96.0 3.0 %collective-permute-done.22 = f32[48,128]{1,0:T(8,128)S(1)} collective-permute-done((f32[48,128]{1,0:T(8,128)S(1)}, f32[48,128]{1,0:T(8,128)S(1)}, u32[]{:S(2)}, u32[]{:S(2)}) %collective-permute-start.22) | collective-permute-done | bytes 24608 | tf_op jit(solution)/shard_map/ppermute | solution.py:35
  99.1 3.3 %collective-permute-start.27 = (f32[48,128]{1,0:T(8,128)S(1)}, f32[48,128]{1,0:T(8,128)S(1)}, u32[]{:S(2)}, u32[]{:S(2)}) collective-permute-start(f32[48,128]{1,0:T(8,128)S(1)} %fusion.6), channel_id=1, source_target_pairs={{0,8},{1,9},{2,10},{3,11},{4,12},{5,13},{6,14},{7,15},{8,0},{9,1},... | collective-permute-start | bytes 73736 | tf_op jit(solution)/shard_map/ppermute | solution.py:35
  102.3 3.2 %collective-permute-start.25 = (f32[48,128]{1,0:T(8,128)S(1)}, f32[48,128]{1,0:T(8,128)S(1)}, u32[]{:S(2)}, u32[]{:S(2)}) collective-permute-start(f32[48,128]{1,0:T(8,128)S(1)} %fusion.6), channel_id=1, source_target_pairs={{0,12},{1,13},{2,14},{3,15},{4,0},{5,1},{6,2},{7,3},{8,4},{9,5},{1... | collective-permute-start | bytes 73736 | tf_op jit(solution)/shard_map/ppermute | solution.py:35
  105.6 1.8 %collective-permute-done.26 = f32[48,128]{1,0:T(8,128)S(1)} collective-permute-done((f32[48,128]{1,0:T(8,128)S(1)}, f32[48,128]{1,0:T(8,128)S(1)}, u32[]{:S(2)}, u32[]{:S(2)}) %collective-permute-start.26) | collective-permute-done | bytes 24608 | tf_op jit(solution)/shard_map/ppermute | solution.py:35
  109.5 2.2 %collective-permute-done.28 = f32[48,128]{1,0:T(8,128)S(1)} collective-permute-done((f32[48,128]{1,0:T(8,128)S(1)}, f32[48,128]{1,0:T(8,128)S(1)}, u32[]{:S(2)}, u32[]{:S(2)}) %collective-permute-start.28) | collective-permute-done | bytes 24608 | tf_op jit(solution)/shard_map/ppermute | solution.py:35
  116.1 2.6 %collective-permute-start.31 = (f32[192,128]{1,0:T(8,128)S(1)}, f32[192,128]{1,0:T(8,128)S(1)}, u32[]{:S(2)}, u32[]{:S(2)}) collective-permute-start(f32[192,128]{1,0:T(8,128)S(1)} %bitcast.107), channel_id=1, source_target_pairs={{0,96},{16,112},{32,0},{48,16},{64,32},{80,48},{96,64},{112,80},{1... | collective-permute-start | bytes 294920 | tf_op jit(solution)/shard_map/ppermute | solution.py:40
  118.7 1.9 %collective-permute-done.33 = f32[192,128]{1,0:T(8,128)S(1)} collective-permute-done((f32[192,128]{1,0:T(8,128)S(1)}, f32[192,128]{1,0:T(8,128)S(1)}, u32[]{:S(2)}, u32[]{:S(2)}) %collective-permute-start.33) | collective-permute-done | bytes 98336 | tf_op jit(solution)/shard_map/ppermute | solution.py:40
  123.5 7.3 %shard_map.50.inv = f32[4,256,256]{2,1,0:T(8,128)S(1)} custom-call(s32[2]{0:T(128)S(1)} %pad_add_fusion.where, f32[4,192,128]{2,1,0:T(8,128)S(1)} %pad_maximum_fusion.own, f32[4,192,128]{2,1,0:T(8,128)S(1)} %collective-permute-done.34.other), custom_call_target="tpu_custom_call" | custom-call | flops 8000000000 | bytes 4194304 | tf_op jit(solution)/shard_map/pallas_call | solution.py:414
  131.9 10.9 %all-gather.2.cloned.1.call-done.s_hbm = bf16[4,3584,256]{2,1,0:T(8,128)(2,1)} async-done(((bf16[4,224,256]{2,1,0:T(8,128)(2,1)}), bf16[4,3584,256]{2,1,0:T(8,128)(2,1)}) %all-gather.2.cloned.1.call-update) | async-done | bytes 7340048 | tf_op jit(solution)/shard_map/all_gather | solution.py:514
  142.7 11.0 %shard_map.52 = (f32[4,128,512]{2,1,0:T(8,128)S(1)}, bf16[4,128,512]{2,1,0:T(8,128)(2,1)S(1)}) custom-call(s32[8]{0:T(128)S(1)} %stack.196.ranks, bf16[4,3584,256]{2,1,0:T(8,128)(2,1)} %all-gather.2.cloned.1.call-done.s_hbm, bf16[4,3584,512]{2,1,0:T(8,128)(2,1)} %g_hbm.1, f32[4,256,256]{2,1,0:T(8,128)} %copy-done.1), custom_call_target="tpu_custom_call" | custom-call | flops 4563402752 | bytes 22020096 | tf_op jit(solution)/shard_map/pallas_call | solution.py:278
  153.8 1.9 %collective-permute-done.35 = bf16[4,128,512]{2,1,0:T(8,128)(2,1)S(1)} collective-permute-done((bf16[4,128,512]{2,1,0:T(8,128)(2,1)S(1)}, bf16[4,128,512]{2,1,0:T(8,128)(2,1)S(1)}, u32[]{:S(2)}, u32[]{:S(2)}) %collective-permute-start.35) | collective-permute-done | bytes 524320 | tf_op jit(solution)/shard_map/ppermute | solution.py:40
  155.9 2.7 %collective-permute-start.38 = (bf16[4,32,512]{2,1,0:T(8,128)(2,1)S(1)}, bf16[4,32,512]{2,1,0:T(8,128)(2,1)S(1)}, u32[]{:S(2)}, u32[]{:S(2)}) collective-permute-start(bf16[4,32,512]{2,1,0:T(8,128)(2,1)S(1)} %get-tuple-element.71), channel_id=1, source_target_pairs={{0,64},{16,80},{32,96},{48,112},{64,0},{80,16},{96,32},{112,48},{1... | collective-permute-start | bytes 393224 | tf_op jit(solution)/shard_map/ppermute | solution.py:40
  160.7 2.5 %shard_map.51 = bf16[4,224,256]{2,1,0:T(8,128)(2,1)} custom-call(f32[4,224,256]{2,1,0:T(8,128)S(1)} %copy-done.4, f32[4,256,256]{2,1,0:T(8,128)S(1)} %copy-done.2), custom_call_target="tpu_custom_call" | custom-call | flops 704643072 | bytes 2293760 | tf_op jit(solution)/shard_map/pallas_call | solution.py:311
  163.9 1.7 collective-permute-done.37
  (108 shorter events, 46.7 us)
Async XLA Ops:
  7.2 135.6 %all-gather.2.cloned.1.call-start = ((), (), s32[]{:S(2)}) async-start(), calls=%async_computation | async-start | bytes 7798784 | tf_op jit(solution)/shard_map/all_gather | solution.py:514
  14.0 14.5 %collective-permute-start.4 = (bf16[1,896,256]{2,1,0:T(8,128)(2,1)S(1)}, bf16[1,896,256]{2,1,0:T(8,128)(2,1)S(1)}, u32[]{:S(2)}, u32[]{:S(2)}) collective-permute-start(bf16[1,896,256]{2,1,0:T(8,128)(2,1)S(1)} %get-tuple-element.35), channel_id=1, source_target_pairs={{0,1},{1,2},{2,3},{3,0},{4,5},{5,6},{6,7},{7,4},{8,9},{9,10},{10,1... | collective-permute-start | bytes 1376264 | tf_op jit(solution)/shard_map/ppermute | solution.py:35
  15.6 14.3 %collective-permute-start.5 = (bf16[1,896,256]{2,1,0:T(8,128)(2,1)S(1)}, bf16[1,896,256]{2,1,0:T(8,128)(2,1)S(1)}, u32[]{:S(2)}, u32[]{:S(2)}) collective-permute-start(bf16[1,896,256]{2,1,0:T(8,128)(2,1)S(1)} %get-tuple-element.36), channel_id=1, source_target_pairs={{0,4},{1,5},{2,6},{3,7},{4,8},{5,9},{6,10},{7,11},{8,12},{9,13},{1... | collective-permute-start | bytes 1376264 | tf_op jit(solution)/shard_map/ppermute | solution.py:35
  17.5 14.4 %collective-permute-start.6 = (bf16[1,896,256]{2,1,0:T(8,128)(2,1)S(1)}, bf16[1,896,256]{2,1,0:T(8,128)(2,1)S(1)}, u32[]{:S(2)}, u32[]{:S(2)}) collective-permute-start(bf16[1,896,256]{2,1,0:T(8,128)(2,1)S(1)} %get-tuple-element.37), channel_id=1, source_target_pairs={{0,3},{1,0},{2,1},{3,2},{4,7},{5,4},{6,5},{7,6},{8,11},{9,8},{10,9... | collective-permute-start | bytes 1376264 | tf_op jit(solution)/shard_map/ppermute | solution.py:35
  19.2 13.7 %collective-permute-start.7 = (bf16[1,896,256]{2,1,0:T(8,128)(2,1)}, bf16[1,896,256]{2,1,0:T(8,128)(2,1)S(1)}, u32[]{:S(2)}, u32[]{:S(2)}) collective-permute-start(bf16[1,896,256]{2,1,0:T(8,128)(2,1)} %get-tuple-element.38), channel_id=1, source_target_pairs={{0,12},{1,13},{2,14},{3,15},{4,0},{5,1},{6,2},{7,3},{8,4},{9,5},{1... | collective-permute-start | bytes 1376264 | tf_op jit(solution)/shard_map/ppermute | solution.py:35
  26.7 14.7 %collective-permute-start = (bf16[1,896,256]{2,1,0:T(8,128)(2,1)S(1)}, bf16[1,896,256]{2,1,0:T(8,128)(2,1)S(1)}, u32[]{:S(2)}, u32[]{:S(2)}) collective-permute-start(bf16[1,896,256]{2,1,0:T(8,128)(2,1)S(1)} %get-tuple-element.42), channel_id=1, source_target_pairs={{0,3},{1,0},{2,1},{3,2},{4,7},{5,4},{6,5},{7,6},{8,11},{9,8},{10,9... | collective-permute-start | bytes 1376264 | tf_op jit(solution)/shard_map/ppermute | solution.py:35
  28.5 14.5 %collective-permute-start.1 = (bf16[1,896,256]{2,1,0:T(8,128)(2,1)S(1)}, bf16[1,896,256]{2,1,0:T(8,128)(2,1)S(1)}, u32[]{:S(2)}, u32[]{:S(2)}) collective-permute-start(bf16[1,896,256]{2,1,0:T(8,128)(2,1)S(1)} %get-tuple-element.40), channel_id=1, source_target_pairs={{0,1},{1,2},{2,3},{3,0},{4,5},{5,6},{6,7},{7,4},{8,9},{9,10},{10,1... | collective-permute-start | bytes 1376264 | tf_op jit(solution)/shard_map/ppermute | solution.py:35
  29.9 14.7 %collective-permute-start.2 = (bf16[1,896,256]{2,1,0:T(8,128)(2,1)}, bf16[1,896,256]{2,1,0:T(8,128)(2,1)S(1)}, u32[]{:S(2)}, u32[]{:S(2)}) collective-permute-start(bf16[1,896,256]{2,1,0:T(8,128)(2,1)} %get-tuple-element.43), channel_id=1, source_target_pairs={{0,12},{1,13},{2,14},{3,15},{4,0},{5,1},{6,2},{7,3},{8,4},{9,5},{1... | collective-permute-start | bytes 1376264 | tf_op jit(solution)/shard_map/ppermute | solution.py:35
  31.9 14.3 %collective-permute-start.3 = (bf16[1,896,256]{2,1,0:T(8,128)(2,1)S(1)}, bf16[1,896,256]{2,1,0:T(8,128)(2,1)S(1)}, u32[]{:S(2)}, u32[]{:S(2)}) collective-permute-start(bf16[1,896,256]{2,1,0:T(8,128)(2,1)S(1)} %get-tuple-element.41), channel_id=1, source_target_pairs={{0,4},{1,5},{2,6},{3,7},{4,8},{5,9},{6,10},{7,11},{8,12},{9,13},{1... | collective-permute-start | bytes 1376264 | tf_op jit(solution)/shard_map/ppermute | solution.py:35
  39.8 13.7 %collective-permute-start.8 = (bf16[1,896,256]{2,1,0:T(8,128)(2,1)S(1)}, bf16[1,896,256]{2,1,0:T(8,128)(2,1)S(1)}, u32[]{:S(2)}, u32[]{:S(2)}) collective-permute-start(bf16[1,896,256]{2,1,0:T(8,128)(2,1)S(1)} %get-tuple-element.45), channel_id=1, source_target_pairs={{0,1},{1,2},{2,3},{3,0},{4,5},{5,6},{6,7},{7,4},{8,9},{9,10},{10,1... | collective-permute-start | bytes 1376264 | tf_op jit(solution)/shard_map/ppermute | solution.py:35
  41.4 12.5 %collective-permute-start.9 = (bf16[1,896,256]{2,1,0:T(8,128)(2,1)S(1)}, bf16[1,896,256]{2,1,0:T(8,128)(2,1)S(1)}, u32[]{:S(2)}, u32[]{:S(2)}) collective-permute-start(bf16[1,896,256]{2,1,0:T(8,128)(2,1)S(1)} %get-tuple-element.46), channel_id=1, source_target_pairs={{0,4},{1,5},{2,6},{3,7},{4,8},{5,9},{6,10},{7,11},{8,12},{9,13},{1... | collective-permute-start | bytes 1376264 | tf_op jit(solution)/shard_map/ppermute | solution.py:35
  43.0 10.9 %collective-permute-start.10 = (bf16[1,896,256]{2,1,0:T(8,128)(2,1)S(1)}, bf16[1,896,256]{2,1,0:T(8,128)(2,1)S(1)}, u32[]{:S(2)}, u32[]{:S(2)}) collective-permute-start(bf16[1,896,256]{2,1,0:T(8,128)(2,1)S(1)} %get-tuple-element.47), channel_id=1, source_target_pairs={{0,3},{1,0},{2,1},{3,2},{4,7},{5,4},{6,5},{7,6},{8,11},{9,8},{10,9... | collective-permute-start | bytes 1376264 | tf_op jit(solution)/shard_map/ppermute | solution.py:35
  44.6 9.8 %collective-permute-start.11 = (bf16[1,896,256]{2,1,0:T(8,128)(2,1)}, bf16[1,896,256]{2,1,0:T(8,128)(2,1)S(1)}, u32[]{:S(2)}, u32[]{:S(2)}) collective-permute-start(bf16[1,896,256]{2,1,0:T(8,128)(2,1)} %get-tuple-element.48), channel_id=1, source_target_pairs={{0,12},{1,13},{2,14},{3,15},{4,0},{5,1},{6,2},{7,3},{8,4},{9,5},{1... | collective-permute-start | bytes 1376264 | tf_op jit(solution)/shard_map/ppermute | solution.py:35
  56.6 9.4 %collective-permute-start.15 = (bf16[2,224,256]{2,1,0:T(8,128)(2,1)S(1)}, bf16[2,224,256]{2,1,0:T(8,128)(2,1)S(1)}, u32[]{:S(2)}, u32[]{:S(2)}) collective-permute-start(bf16[2,224,256]{2,1,0:T(8,128)(2,1)S(1)} %get-tuple-element.59), channel_id=1, source_target_pairs={{0,4},{1,5},{2,6},{3,7},{4,8},{5,9},{6,10},{7,11},{8,12},{9,13},{1... | collective-permute-start | bytes 688136 | tf_op jit(solution)/shard_map/ppermute | solution.py:35
  59.7 11.9 %collective-permute-start.12 = (bf16[2,224,256]{2,1,0:T(8,128)(2,1)S(1)}, bf16[2,224,256]{2,1,0:T(8,128)(2,1)S(1)}, u32[]{:S(2)}, u32[]{:S(2)}) collective-permute-start(bf16[2,224,256]{2,1,0:T(8,128)(2,1)S(1)} %get-tuple-element.53), channel_id=1, source_target_pairs={{0,1},{1,2},{2,3},{3,0},{4,5},{5,6},{6,7},{7,4},{8,9},{9,10},{10,1... | collective-permute-start | bytes 688136 | tf_op jit(solution)/shard_map/ppermute | solution.py:35
  59.9 10.7 %collective-permute-start.16 = (bf16[2,224,256]{2,1,0:T(8,128)(2,1)S(1)}, bf16[2,224,256]{2,1,0:T(8,128)(2,1)S(1)}, u32[]{:S(2)}, u32[]{:S(2)}) collective-permute-start(bf16[2,224,256]{2,1,0:T(8,128)(2,1)S(1)} %get-tuple-element.60), channel_id=1, source_target_pairs={{0,12},{1,13},{2,14},{3,15},{4,0},{5,1},{6,2},{7,3},{8,4},{9,5},{1... | collective-permute-start | bytes 688136 | tf_op jit(solution)/shard_map/ppermute | solution.py:35
  63.1 7.5 %collective-permute-start.17 = (bf16[2,224,256]{2,1,0:T(8,128)(2,1)S(1)}, bf16[2,224,256]{2,1,0:T(8,128)(2,1)S(1)}, u32[]{:S(2)}, u32[]{:S(2)}) collective-permute-start(bf16[2,224,256]{2,1,0:T(8,128)(2,1)S(1)} %get-tuple-element.61), channel_id=1, source_target_pairs={{0,8},{1,9},{2,10},{3,11},{4,12},{5,13},{6,14},{7,15},{8,0},{9,1},... | collective-permute-start | bytes 688136 | tf_op jit(solution)/shard_map/ppermute | solution.py:35
  63.1 9.4 %collective-permute-start.13 = (bf16[2,224,256]{2,1,0:T(8,128)(2,1)S(1)}, bf16[2,224,256]{2,1,0:T(8,128)(2,1)S(1)}, u32[]{:S(2)}, u32[]{:S(2)}) collective-permute-start(bf16[2,224,256]{2,1,0:T(8,128)(2,1)S(1)} %get-tuple-element.54), channel_id=1, source_target_pairs={{0,3},{1,0},{2,1},{3,2},{4,7},{5,4},{6,5},{7,6},{8,11},{9,8},{10,9... | collective-permute-start | bytes 688136 | tf_op jit(solution)/shard_map/ppermute | solution.py:35
  66.0 7.5 %collective-permute-start.14 = (bf16[2,224,256]{2,1,0:T(8,128)(2,1)S(1)}, bf16[2,224,256]{2,1,0:T(8,128)(2,1)S(1)}, u32[]{:S(2)}, u32[]{:S(2)}) collective-permute-start(bf16[2,224,256]{2,1,0:T(8,128)(2,1)S(1)} %get-tuple-element.55), channel_id=1, source_target_pairs={{0,2},{1,3},{2,0},{3,1},{4,6},{5,7},{6,4},{7,5},{8,10},{9,11},{10,... | collective-permute-start | bytes 688136 | tf_op jit(solution)/shard_map/ppermute | solution.py:35
  79.4 6.6 %collective-permute-start.21 = (f32[192,128]{1,0:T(8,128)S(1)}, f32[192,128]{1,0:T(8,128)S(1)}, u32[]{:S(2)}, u32[]{:S(2)}) collective-permute-start(f32[192,128]{1,0:T(8,128)S(1)} %get-tuple-element.74), channel_id=1, source_target_pairs={{0,64},{16,80},{32,96},{48,112},{64,0},{80,16},{96,32},{112,48},{1... | collective-permute-start | bytes 294920 | tf_op jit(solution)/shard_map/ppermute | solution.py:40
  83.6 5.8 %collective-permute-start.19 = (f32[192,128]{1,0:T(8,128)S(1)}, f32[192,128]{1,0:T(8,128)S(1)}, u32[]{:S(2)}, u32[]{:S(2)}) collective-permute-start(f32[192,128]{1,0:T(8,128)S(1)} %get-tuple-element.73), channel_id=1, source_target_pairs={{0,32},{16,48},{32,64},{48,80},{64,96},{80,112},{96,0},{112,16},{1... | collective-permute-start | bytes 294920 | tf_op jit(solution)/shard_map/ppermute | solution.py:40
  89.5 5.5 %collective-permute-start.24 = (f32[48,128]{1,0:T(8,128)S(1)}, f32[48,128]{1,0:T(8,128)S(1)}, u32[]{:S(2)}, u32[]{:S(2)}) collective-permute-start(f32[48,128]{1,0:T(8,128)S(1)} %get-tuple-element.77), channel_id=1, source_target_pairs={{0,2},{1,3},{2,0},{3,1},{4,6},{5,7},{6,4},{7,5},{8,10},{9,11},{10,... | collective-permute-start | bytes 73736 | tf_op jit(solution)/shard_map/ppermute | solution.py:35
  90.5 5.5 %collective-permute-start.23 = (f32[48,128]{1,0:T(8,128)S(1)}, f32[48,128]{1,0:T(8,128)S(1)}, u32[]{:S(2)}, u32[]{:S(2)}) collective-permute-start(f32[48,128]{1,0:T(8,128)S(1)} %get-tuple-element.78), channel_id=1, source_target_pairs={{0,3},{1,0},{2,1},{3,2},{4,7},{5,4},{6,5},{7,6},{8,11},{9,8},{10,9... | collective-permute-start | bytes 73736 | tf_op jit(solution)/shard_map/ppermute | solution.py:35
  99.1 6.5 %collective-permute-start.27 = (f32[48,128]{1,0:T(8,128)S(1)}, f32[48,128]{1,0:T(8,128)S(1)}, u32[]{:S(2)}, u32[]{:S(2)}) collective-permute-start(f32[48,128]{1,0:T(8,128)S(1)} %fusion.6), channel_id=1, source_target_pairs={{0,8},{1,9},{2,10},{3,11},{4,12},{5,13},{6,14},{7,15},{8,0},{9,1},... | collective-permute-start | bytes 73736 | tf_op jit(solution)/shard_map/ppermute | solution.py:35
  107.6 5.7 %collective-permute-start.29 = (f32[48,128]{1,0:T(8,128)S(1)}, f32[48,128]{1,0:T(8,128)S(1)}, u32[]{:S(2)}, u32[]{:S(2)}) collective-permute-start(f32[48,128]{1,0:T(8,128)S(1)} %get-tuple-element.69), channel_id=1, source_target_pairs={{0,2},{1,3},{2,0},{3,1},{4,6},{5,7},{6,4},{7,5},{8,10},{9,11},{10,... | collective-permute-start | bytes 73736 | tf_op jit(solution)/shard_map/ppermute | solution.py:35
  108.5 5.8 %collective-permute-start.30 = (f32[48,128]{1,0:T(8,128)S(1)}, f32[48,128]{1,0:T(8,128)S(1)}, u32[]{:S(2)}, u32[]{:S(2)}) collective-permute-start(f32[48,128]{1,0:T(8,128)S(1)} %get-tuple-element.69), channel_id=1, source_target_pairs={{0,1},{1,2},{2,3},{3,0},{4,5},{5,6},{6,7},{7,4},{8,9},{9,10},{10,1... | collective-permute-start | bytes 73736 | tf_op jit(solution)/shard_map/ppermute | solution.py:35
  114.4 6.2 %collective-permute-start.33 = (f32[192,128]{1,0:T(8,128)S(1)}, f32[192,128]{1,0:T(8,128)S(1)}, u32[]{:S(2)}, u32[]{:S(2)}) collective-permute-start(f32[192,128]{1,0:T(8,128)S(1)} %bitcast.105), channel_id=1, source_target_pairs={{0,64},{16,80},{32,96},{48,112},{64,0},{80,16},{96,32},{112,48},{1... | collective-permute-start | bytes 294920 | tf_op jit(solution)/shard_map/ppermute | solution.py:40
  115.5 6.1 %collective-permute-start.32 = (f32[192,128]{1,0:T(8,128)S(1)}, f32[192,128]{1,0:T(8,128)S(1)}, u32[]{:S(2)}, u32[]{:S(2)}) collective-permute-start(f32[192,128]{1,0:T(8,128)S(1)} %bitcast.106), channel_id=1, source_target_pairs={{0,32},{16,48},{32,64},{48,80},{64,96},{80,112},{96,0},{112,16},{1... | collective-permute-start | bytes 294920 | tf_op jit(solution)/shard_map/ppermute | solution.py:40
  116.1 5.5 %collective-permute-start.31 = (f32[192,128]{1,0:T(8,128)S(1)}, f32[192,128]{1,0:T(8,128)S(1)}, u32[]{:S(2)}, u32[]{:S(2)}) collective-permute-start(f32[192,128]{1,0:T(8,128)S(1)} %bitcast.107), channel_id=1, source_target_pairs={{0,96},{16,112},{32,0},{48,16},{64,32},{80,48},{96,64},{112,80},{1... | collective-permute-start | bytes 294920 | tf_op jit(solution)/shard_map/ppermute | solution.py:40
  155.9 7.9 %collective-permute-start.38 = (bf16[4,32,512]{2,1,0:T(8,128)(2,1)S(1)}, bf16[4,32,512]{2,1,0:T(8,128)(2,1)S(1)}, u32[]{:S(2)}, u32[]{:S(2)}) collective-permute-start(bf16[4,32,512]{2,1,0:T(8,128)(2,1)S(1)} %get-tuple-element.71), channel_id=1, source_target_pairs={{0,64},{16,80},{32,96},{48,112},{64,0},{80,16},{96,32},{112,48},{1... | collective-permute-start | bytes 393224 | tf_op jit(solution)/shard_map/ppermute | solution.py:40
  158.7 6.9 %collective-permute-start.37 = (bf16[4,32,512]{2,1,0:T(8,128)(2,1)S(1)}, bf16[4,32,512]{2,1,0:T(8,128)(2,1)S(1)}, u32[]{:S(2)}, u32[]{:S(2)}) collective-permute-start(bf16[4,32,512]{2,1,0:T(8,128)(2,1)S(1)} %get-tuple-element.72), channel_id=1, source_target_pairs={{0,96},{16,112},{32,0},{48,16},{64,32},{80,48},{96,64},{112,80},{1... | collective-permute-start | bytes 393224 | tf_op jit(solution)/shard_map/ppermute | solution.py:40
  159.8 6.5 %collective-permute-start.36 = (bf16[4,32,512]{2,1,0:T(8,128)(2,1)S(1)}, bf16[4,32,512]{2,1,0:T(8,128)(2,1)S(1)}, u32[]{:S(2)}, u32[]{:S(2)}) collective-permute-start(bf16[4,32,512]{2,1,0:T(8,128)(2,1)S(1)} %get-tuple-element.70), channel_id=1, source_target_pairs={{0,32},{16,48},{32,64},{48,80},{64,96},{80,112},{96,0},{112,16},{1... | collective-permute-start | bytes 393224 | tf_op jit(solution)/shard_map/ppermute | solution.py:40
  (20 other events, 94.9 us)
Sparse Core Ops, SparseCore 0:
  74.6 68.1 all-gather.1
